TPU v7x, 256 devices: a whole 4x4x8 slice. The times are simulated.
256 devices in a mesh: rep: 16 (over z_hi, x), fsdp: 16 (over y, z_lo, core).
Axes of the slice: x: 4, y: 4, z: 8 (z_hi: 4, z_lo: 2; z = z_hi * 2 + z_lo), core: 2. Of those that a mesh axis runs over, the one named last changes fastest.
Arguments:
- partial_grads: bfloat16 [256, 512, 8192], P(('rep', 'fsdp')), may hold values from -6 to 6
- momentum: float32 [8192, 8192], P('rep', 'fsdp'), may hold values from -6 to 6
- freq_index: int32 [16, 8, 128, 32], P('rep', None, 'fsdp'), may hold values from 0 to 4095, all different within a row
Outputs:
- new_momentum: float32 [8192, 8192], P('rep', 'fsdp')
- update: float32 [512, 8192], P(None, 'fsdp')
Inputs may be any that keep to these rules, and one draw needn't show every extreme that they name: `freq_index`: the 32 frequencies of one block of one replica are distinct.
All inputs are finite; a program needn't handle non-finite values.
Results may differ from a plain program's by a relative error of at most 0.0003.
Values may be sent and summed in bfloat16 or wider, within the bound.
No kernel may reach another device: no remote copies, remote signals or barrier semaphores. Data moves between devices by JAX's collectives and lax.ppermute only.
A program may use at most 128 MiB of HBM per device.

v0:
```python
import jax
import jax.numpy as jnp
from jax import lax
from jax.sharding import PartitionSpec as P

GROUP = 64


momentum_decay = 0.9


def dct_basis(order):
    freq = jnp.arange(order, dtype=jnp.int32)[:, None]
    place = jnp.arange(order, dtype=jnp.int32)[None, :]
    phase = (2 * place + 1) * freq % (4 * order)
    scaling = jnp.where(
        freq == 0, jnp.sqrt(jnp.float32(1.0) / order), jnp.sqrt(jnp.float32(2.0) / order)
    )
    return scaling * jnp.cos(jnp.pi * phase.astype(jnp.float32) / (2.0 * order))


def forward_blocks(field, basis, order):
    row_blocks = field.shape[0] // order
    col_blocks = field.shape[1] // order
    blocks = field.reshape(row_blocks, order, col_blocks, order)
    coef = jnp.einsum("kn,anbm,lm->abkl", basis, blocks, basis, precision=lax.Precision.HIGHEST)
    return coef.reshape(row_blocks, col_blocks, order * order)


def inverse_blocks(coef, basis, order):
    row_blocks, col_blocks = (coef.shape[0], coef.shape[1])
    square = coef.reshape(row_blocks, col_blocks, order, order)
    field = jnp.einsum("kn,abkl,lm->anbm", basis, square, basis, precision=lax.Precision.HIGHEST)
    return field.reshape(row_blocks * order, col_blocks * order)


def select_kept(coef, positions):
    freqs = jnp.arange(coef.shape[2], dtype=jnp.int32)

    def select_one_row(pair):
        row_coef, row_pos = pair
        hits = row_pos[:, :, None] == freqs[None, None, :]
        return jnp.sum(jnp.where(hits, row_coef[:, None, :], jnp.float32(0.0)), axis=2)

    return lax.map(select_one_row, (coef, positions))


def place_values(values, positions, width):
    freqs = jnp.arange(width, dtype=jnp.int32)

    def place_one_row(pair):
        row_vals, row_pos = pair
        hits = row_pos[:, :, None] == freqs[None, None, :]
        return jnp.sum(jnp.where(hits, row_vals[:, :, None], jnp.float32(0.0)), axis=1)

    return lax.map(place_one_row, (values, positions))


def local(partial_grads, momentum, freq_index):
    order = GROUP
    basis = dct_basis(order)
    total_rows = momentum.shape[0]
    blocks_count = 1
    span = total_rows // blocks_count
    span_blocks = span // order
    slab = partial_grads[0, 0:span, :].astype(jnp.float32)
    grad = lax.psum_scatter(slab, "fsdp", scatter_dimension=1, tiled=True)
    field = momentum_decay * momentum + grad
    positions = freq_index[0, 0:span_blocks]
    coef = forward_blocks(field, basis, order)
    width = coef.shape[2]
    kept = select_kept(coef, positions)
    own_dense = place_values(kept, positions, width)
    fresh_parts = field - inverse_blocks(own_dense, basis, order)
    all_values = lax.all_gather(kept[None], "rep", axis=0, tiled=True)
    all_positions = lax.all_gather(positions[None], "rep", axis=0, tiled=True)

    def add_replica(total, pair):
        vals, poss = pair
        return (total + place_values(vals, poss, width), None)

    summed, unused = lax.scan(
        add_replica, jnp.zeros(coef.shape, jnp.float32), (all_values, all_positions)
    )
    update_parts = inverse_blocks(summed, basis, order)
    return (fresh_parts, update_parts)


def solution(mesh):
    return jax.shard_map(
        local,
        mesh=mesh,
        in_specs=(P(("rep", "fsdp"), None, None), P("rep", "fsdp"), P("rep", None, "fsdp", None)),
        out_specs=(P("rep", "fsdp"), P(None, "fsdp")),
        check_vma=False,
    )
```

profile of v0, /device:TPU:40, one launch (start us, length us, event | category | flops | bytes accessed | tf_op | source)
XLA Modules:
  0.0 481.6 jit_solution(9750800390041773434)
XLA Ops:
  7.2 11.3 %bitcast_convert_fusion = f32[512,8192]{1,0:T(8,128)} fusion(bf16[1,512,8192]{2,1,0:T(8,128)(2,1)} %param.11), kind=kLoop, calls=%fused_computation.21 | loop fusion | flops 4194304 | bytes 25165824 | tf_op jit(solution)/shard_map/convert_element_type | solution.py:66
  19.3 54.5 %all_gather.7 = s32[16,8,8,32]{3,2,1,0:T(8,128)} all-gather(s32[1,8,8,32]{3,2,1,0:T(8,128)S(1)} %copy-done.1), channel_id=1, replica_groups=mesh['rep'=16,'fsdp'=16] {'rep'}, dimensions={0}, use_global_device_ids=true | all-gather | bytes 139264 | tf_op jit(solution)/shard_map/all_gather | solution.py:76
  73.8 135.1 %reduce-scatter.2.cloned.1.call-done = f32[512,512]{1,0:T(8,128)} async-done(((f32[512,8192]{1,0:T(8,128)}), f32[512,512]{1,0:T(8,128)}) %reduce-scatter.2.cloned.1.call-update) | async-done | bytes 1048592 | tf_op jit(solution)/shard_map/reduce_scatter | solution.py:67
  208.9 1.4 multiply_add_fusion
  210.4 1.8 reshape.53
  212.2 3.9 fusion.6
  216.1 3.3 fusion.23
  219.3 2.1 reshape.54
  221.5 5.8 %while.50 = (s32[]{:T(128)}, f32[8,8,32]{2,1,0:T(8,128)S(1)}, s32[8,8,32]{2,1,0:T(8,128)S(1)}, f32[8,8,4096]{2,1,0:T(8,128)S(1)}) while((s32[]{:T(128)}, f32[8,8,32]{2,1,0:T(8,128)S(1)}, s32[8,8,32]{2,1,0:T(8,128)S(1)}, f32[8,8,4096]{2,1,0:T(8,128)S(1)}) %tuple.103), condition=%wide.region_3.4_spmd.clone.clone, body=%wide.region_1.3_spmd.clone.sunk.clone | while | flops 3145474 | bytes 405577 | solution.py:45
  227.3 53.2 %all-gather = f32[128,8,32]{2,1,0:T(8,128)} all-gather(f32[8,8,32]{2,1,0:T(8,128)S(1)} %get-tuple-element.366), channel_id=2, replica_groups=mesh['rep'=16,'fsdp'=16] {'rep'}, dimensions={0}, use_global_device_ids=true | all-gather | bytes 139264 | tf_op jit(solution)/shard_map/all_gather | solution.py:75
  280.4 12.8 %while.51 = (s32[]{:T(128)}, f32[8,8,4096]{2,1,0:T(8,128)}, s32[8,8,32]{2,1,0:T(8,128)S(1)}, f32[8,8,32]{2,1,0:T(8,128)S(1)}) while((s32[]{:T(128)}, f32[8,8,4096]{2,1,0:T(8,128)}, s32[8,8,32]{2,1,0:T(8,128)S(1)}, f32[8,8,32]{2,1,0:T(8,128)S(1)}) %tuple.104), condition=%wide.region_6.7_spmd.clone.clone, body=%wide.region_4.6_spmd.clone.sunk.clone | while | flops 3112962 | bytes 399433 | solution.py:56
  293.3 3.1 reshape.55
  296.4 3.6 fusion.21
  300.0 2.0 convolution_bitcast_fusion.1
  302.0 2.5 copy.19
  304.6 1.9 reshape.56
  306.5 1.2 sub.3
  307.7 159.4 %while.53 = (s32[]{:T(128)}, f32[8,8,4096]{2,1,0:T(8,128)S(1)}, f32[16,8,8,32]{3,2,1,0:T(8,128)}, s32[16,8,8,32]{3,2,1,0:T(8,128)}, s32[]{:T(128)}, /*index=5*/s32[]{:T(128)}, f32[]{:T(128)}) while((s32[]{:T(128)}, f32[8,8,4096]{2,1,0:T(8,128)S(1)}, f32[16,8,8,32]{3,2,1,0:T(8,128)}, s32[16,8,8,32]{3,2,1,0:T(8,128)}, ...), condition=%wide.region_11.12_spmd.clone.clone, body=%wide.region_7.11_spmd.clone.sunk.clone | while | flops 3637253 | bytes 3578088 | solution.py:82
  309.2 8.0 %while.52 = (s32[]{:T(128)}, f32[8,8,4096]{2,1,0:T(8,128)S(1)}, s32[8,8,32]{2,1,0:T(8,128)S(1)}, f32[8,8,32]{2,1,0:T(8,128)S(1)}, s32[]{:T(128)}) while((s32[]{:T(128)}, f32[8,8,4096]{2,1,0:T(8,128)S(1)}, s32[8,8,32]{2,1,0:T(8,128)S(1)}, f32[8,8,32]{2,1,0:T(8,128)S(1)}, s32[]{:T(128)}) %tuple.88), condition=%wide.region_10.10_spmd.clone, body=%wide.region_8.9_spmd.clone.sunk | while | flops 3112962 | bytes 399441 | solution.py:56
  309.2 0.9 select_reduce_fusion.8
  310.2 0.9 select_reduce_fusion.8
  311.3 0.9 select_reduce_fusion.8
  312.3 0.9 select_reduce_fusion.8
  313.3 0.9 select_reduce_fusion.8
  314.3 0.9 select_reduce_fusion.8
  316.3 0.9 select_reduce_fusion.8
  319.2 8.0 %while.52 = (s32[]{:T(128)}, f32[8,8,4096]{2,1,0:T(8,128)S(1)}, s32[8,8,32]{2,1,0:T(8,128)S(1)}, f32[8,8,32]{2,1,0:T(8,128)S(1)}, s32[]{:T(128)}) while((s32[]{:T(128)}, f32[8,8,4096]{2,1,0:T(8,128)S(1)}, s32[8,8,32]{2,1,0:T(8,128)S(1)}, f32[8,8,32]{2,1,0:T(8,128)S(1)}, s32[]{:T(128)}) %tuple.88), condition=%wide.region_10.10_spmd.clone, body=%wide.region_8.9_spmd.clone.sunk | while | flops 3112962 | bytes 399441 | solution.py:56
  319.2 0.9 select_reduce_fusion.8
  320.2 0.9 select_reduce_fusion.8
  321.2 0.9 select_reduce_fusion.8
  322.2 0.9 select_reduce_fusion.8
  323.2 0.9 select_reduce_fusion.8
  329.1 8.0 %while.52 = (s32[]{:T(128)}, f32[8,8,4096]{2,1,0:T(8,128)S(1)}, s32[8,8,32]{2,1,0:T(8,128)S(1)}, f32[8,8,32]{2,1,0:T(8,128)S(1)}, s32[]{:T(128)}) while((s32[]{:T(128)}, f32[8,8,4096]{2,1,0:T(8,128)S(1)}, s32[8,8,32]{2,1,0:T(8,128)S(1)}, f32[8,8,32]{2,1,0:T(8,128)S(1)}, s32[]{:T(128)}) %tuple.88), condition=%wide.region_10.10_spmd.clone, body=%wide.region_8.9_spmd.clone.sunk | while | flops 3112962 | bytes 399441 | solution.py:56
  329.1 0.9 select_reduce_fusion.8
  339.1 8.0 %while.52 = (s32[]{:T(128)}, f32[8,8,4096]{2,1,0:T(8,128)S(1)}, s32[8,8,32]{2,1,0:T(8,128)S(1)}, f32[8,8,32]{2,1,0:T(8,128)S(1)}, s32[]{:T(128)}) while((s32[]{:T(128)}, f32[8,8,4096]{2,1,0:T(8,128)S(1)}, s32[8,8,32]{2,1,0:T(8,128)S(1)}, f32[8,8,32]{2,1,0:T(8,128)S(1)}, s32[]{:T(128)}) %tuple.88), condition=%wide.region_10.10_spmd.clone, body=%wide.region_8.9_spmd.clone.sunk | while | flops 3112962 | bytes 399441 | solution.py:56
  339.1 0.9 select_reduce_fusion.8
  349.0 8.0 %while.52 = (s32[]{:T(128)}, f32[8,8,4096]{2,1,0:T(8,128)S(1)}, s32[8,8,32]{2,1,0:T(8,128)S(1)}, f32[8,8,32]{2,1,0:T(8,128)S(1)}, s32[]{:T(128)}) while((s32[]{:T(128)}, f32[8,8,4096]{2,1,0:T(8,128)S(1)}, s32[8,8,32]{2,1,0:T(8,128)S(1)}, f32[8,8,32]{2,1,0:T(8,128)S(1)}, s32[]{:T(128)}) %tuple.88), condition=%wide.region_10.10_spmd.clone, body=%wide.region_8.9_spmd.clone.sunk | while | flops 3112962 | bytes 399441 | solution.py:56
  349.0 0.9 select_reduce_fusion.8
  359.0 8.0 %while.52 = (s32[]{:T(128)}, f32[8,8,4096]{2,1,0:T(8,128)S(1)}, s32[8,8,32]{2,1,0:T(8,128)S(1)}, f32[8,8,32]{2,1,0:T(8,128)S(1)}, s32[]{:T(128)}) while((s32[]{:T(128)}, f32[8,8,4096]{2,1,0:T(8,128)S(1)}, s32[8,8,32]{2,1,0:T(8,128)S(1)}, f32[8,8,32]{2,1,0:T(8,128)S(1)}, s32[]{:T(128)}) %tuple.88), condition=%wide.region_10.10_spmd.clone, body=%wide.region_8.9_spmd.clone.sunk | while | flops 3112962 | bytes 399441 | solution.py:56
  359.0 0.9 select_reduce_fusion.8
  368.9 8.0 %while.52 = (s32[]{:T(128)}, f32[8,8,4096]{2,1,0:T(8,128)S(1)}, s32[8,8,32]{2,1,0:T(8,128)S(1)}, f32[8,8,32]{2,1,0:T(8,128)S(1)}, s32[]{:T(128)}) while((s32[]{:T(128)}, f32[8,8,4096]{2,1,0:T(8,128)S(1)}, s32[8,8,32]{2,1,0:T(8,128)S(1)}, f32[8,8,32]{2,1,0:T(8,128)S(1)}, s32[]{:T(128)}) %tuple.88), condition=%wide.region_10.10_spmd.clone, body=%wide.region_8.9_spmd.clone.sunk | while | flops 3112962 | bytes 399441 | solution.py:56
  368.9 0.9 select_reduce_fusion.8
  378.9 8.0 %while.52 = (s32[]{:T(128)}, f32[8,8,4096]{2,1,0:T(8,128)S(1)}, s32[8,8,32]{2,1,0:T(8,128)S(1)}, f32[8,8,32]{2,1,0:T(8,128)S(1)}, s32[]{:T(128)}) while((s32[]{:T(128)}, f32[8,8,4096]{2,1,0:T(8,128)S(1)}, s32[8,8,32]{2,1,0:T(8,128)S(1)}, f32[8,8,32]{2,1,0:T(8,128)S(1)}, s32[]{:T(128)}) %tuple.88), condition=%wide.region_10.10_spmd.clone, body=%wide.region_8.9_spmd.clone.sunk | while | flops 3112962 | bytes 399441 | solution.py:56
  378.9 0.9 select_reduce_fusion.8
  388.8 8.0 %while.52 = (s32[]{:T(128)}, f32[8,8,4096]{2,1,0:T(8,128)S(1)}, s32[8,8,32]{2,1,0:T(8,128)S(1)}, f32[8,8,32]{2,1,0:T(8,128)S(1)}, s32[]{:T(128)}) while((s32[]{:T(128)}, f32[8,8,4096]{2,1,0:T(8,128)S(1)}, s32[8,8,32]{2,1,0:T(8,128)S(1)}, f32[8,8,32]{2,1,0:T(8,128)S(1)}, s32[]{:T(128)}) %tuple.88), condition=%wide.region_10.10_spmd.clone, body=%wide.region_8.9_spmd.clone.sunk | while | flops 3112962 | bytes 399441 | solution.py:56
  388.8 0.9 select_reduce_fusion.8
  398.8 8.0 %while.52 = (s32[]{:T(128)}, f32[8,8,4096]{2,1,0:T(8,128)S(1)}, s32[8,8,32]{2,1,0:T(8,128)S(1)}, f32[8,8,32]{2,1,0:T(8,128)S(1)}, s32[]{:T(128)}) while((s32[]{:T(128)}, f32[8,8,4096]{2,1,0:T(8,128)S(1)}, s32[8,8,32]{2,1,0:T(8,128)S(1)}, f32[8,8,32]{2,1,0:T(8,128)S(1)}, s32[]{:T(128)}) %tuple.88), condition=%wide.region_10.10_spmd.clone, body=%wide.region_8.9_spmd.clone.sunk | while | flops 3112962 | bytes 399441 | solution.py:56
  398.8 0.9 select_reduce_fusion.8
  408.7 8.0 %while.52 = (s32[]{:T(128)}, f32[8,8,4096]{2,1,0:T(8,128)S(1)}, s32[8,8,32]{2,1,0:T(8,128)S(1)}, f32[8,8,32]{2,1,0:T(8,128)S(1)}, s32[]{:T(128)}) while((s32[]{:T(128)}, f32[8,8,4096]{2,1,0:T(8,128)S(1)}, s32[8,8,32]{2,1,0:T(8,128)S(1)}, f32[8,8,32]{2,1,0:T(8,128)S(1)}, s32[]{:T(128)}) %tuple.88), condition=%wide.region_10.10_spmd.clone, body=%wide.region_8.9_spmd.clone.sunk | while | flops 3112962 | bytes 399441 | solution.py:56
  408.7 0.9 select_reduce_fusion.8
  418.7 8.0 %while.52 = (s32[]{:T(128)}, f32[8,8,4096]{2,1,0:T(8,128)S(1)}, s32[8,8,32]{2,1,0:T(8,128)S(1)}, f32[8,8,32]{2,1,0:T(8,128)S(1)}, s32[]{:T(128)}) while((s32[]{:T(128)}, f32[8,8,4096]{2,1,0:T(8,128)S(1)}, s32[8,8,32]{2,1,0:T(8,128)S(1)}, f32[8,8,32]{2,1,0:T(8,128)S(1)}, s32[]{:T(128)}) %tuple.88), condition=%wide.region_10.10_spmd.clone, body=%wide.region_8.9_spmd.clone.sunk | while | flops 3112962 | bytes 399441 | solution.py:56
  418.7 0.9 select_reduce_fusion.8
  428.6 8.0 %while.52 = (s32[]{:T(128)}, f32[8,8,4096]{2,1,0:T(8,128)S(1)}, s32[8,8,32]{2,1,0:T(8,128)S(1)}, f32[8,8,32]{2,1,0:T(8,128)S(1)}, s32[]{:T(128)}) while((s32[]{:T(128)}, f32[8,8,4096]{2,1,0:T(8,128)S(1)}, s32[8,8,32]{2,1,0:T(8,128)S(1)}, f32[8,8,32]{2,1,0:T(8,128)S(1)}, s32[]{:T(128)}) %tuple.88), condition=%wide.region_10.10_spmd.clone, body=%wide.region_8.9_spmd.clone.sunk | while | flops 3112962 | bytes 399441 | solution.py:56
  428.6 0.9 select_reduce_fusion.8
  438.6 8.0 %while.52 = (s32[]{:T(128)}, f32[8,8,4096]{2,1,0:T(8,128)S(1)}, s32[8,8,32]{2,1,0:T(8,128)S(1)}, f32[8,8,32]{2,1,0:T(8,128)S(1)}, s32[]{:T(128)}) while((s32[]{:T(128)}, f32[8,8,4096]{2,1,0:T(8,128)S(1)}, s32[8,8,32]{2,1,0:T(8,128)S(1)}, f32[8,8,32]{2,1,0:T(8,128)S(1)}, s32[]{:T(128)}) %tuple.88), condition=%wide.region_10.10_spmd.clone, body=%wide.region_8.9_spmd.clone.sunk | while | flops 3112962 | bytes 399441 | solution.py:56
  438.6 0.9 select_reduce_fusion.8
  448.5 8.0 %while.52 = (s32[]{:T(128)}, f32[8,8,4096]{2,1,0:T(8,128)S(1)}, s32[8,8,32]{2,1,0:T(8,128)S(1)}, f32[8,8,32]{2,1,0:T(8,128)S(1)}, s32[]{:T(128)}) while((s32[]{:T(128)}, f32[8,8,4096]{2,1,0:T(8,128)S(1)}, s32[8,8,32]{2,1,0:T(8,128)S(1)}, f32[8,8,32]{2,1,0:T(8,128)S(1)}, s32[]{:T(128)}) %tuple.88), condition=%wide.region_10.10_spmd.clone, body=%wide.region_8.9_spmd.clone.sunk | while | flops 3112962 | bytes 399441 | solution.py:56
  448.5 0.9 select_reduce_fusion.8
  458.5 8.0 %while.52 = (s32[]{:T(128)}, f32[8,8,4096]{2,1,0:T(8,128)S(1)}, s32[8,8,32]{2,1,0:T(8,128)S(1)}, f32[8,8,32]{2,1,0:T(8,128)S(1)}, s32[]{:T(128)}) while((s32[]{:T(128)}, f32[8,8,4096]{2,1,0:T(8,128)S(1)}, s32[8,8,32]{2,1,0:T(8,128)S(1)}, f32[8,8,32]{2,1,0:T(8,128)S(1)}, s32[]{:T(128)}) %tuple.88), condition=%wide.region_10.10_spmd.clone, body=%wide.region_8.9_spmd.clone.sunk | while | flops 3112962 | bytes 399441 | solution.py:56
  458.5 0.9 select_reduce_fusion.8
  467.9 2.1 fusion.18
  470.1 2.0 convolution_bitcast_fusion
  472.1 1.2 copy.22
  473.3 1.5 reshape.58
  (626 shorter events, 148.8 us)
Async XLA Ops:
  7.2 201.8 %reduce-scatter.2.cloned.1.call-start = ((), (), s32[]{:S(2)}) async-start(), calls=%async_computation.1 | async-start | bytes 17825792 | tf_op jit(solution)/shard_map/reduce_scatter | solution.py:67
  18.5 0.8 copy-start.1
  18.5 190.4 %copy-start = (f32[512,512]{1,0:T(8,128)S(1)}, f32[512,512]{1,0:T(8,128)}, u32[]{:S(2)}) copy-start(f32[512,512]{1,0:T(8,128)} %param.12) | copy-start | bytes 3145732
Sparse Core Ops, SparseCore 0:
  18.7 190.2 reduce-scatter.1
where the time goes:
time: 484 us; the launch traced here: 482 us
  other arithmetic  151 us (31%)
  waiting for transfers between devices  135 us (28%)
  blocking collectives  108 us (22%)
  local copies, waits for them, and re-layouts  49.7 us (10%)
  matrix products  16.9 us (3%)
  between operations  14.1 us (3%)
  loops' own time  6.61 us (1%)
    reduce_scatter x1, waiting for transfers between devices, local(): grad = lax.psum_scatter(slab, 'fsdp', scatter_dimension=1, tiled=True)  135 us
    reduce_sum x136, other arithmetic, place_one_row(): jnp.sum(jnp.where(hits, row_vals[:, :, None], jnp.float32(0.0)), axis=1)  127 us
    all_gather x1, blocking collectives, local(): all_positions = lax.all_gather(positions[None], 'rep', axis=0, tiled=True)  54.5 us
    all_gather x1, blocking collectives, local(): all_values = lax.all_gather(kept[None], 'rep', axis=0, tiled=True)  53.2 us
    squeeze x32, local copies, waits for them, and re-layouts, local(): lax.scan(add_replica, jnp.zeros(coef.shape, jnp.float32), (all_values, al...  24.4 us
    convert_element_type x1, other arithmetic, local(): slab = partial_grads[0, 0:span, :].astype(jnp.float32)  11.3 us
    dot_general x4, matrix products, inverse_blocks(): jnp.einsum('kn,abkl,lm->anbm', basis, square, basis, precision=lax.Precis...  9.78 us
  transfers between devices with their start and end apart: 1, of which 1 were waited for; matrix products, arithmetic and copies ran while one was open for 0% of the time, Pallas kernels for 0%

commit v1 on v0

v1 whole, which is shorter than its diff:
```python
import functools

import jax
import jax.numpy as jnp
import numpy as np
from jax import lax
from jax.experimental import pallas as pl
from jax.experimental.pallas import tpu as pltpu
from jax.sharding import PartitionSpec as P

GROUP = 64
K = 32
WIDE = 256
KEPT = 128
CHUNK = 128
DECAY = 0.9
BF = jnp.bfloat16
F32 = jnp.float32


def dct_constants():
    k = np.arange(GROUP)[:, None]
    n = np.arange(GROUP)[None, :]
    scale = np.where(k == 0, np.sqrt(1.0 / GROUP), np.sqrt(2.0 / GROUP))
    basis = scale * np.cos(np.pi * ((2 * n + 1) * k % (4 * GROUP)) / (2.0 * GROUP))
    wide = np.kron(np.eye(WIDE // GROUP), basis)
    both = np.stack([wide, wide.T]).astype(np.float32)
    high = both.astype(BF)
    low = (both - high.astype(np.float32)).astype(BF)
    return np.stack([high, low], axis=1)


def cut(x):
    high = x.astype(BF)
    return high, (x - high.astype(F32)).astype(BF)


def dot(a, b):
    return jnp.dot(a, b, preferred_element_type=F32)


def times_right(x, m_high, m_low):
    high, low = cut(x)
    return dot(high, m_high) + dot(high, m_low) + dot(low, m_high)


def times_left(m_high, m_low, x):
    high, low = cut(x)
    return dot(m_high, high) + dot(m_low, high) + dot(m_high, low)


def forward(field, basis):
    rows = field.shape[0]
    part = times_right(field, basis[1, 0], basis[1, 1])
    return times_left(basis[0, 0, :rows, :rows], basis[0, 1, :rows, :rows], part)


def inverse(coef, basis):
    rows = coef.shape[0]
    part = times_right(coef, basis[0, 0], basis[0, 1])
    return times_left(basis[1, 0, :rows, :rows], basis[1, 1, :rows, :rows], part)


def hits(pos):
    block = lax.broadcasted_iota(jnp.int32, (1, KEPT), 1) // K
    row = pos // GROUP
    col = pos % GROUP + block * GROUP
    on_row = lax.broadcasted_iota(jnp.int32, (GROUP, KEPT), 0) == row
    on_col = lax.broadcasted_iota(jnp.int32, (WIDE, KEPT), 0) == col
    return on_row, on_col


def one(mask):
    return jnp.where(mask, F32(1.0), F32(0.0)).astype(BF)


def by_lanes(a, b):
    return lax.dot_general(a, b, (((1,), (1,)), ((), ())), preferred_element_type=F32)


def by_rows(a, b):
    return lax.dot_general(a, b, (((0,), (0,)), ((), ())), preferred_element_type=F32)


def encode(field, pos_ref, basis, fresh_ref, kept_ref):
    rows, cols = field.shape
    for half in range(cols // WIDE):
        span = slice(half * WIDE, (half + 1) * WIDE)
        part = field[:, span]
        coef = forward(part, basis)
        dense = []
        for a in range(rows // GROUP):
            g = a * (cols // WIDE) + half
            block = coef[a * GROUP:(a + 1) * GROUP]
            on_row, on_col = hits(pos_ref[g:g + 1])
            row_one = one(on_row)
            chosen = by_lanes(row_one, one(on_col))
            dense.append(jnp.where(chosen > 0.5, block, F32(0.0)))
            high, low = cut(block)
            rest = (block - high.astype(F32) - low.astype(F32)).astype(BF)
            three = jnp.concatenate([high, low, rest], axis=0)
            rows_of = by_rows(three, jnp.concatenate([row_one] * 3, axis=0))
            kept_ref[g:g + 1] = jnp.sum(jnp.where(on_col, rows_of, F32(0.0)), axis=0, keepdims=True)
        fresh_ref[:, span] = part - inverse(jnp.concatenate(dense, axis=0), basis)


def encode_kernel(terms_ref, momentum_ref, pos_ref, basis_ref, fresh_ref, kept_ref):
    total = DECAY * momentum_ref[...]
    grad = terms_ref[0].astype(F32)
    for i in range(1, terms_ref.shape[0]):
        grad += terms_ref[i].astype(F32)
    encode(total + grad, pos_ref.at[0], basis_ref, fresh_ref, kept_ref.at[0])


def decode_kernel(*refs):
    n = (len(refs) - 2) // 2
    vals, poss = refs[:n], refs[n:2 * n]
    basis, out_ref = refs[2 * n:]
    groups = vals[0].shape[2]
    per_row = out_ref.shape[1] // WIDE
    for g in range(groups):
        left, right = [], []
        for val, pos in zip(vals, poss):
            for r in range(val.shape[0]):
                on_row, on_col = hits(pos[r, 0, g:g + 1])
                high, low = cut(jnp.where(on_row, val[r, 0, g:g + 1], F32(0.0)))
                left.append(jnp.concatenate([high, low], axis=0))
                right.append(one(on_col))
        both = by_lanes(jnp.concatenate(left, axis=1), jnp.concatenate(right, axis=1))
        field = inverse(both[:GROUP] + both[GROUP:], basis)
        a, half = g // per_row, g % per_row
        out_ref[a * GROUP:(a + 1) * GROUP, half * WIDE:(half + 1) * WIDE] = field


def across(n_hi, n_x, shift_hi, shift_x):
    return [
        (h * n_x + x, (h + shift_hi) % n_hi * n_x + (x + shift_x) % n_x)
        for h in range(n_hi)
        for x in range(n_x)
    ]


def gather_replicas(own):
    near = [own] + [lax.ppermute(own, "rep", across(4, 4, 0, s)) for s in (1, 2, 3)]
    near = jnp.stack(near)
    return [near] + [lax.ppermute(near, "rep", across(4, 4, s, 0)) for s in (1, 2, 3)]


def local(partial_grads, momentum, freq_index):
    rows, cols = momentum.shape
    n_fsdp = lax.axis_size("fsdp")
    chunks = rows // CHUNK
    groups = CHUNK // GROUP * (cols // WIDE)
    basis = jnp.asarray(dct_constants())
    pos = freq_index.reshape(chunks, groups, KEPT)
    pos_all = gather_replicas(pos)
    slab = partial_grads[0].reshape(rows, n_fsdp, cols).transpose(1, 0, 2)
    terms = lax.all_to_all(slab, "fsdp", 0, 0, tiled=True)
    params = pltpu.CompilerParams(vmem_limit_bytes=48 * 1024 * 1024)
    fresh, kept = pl.pallas_call(
        encode_kernel,
        grid=(chunks,),
        in_specs=[
            pl.BlockSpec((n_fsdp, CHUNK, cols), lambda i: (0, i, 0)),
            pl.BlockSpec((CHUNK, cols), lambda i: (i, 0)),
            pl.BlockSpec((1, groups, KEPT), lambda i: (i, 0, 0)),
            pl.BlockSpec(basis.shape, lambda i: (0, 0, 0, 0)),
        ],
        out_specs=[
            pl.BlockSpec((CHUNK, cols), lambda i: (i, 0)),
            pl.BlockSpec((1, groups, KEPT), lambda i: (i, 0, 0)),
        ],
        out_shape=[
            jax.ShapeDtypeStruct((rows, cols), F32),
            jax.ShapeDtypeStruct((chunks, groups, KEPT), F32),
        ],
        compiler_params=params,
        name="encode",
    )(terms, momentum, pos, basis)
    val_all = gather_replicas(kept)
    spec = pl.BlockSpec((4, 1, groups, KEPT), lambda i: (0, i, 0, 0))
    update = pl.pallas_call(
        decode_kernel,
        grid=(chunks,),
        in_specs=[spec] * 8 + [pl.BlockSpec(basis.shape, lambda i: (0, 0, 0, 0))],
        out_specs=pl.BlockSpec((CHUNK, cols), lambda i: (i, 0)),
        out_shape=jax.ShapeDtypeStruct((rows, cols), F32),
        compiler_params=params,
        name="decode",
    )(*val_all, *pos_all, basis)
    return fresh, update


def solution(mesh):
    return jax.shard_map(
        local,
        mesh=mesh,
        in_specs=(P(("rep", "fsdp"), None, None), P("rep", "fsdp"), P("rep", None, "fsdp", None)),
        out_specs=(P("rep", "fsdp"), P(None, "fsdp")),
        check_vma=False,
    )
```

time: 484 us -> 178 us (0.37)
  the two profiles are of different devices: /device:TPU:40 before, /device:TPU:6 now
where the time goes in v1:
time: 178 us; the launch traced here: 176 us
  waiting for transfers between devices  94.6 us (53%)
  starting transfers between devices  29.9 us (17%)
  Pallas kernels  26.2 us (15%)
  local copies, waits for them, and re-layouts  24.2 us (14%)
    all_to_all x1, waiting for transfers between devices, local(): terms = lax.all_to_all(slab, 'fsdp', 0, 0, tiled=True)  91.1 us
    pallas_call x1, Pallas kernels, local(): pl.pallas_call(decode_kernel, grid=(chunks,), in_specs=[spec] * 8 + [pl.B...  16.6 us
    ppermute x6, starting transfers between devices, gather_replicas(): lax.ppermute(near, 'rep', across(4, 4, s, 0))  15.7 us
    another operation x1, local copies, waits for them, and re-layouts, local(): slab = partial_grads[0].reshape(rows, n_fsdp, cols).transpose(1, 0, 2)  12.4 us
    unnamed x7, local copies, waits for them, and re-layouts  11.7 us
    pallas_call x1, Pallas kernels, local(): pl.pallas_call(encode_kernel, grid=(chunks,), in_specs=[pl.BlockSpec((n_f...  9.62 us
    ppermute x6, starting transfers between devices, gather_replicas(): lax.ppermute(own, 'rep', across(4, 4, 0, s))  8.09 us
    all_to_all x1, starting transfers between devices, local(): terms = lax.all_to_all(slab, 'fsdp', 0, 0, tiled=True)  6.12 us
  transfers between devices with their start and end apart: 13, of which 4 were waited for; matrix products, arithmetic and copies ran while one was open for 0% of the time, Pallas kernels for 5%

profile of v1, /device:TPU:6, one launch (start us, length us, event | category | flops | bytes accessed | tf_op | source)
XLA Modules:
  0.0 175.5 jit_solution(5509129668009273354)
XLA Ops:
  0.6 11.6 %copy.6 = bf16[1,512,8192]{1,2,0:T(8,128)(2,1)} copy(bf16[1,512,8192]{2,1,0:T(8,128)(2,1)} %param.4) | data formatting | bytes 16777216 | tf_op args[0]
  12.3 12.4 %copy.7 = bf16[512,16,512]{2,0,1:T(8,128)(2,1)} copy(bf16[512,16,512]{0,2,1:T(8,128)(2,1)} %bitcast.15) | data formatting | bytes 16777216 | tf_op jit(solution)/shard_map/reshape;squeeze | solution.py:157
  24.6 0.0 copy-start.2
  24.6 0.0 copy-start
  24.6 0.0 copy-start.1
  24.6 6.1 %all-to-all-start = ((bf16[16,512,512]{2,1,0:T(8,128)(2,1)}), bf16[16,512,512]{2,1,0:T(8,128)(2,1)}, u32[]{:S(2)}, u32[]{:S(2)}) async-start(bf16[16,512,512]{2,1,0:T(8,128)(2,1)} %bitcast.14), calls=%async_computation | async-start | bytes 16777216 | tf_op jit(solution)/shard_map/all_to_all | solution.py:158
  30.8 0.0 copy-done.2
  30.8 0.1 reshape.7.pos_ref
  30.8 0.8 collective-permute-start.8
  31.7 1.7 collective-permute-start.7
  33.4 1.5 collective-permute-start.6
  34.9 0.1 stack_reshape.3
  35.0 91.1 %all-to-all-done.terms_ref = bf16[16,512,512]{2,1,0:T(8,128)(2,1)} async-done(((bf16[16,512,512]{2,1,0:T(8,128)(2,1)}), bf16[16,512,512]{2,1,0:T(8,128)(2,1)}, u32[]{:S(2)}, u32[]{:S(2)}) %all-to-all-start) | async-done | bytes 8388640 | tf_op jit(solution)/shard_map/all_to_all | solution.py:158
  126.1 0.0 copy-done
  126.1 0.0 copy-done.1
  126.1 9.6 %encode.1 = (f32[512,512]{1,0:T(8,128)}, f32[4,4,128]{2,1,0:T(4,128)S(1)}) custom-call(bf16[16,512,512]{2,1,0:T(8,128)(2,1)} %all-to-all-done.terms_ref, f32[512,512]{1,0:T(8,128)S(1)} %copy-done.1, s32[4,4,128]{2,1,0:T(4,128)S(1)} %reshape.7.pos_ref, bf16[2,2,256,256]{3,2,1,0:T(8,128)(2,1)S(1)} %copy-done), custom_call_target="tpu_custom_call" | custom-call | tf_op jit(solution)/shard_map/encode/pallas_call | solution.py:160
  135.7 0.8 collective-permute-start.2
  136.5 1.6 collective-permute-start.1
  138.2 0.0 collective-permute-done.8
  138.2 1.6 collective-permute-start
  139.8 0.0 collective-permute-done.7
  139.8 0.0 collective-permute-done.6
  139.8 3.3 %collective-permute-start.9 = (s32[4,4,4,128]{3,2,1,0:T(4,128)S(1)}, s32[4,4,4,128]{3,2,1,0:T(4,128)S(1)}, u32[]{:S(2)}, u32[]{:S(2)}) collective-permute-start(s32[4,4,4,128]{3,2,1,0:T(4,128)S(1)} %pad_add_fusion.refs_4_), channel_id=1, source_target_pairs={{0,64},{16,80},{32,96},{48,112},{64,128},{80,144},{96,160},{112,17... | collective-permute-start | bytes 98312 | tf_op jit(solution)/shard_map/ppermute | solution.py:146
  143.1 4.5 %collective-permute-start.10 = (s32[4,4,4,128]{3,2,1,0:T(4,128)S(1)}, s32[4,4,4,128]{3,2,1,0:T(4,128)S(1)}, u32[]{:S(2)}, u32[]{:S(2)}) collective-permute-start(s32[4,4,4,128]{3,2,1,0:T(4,128)S(1)} %pad_add_fusion.refs_4_), channel_id=1, source_target_pairs={{0,128},{16,144},{32,160},{48,176},{64,192},{80,208},{96,224},{112... | collective-permute-start | bytes 98312 | tf_op jit(solution)/shard_map/ppermute | solution.py:146
  147.6 0.0 collective-permute-done.2
  147.6 2.7 %collective-permute-start.11 = (s32[4,4,4,128]{3,2,1,0:T(4,128)S(1)}, s32[4,4,4,128]{3,2,1,0:T(4,128)S(1)}, u32[]{:S(2)}, u32[]{:S(2)}) collective-permute-start(s32[4,4,4,128]{3,2,1,0:T(4,128)S(1)} %pad_add_fusion.refs_4_), channel_id=1, source_target_pairs={{0,192},{16,208},{32,224},{48,240},{64,0},{80,16},{96,32},{112,48}... | collective-permute-start | bytes 98312 | tf_op jit(solution)/shard_map/ppermute | solution.py:146
  150.3 0.0 collective-permute-done.1
  150.3 0.0 collective-permute-done
  150.3 0.3 collective-permute-start.3
  150.6 2.1 %collective-permute-start.4 = (f32[4,4,4,128]{3,2,1,0:T(4,128)S(1)}, f32[4,4,4,128]{3,2,1,0:T(4,128)S(1)}, u32[]{:S(2)}, u32[]{:S(2)}) collective-permute-start(f32[4,4,4,128]{3,2,1,0:T(4,128)S(1)} %pad_maximum_fusion.refs_0_), channel_id=1, source_target_pairs={{0,128},{16,144},{32,160},{48,176},{64,192},{80,208},{96,224},{112... | collective-permute-start | bytes 98312 | tf_op jit(solution)/shard_map/ppermute | solution.py:146
  152.8 0.0 collective-permute-done.9.refs_5_
  152.8 2.8 %collective-permute-start.5 = (f32[4,4,4,128]{3,2,1,0:T(4,128)S(1)}, f32[4,4,4,128]{3,2,1,0:T(4,128)S(1)}, u32[]{:S(2)}, u32[]{:S(2)}) collective-permute-start(f32[4,4,4,128]{3,2,1,0:T(4,128)S(1)} %pad_maximum_fusion.refs_0_), channel_id=1, source_target_pairs={{0,192},{16,208},{32,224},{48,240},{64,0},{80,16},{96,32},{112,48}... | collective-permute-start | bytes 98312 | tf_op jit(solution)/shard_map/ppermute | solution.py:146
  155.5 0.0 collective-permute-done.10.refs_6_
  155.5 0.0 collective-permute-done.11.refs_7_
  155.5 0.9 collective-permute-done.3.refs_1_
  156.4 2.4 %collective-permute-done.4.refs_2_ = f32[4,4,4,128]{3,2,1,0:T(4,128)S(1)} collective-permute-done((f32[4,4,4,128]{3,2,1,0:T(4,128)S(1)}, f32[4,4,4,128]{3,2,1,0:T(4,128)S(1)}, u32[]{:S(2)}, u32[]{:S(2)}) %collective-permute-start.4) | collective-permute-done | bytes 32800 | tf_op jit(solution)/shard_map/ppermute | solution.py:146
  158.8 0.2 collective-permute-done.5.refs_3_
  159.0 16.6 %decode.1 = f32[512,512]{1,0:T(8,128)} custom-call(f32[4,4,4,128]{3,2,1,0:T(4,128)S(1)} %pad_maximum_fusion.refs_0_, f32[4,4,4,128]{3,2,1,0:T(4,128)S(1)} %collective-permute-done.3.refs_1_, f32[4,4,4,128]{3,2,1,0:T(4,128)S(1)} %collective-permute-done.4.refs_2_, f32[4,4,4,128]{3,2,1,0:T(4,128)S(1)} %collective-permute-done.5.refs_3_, ...), custom_call_target="tpu_custom_call" | custom-call | tf_op jit(solution)/shard_map/decode/pallas_call | solution.py:182
  (2 shorter events, 0.0 us)
Async XLA Ops:
  24.6 6.1 %copy-start.2 = (s32[1,8,8,32]{3,2,1,0:T(8,128)S(1)}, s32[1,8,8,32]{3,2,1,0:T(8,128)}, u32[]{:S(2)}) copy-start(s32[1,8,8,32]{3,2,1,0:T(8,128)} %param.6) | copy-start | bytes 24580
  24.6 101.5 %copy-start = (bf16[2,2,256,256]{3,2,1,0:T(8,128)(2,1)S(1)}, bf16[2,2,256,256]{3,2,1,0:T(8,128)(2,1)}, u32[]{:S(2)}) copy-start(bf16[2,2,256,256]{3,2,1,0:T(8,128)(2,1)} %constant.2.clone.basis_ref.refs_8_) | copy-start | bytes 1572868
  24.6 101.5 %copy-start.1 = (f32[512,512]{1,0:T(8,128)S(1)}, f32[512,512]{1,0:T(8,128)}, u32[]{:S(2)}) copy-start(f32[512,512]{1,0:T(8,128)} %momentum_ref.1) | copy-start | bytes 3145732
  24.6 101.5 %all-to-all-start = ((bf16[16,512,512]{2,1,0:T(8,128)(2,1)}), bf16[16,512,512]{2,1,0:T(8,128)(2,1)}, u32[]{:S(2)}, u32[]{:S(2)}) async-start(bf16[16,512,512]{2,1,0:T(8,128)(2,1)} %bitcast.14), calls=%async_computation | async-start | bytes 16777216 | tf_op jit(solution)/shard_map/all_to_all | solution.py:158
  30.8 107.3 %collective-permute-start.8 = (s32[4,4,128]{2,1,0:T(4,128)S(1)}, s32[4,4,128]{2,1,0:T(4,128)S(1)}, u32[]{:S(2)}, u32[]{:S(2)}) collective-permute-start(s32[4,4,128]{2,1,0:T(4,128)S(1)} %reshape.7.pos_ref), channel_id=1, source_target_pairs={{0,48},{16,0},{32,16},{48,32},{64,112},{80,64},{96,80},{112,96},{1... | collective-permute-start | bytes 24584 | tf_op jit(solution)/shard_map/ppermute | solution.py:144
  31.7 108.1 %collective-permute-start.7 = (s32[4,4,128]{2,1,0:T(4,128)S(1)}, s32[4,4,128]{2,1,0:T(4,128)S(1)}, u32[]{:S(2)}, u32[]{:S(2)}) collective-permute-start(s32[4,4,128]{2,1,0:T(4,128)S(1)} %reshape.7.pos_ref), channel_id=1, source_target_pairs={{0,32},{16,48},{32,0},{48,16},{64,96},{80,112},{96,64},{112,80},{1... | collective-permute-start | bytes 24584 | tf_op jit(solution)/shard_map/ppermute | solution.py:144
  33.4 106.4 %collective-permute-start.6 = (s32[4,4,128]{2,1,0:T(4,128)S(1)}, s32[4,4,128]{2,1,0:T(4,128)S(1)}, u32[]{:S(2)}, u32[]{:S(2)}) collective-permute-start(s32[4,4,128]{2,1,0:T(4,128)S(1)} %reshape.7.pos_ref), channel_id=1, source_target_pairs={{0,16},{16,32},{32,48},{48,0},{64,80},{80,96},{96,112},{112,64},{1... | collective-permute-start | bytes 24584 | tf_op jit(solution)/shard_map/ppermute | solution.py:144
  135.7 11.9 %collective-permute-start.2 = (f32[4,4,128]{2,1,0:T(4,128)S(1)}, f32[4,4,128]{2,1,0:T(4,128)S(1)}, u32[]{:S(2)}, u32[]{:S(2)}) collective-permute-start(f32[4,4,128]{2,1,0:T(4,128)S(1)} %get-tuple-element.5), channel_id=1, source_target_pairs={{0,48},{16,0},{32,16},{48,32},{64,112},{80,64},{96,80},{112,96},{1... | collective-permute-start | bytes 24584 | tf_op jit(solution)/shard_map/ppermute | solution.py:144
  136.5 13.7 %collective-permute-start.1 = (f32[4,4,128]{2,1,0:T(4,128)S(1)}, f32[4,4,128]{2,1,0:T(4,128)S(1)}, u32[]{:S(2)}, u32[]{:S(2)}) collective-permute-start(f32[4,4,128]{2,1,0:T(4,128)S(1)} %get-tuple-element.5), channel_id=1, source_target_pairs={{0,32},{16,48},{32,0},{48,16},{64,96},{80,112},{96,64},{112,80},{1... | collective-permute-start | bytes 24584 | tf_op jit(solution)/shard_map/ppermute | solution.py:144
  138.2 12.1 %collective-permute-start = (f32[4,4,128]{2,1,0:T(4,128)S(1)}, f32[4,4,128]{2,1,0:T(4,128)S(1)}, u32[]{:S(2)}, u32[]{:S(2)}) collective-permute-start(f32[4,4,128]{2,1,0:T(4,128)S(1)} %get-tuple-element.5), channel_id=1, source_target_pairs={{0,16},{16,32},{32,48},{48,0},{64,80},{80,96},{96,112},{112,64},{1... | collective-permute-start | bytes 24584 | tf_op jit(solution)/shard_map/ppermute | solution.py:144
  139.8 13.0 %collective-permute-start.9 = (s32[4,4,4,128]{3,2,1,0:T(4,128)S(1)}, s32[4,4,4,128]{3,2,1,0:T(4,128)S(1)}, u32[]{:S(2)}, u32[]{:S(2)}) collective-permute-start(s32[4,4,4,128]{3,2,1,0:T(4,128)S(1)} %pad_add_fusion.refs_4_), channel_id=1, source_target_pairs={{0,64},{16,80},{32,96},{48,112},{64,128},{80,144},{96,160},{112,17... | collective-permute-start | bytes 98312 | tf_op jit(solution)/shard_map/ppermute | solution.py:146
  143.1 12.4 %collective-permute-start.10 = (s32[4,4,4,128]{3,2,1,0:T(4,128)S(1)}, s32[4,4,4,128]{3,2,1,0:T(4,128)S(1)}, u32[]{:S(2)}, u32[]{:S(2)}) collective-permute-start(s32[4,4,4,128]{3,2,1,0:T(4,128)S(1)} %pad_add_fusion.refs_4_), channel_id=1, source_target_pairs={{0,128},{16,144},{32,160},{48,176},{64,192},{80,208},{96,224},{112... | collective-permute-start | bytes 98312 | tf_op jit(solution)/shard_map/ppermute | solution.py:146
  147.6 7.9 %collective-permute-start.11 = (s32[4,4,4,128]{3,2,1,0:T(4,128)S(1)}, s32[4,4,4,128]{3,2,1,0:T(4,128)S(1)}, u32[]{:S(2)}, u32[]{:S(2)}) collective-permute-start(s32[4,4,4,128]{3,2,1,0:T(4,128)S(1)} %pad_add_fusion.refs_4_), channel_id=1, source_target_pairs={{0,192},{16,208},{32,224},{48,240},{64,0},{80,16},{96,32},{112,48}... | collective-permute-start | bytes 98312 | tf_op jit(solution)/shard_map/ppermute | solution.py:146
  150.3 6.1 %collective-permute-start.3 = (f32[4,4,4,128]{3,2,1,0:T(4,128)S(1)}, f32[4,4,4,128]{3,2,1,0:T(4,128)S(1)}, u32[]{:S(2)}, u32[]{:S(2)}) collective-permute-start(f32[4,4,4,128]{3,2,1,0:T(4,128)S(1)} %pad_maximum_fusion.refs_0_), channel_id=1, source_target_pairs={{0,64},{16,80},{32,96},{48,112},{64,128},{80,144},{96,160},{112,17... | collective-permute-start | bytes 98312 | tf_op jit(solution)/shard_map/ppermute | solution.py:146
  150.6 8.2 %collective-permute-start.4 = (f32[4,4,4,128]{3,2,1,0:T(4,128)S(1)}, f32[4,4,4,128]{3,2,1,0:T(4,128)S(1)}, u32[]{:S(2)}, u32[]{:S(2)}) collective-permute-start(f32[4,4,4,128]{3,2,1,0:T(4,128)S(1)} %pad_maximum_fusion.refs_0_), channel_id=1, source_target_pairs={{0,128},{16,144},{32,160},{48,176},{64,192},{80,208},{96,224},{112... | collective-permute-start | bytes 98312 | tf_op jit(solution)/shard_map/ppermute | solution.py:146
  152.8 6.2 %collective-permute-start.5 = (f32[4,4,4,128]{3,2,1,0:T(4,128)S(1)}, f32[4,4,4,128]{3,2,1,0:T(4,128)S(1)}, u32[]{:S(2)}, u32[]{:S(2)}) collective-permute-start(f32[4,4,4,128]{3,2,1,0:T(4,128)S(1)} %pad_maximum_fusion.refs_0_), channel_id=1, source_target_pairs={{0,192},{16,208},{32,224},{48,240},{64,0},{80,16},{96,32},{112,48}... | collective-permute-start | bytes 98312 | tf_op jit(solution)/shard_map/ppermute | solution.py:146

commit v2 on v1

v2 whole, which is shorter than its diff:
```python
import functools

import jax
import jax.numpy as jnp
import numpy as np
from jax import lax
from jax.experimental import pallas as pl
from jax.experimental.pallas import tpu as pltpu
from jax.sharding import PartitionSpec as P

GROUP = 64
K = 32
WIDE = 256
KEPT = 128
CHUNK = 128
DECAY = 0.9
BF = jnp.bfloat16
F32 = jnp.float32


def dct_constants():
    k = np.arange(GROUP)[:, None]
    n = np.arange(GROUP)[None, :]
    scale = np.where(k == 0, np.sqrt(1.0 / GROUP), np.sqrt(2.0 / GROUP))
    basis = scale * np.cos(np.pi * ((2 * n + 1) * k % (4 * GROUP)) / (2.0 * GROUP))
    wide = np.kron(np.eye(WIDE // GROUP), basis)
    both = np.stack([wide, wide.T]).astype(np.float32)
    high = both.astype(BF)
    low = (both - high.astype(np.float32)).astype(BF)
    return np.stack([high, low], axis=1)


def cut(x):
    high = x.astype(BF)
    return high, (x - high.astype(F32)).astype(BF)


def dot(a, b):
    return jnp.dot(a, b, preferred_element_type=F32)


def times_right(x, m_high, m_low):
    high, low = cut(x)
    return dot(high, m_high) + dot(high, m_low) + dot(low, m_high)


def times_left(m_high, m_low, x):
    high, low = cut(x)
    return dot(m_high, high) + dot(m_low, high) + dot(m_high, low)


def down_rows(m, x):
    step = min(x.shape[0], 2 * GROUP)
    high, low = m[0, :step, :step], m[1, :step, :step]
    parts = [times_left(high, low, x[i:i + step]) for i in range(0, x.shape[0], step)]
    return jnp.concatenate(parts, axis=0) if len(parts) > 1 else parts[0]


def forward(field, basis):
    return down_rows(basis[0], times_right(field, basis[1, 0], basis[1, 1]))


def inverse(coef, basis):
    return down_rows(basis[1], times_right(coef, basis[0, 0], basis[0, 1]))


def match(places, count):
    return lax.broadcasted_iota(jnp.int32, (count, places.shape[1]), 0) == places


def one(mask):
    return jnp.where(mask, F32(1.0), F32(0.0)).astype(BF)


def by_lanes(a, b):
    return lax.dot_general(a, b, (((1,), (1,)), ((), ())), preferred_element_type=F32)


def by_rows(a, b):
    return lax.dot_general(a, b, (((0,), (0,)), ((), ())), preferred_element_type=F32)


def encode(field, pos_ref, basis, shift, fresh_ref, kept_ref):
    rows, cols = field.shape
    lane_block = lax.broadcasted_iota(jnp.int32, (1, KEPT), 1) // K
    per_group = KEPT // K
    kept = [None] * (rows // GROUP * (cols // WIDE))
    for half in range(cols // WIDE):
        span = slice(half * WIDE, (half + 1) * WIDE)
        part = field[:, span]
        coef = forward(part, basis)
        dense = []
        for a in range(rows // GROUP):
            g = a * (cols // WIDE) + half
            block = coef[a * GROUP:(a + 1) * GROUP]
            pos = pos_ref[g:g + 1]
            on_col = match(pos % GROUP + lane_block * GROUP, WIDE)
            row_one = one(match(pos // GROUP, GROUP))
            chosen = by_lanes(row_one, one(on_col))
            dense.append(jnp.where(chosen > 0.5, block, F32(0.0)))
            high, low = cut(block)
            rest = (block - high.astype(F32) - low.astype(F32)).astype(BF)
            three = jnp.concatenate([high, low, rest], axis=0)
            rows_of = by_rows(three, jnp.concatenate([row_one] * 3, axis=0))
            found = jnp.where(on_col, rows_of, F32(0.0))
            lines = []
            for q in range(per_group):
                line = jnp.sum(found[q * GROUP:(q + 1) * GROUP], axis=0, keepdims=True)
                lines.append(pltpu.roll(line, (KEPT - q * K) % KEPT, 1) if q else line)
            kept[g] = jnp.concatenate(lines, axis=0)
        fresh_ref[:, span] = part - inverse(jnp.concatenate(dense, axis=0), basis)
    kept = jnp.concatenate(kept, axis=0)
    kept_ref[...] = pltpu.roll(kept, shift, 1)


LEVELS = 32767.0
STEPS = 511.0
PAD = 16


def put(ref, x):
    if ref.dtype == F32:
        ref[...] = x
        return
    rows = x.shape[0]
    scale = jnp.maximum(jnp.ceil(jnp.max(jnp.abs(x), axis=0, keepdims=True) * STEPS), 1.0)
    ref[:rows] = jnp.round(x * (LEVELS * STEPS / scale)).astype(jnp.int32).astype(jnp.int16)
    ref[rows:] = jnp.broadcast_to(scale, (PAD, x.shape[1])).astype(jnp.int32).astype(jnp.int16)


def get(ref):
    if ref.dtype == F32:
        return ref[...]
    rows = ref.shape[0] - PAD
    scale = ref[rows:].astype(jnp.int32).astype(F32)[:1]
    return ref[:rows].astype(jnp.int32).astype(F32) * (scale * (1.0 / (LEVELS * STEPS)))


def pack_kernel(at_ref, *refs):
    for i in range(len(refs) // 2):
        refs[len(refs) // 2 + i][...] = refs[i][...]


def far_kernel(at_ref, own0, own1, sib_ref, up_ref, down_ref):
    put(up_ref, own0[0].astype(F32) + sib_ref[0].astype(F32))
    put(down_ref, own1[0].astype(F32) + sib_ref[1].astype(F32))


def near_kernel(at_ref, up0, up1, down0, down1, sib_up, sib_down, far_up, far_down, up_ref, down_ref):
    put(up_ref.at[0], up0[0].astype(F32) + sib_up[0].astype(F32) + get(far_up))
    put(up_ref.at[1], up1[0].astype(F32) + sib_up[1].astype(F32))
    put(down_ref.at[0], down0[0].astype(F32) + sib_down[0].astype(F32))
    put(down_ref.at[1], down1[0].astype(F32) + sib_down[1].astype(F32) + get(far_down))


def cross_kernel(at_ref, own0, own1, sib_ref, up_ref, down_ref, own_ref, out_ref):
    put(out_ref, own1[0].astype(F32) + sib_ref[1].astype(F32) + (get(up_ref.at[1]) + get(down_ref.at[1])))
    own_ref[...] = own0[0].astype(F32) + sib_ref[0].astype(F32) + (get(up_ref.at[0]) + get(down_ref.at[0]))


def encode_kernel(at_ref, own_ref, cross_ref, momentum_ref, pos_ref, basis_ref, *refs):
    *before, fresh_ref, kept_ref = refs
    field = DECAY * momentum_ref[...] + (own_ref[...] + get(cross_ref))
    first = 0
    for ref in before:
        kept_ref[first:first + ref.shape[0]] = ref[...]
        first += ref.shape[0]
    encode(field, pos_ref, basis_ref, at_ref[3] * K, fresh_ref, kept_ref.at[first:])


def decode_kernel(at_ref, *refs):
    *sent, basis, out_ref = refs
    count = len(sent) // 2
    vals, poss = sent[:count], sent[count:]
    per_row = out_ref.shape[1] // GROUP
    dense = []
    for i in range(vals[0].shape[0]):
        val = jnp.concatenate([ref[i:i + 1] for ref in vals], axis=1)
        pos = jnp.concatenate([ref[i:i + 1] for ref in poss], axis=1).astype(jnp.int32)
        high, low = cut(jnp.where(match(pos // GROUP, GROUP), val, F32(0.0)))
        both = by_lanes(jnp.concatenate([high, low], axis=0), one(match(pos % GROUP, GROUP)))
        dense.append(both[:GROUP] + both[GROUP:])
    wide = WIDE // GROUP
    for half in range(out_ref.shape[1] // WIDE):
        lines = [
            jnp.concatenate(dense[a + half * wide:a + (half + 1) * wide], axis=1)
            for a in range(0, len(dense), per_row)
        ]
        out_ref[:, half * WIDE:(half + 1) * WIDE] = inverse(jnp.concatenate(lines, axis=0), basis)


def across(n_hi, n_x, shift_hi, shift_x):
    return [
        (h * n_x + x, (h + shift_hi) % n_hi * n_x + (x + shift_x) % n_x)
        for h in range(n_hi)
        for x in range(n_x)
    ]


def along_x(own):
    return [own] + [lax.ppermute(own, "rep", across(4, 4, 0, s)) for s in (1, 2, 3)]


def along_z(near):
    return [near] + [lax.ppermute(near, "rep", across(4, 4, s, 0)) for s in (1, 2, 3)]


def places(shift_y, flip_z, flip_core):
    return [
        ((y * 2 + z) * 2 + c, ((y + shift_y) % 4 * 2 + (z ^ flip_z)) * 2 + (c ^ flip_core))
        for y in range(4)
        for z in range(2)
        for c in range(2)
    ]


def send(x, shift_y=0, flip_z=0, flip_core=0):
    return lax.ppermute(x, "fsdp", places(shift_y, flip_z, flip_core))


def piece(at, dy, dz, flip_core=0):
    return ((at[0] + dy) % 4 * 2 + (at[1] + dz) % 2) * 2 + (at[2] + flip_core) % 2


class Program:
    def __init__(self, at):
        self.at = at
        self.last = None

    def call(self, body, name, ins, outs, grid=(1,), onto=None):
        operands, specs = map(list, zip(*ins))
        count = len(operands)
        extra = [x for x in (onto, self.last) if x is not None]
        operands += extra
        specs += [pl.BlockSpec(memory_space=pl.ANY)] * len(extra)

        def kernel(at_ref, *refs):
            body(at_ref, *refs[:count], *refs[count + len(extra):])

        results = pl.pallas_call(
            kernel,
            grid_spec=pltpu.PrefetchScalarGridSpec(
                num_scalar_prefetch=1,
                grid=grid,
                in_specs=specs,
                out_specs=[spec for _, spec in outs],
            ),
            out_shape=[shape for shape, _ in outs],
            input_output_aliases={} if onto is None else {count + 1: 0},
            compiler_params=pltpu.CompilerParams(vmem_limit_bytes=VMEM),
            name=name,
        )(self.at, *operands)
        self.last = results[-1]
        return results


def whole(x):
    return x, pl.BlockSpec(x.shape, lambda s, at: (0,) * x.ndim)


class Chunk:
    def __init__(self, program, slab, start, rows, cols):
        self.program, self.call = program, program.call
        self.slab, self.rows, self.cols = slab, rows, cols
        self.start, self.index = start, start // rows

    def own(self, dy, dz):
        i, k = self.index, dy * 2 + dz
        return self.program.own, pl.BlockSpec((1, self.rows, self.cols), lambda s, at: (k, i, 0))

    def part(self, x, first, count):
        return x, pl.BlockSpec((count, *x.shape[1:]), lambda s, at: (first // count, 0, 0))

    def out(self, kind, *lead):
        shape = (*lead, self.rows + (0 if kind == F32 else PAD), self.cols)
        return jax.ShapeDtypeStruct(shape, kind), pl.BlockSpec(shape, lambda s, at: (0,) * len(shape))

    def pack(self, own_too):
        i, rows, cols, height = self.index, self.rows, self.cols, self.slab.shape[1]
        slab_spec = pl.BlockSpec((1, rows, cols), lambda s, at: (0, i, piece(at, s // 2, s % 2, 1)))
        out_spec = pl.BlockSpec((1, rows, cols), lambda s, at: (s, 0, 0))
        ins = [(self.slab, slab_spec)]
        outs = [(jax.ShapeDtypeStruct((8, rows, cols), BF), out_spec)]
        if own_too:
            ins.append((self.slab, pl.BlockSpec((1, height, cols), lambda s, at: (0, 0, piece(at, s // 2, s % 2)))))
            outs.append((jax.ShapeDtypeStruct((8, height, cols), BF),
                         pl.BlockSpec((1, height, cols), lambda s, at: (s, 0, 0))))
        packed, *own = self.call(pack_kernel, "pack", ins, outs, (8,))
        if own_too:
            self.program.own = own[0]
        self.sib = send(packed, flip_core=1)

    def far(self):
        up, down = self.call(
            far_kernel, "far", [self.own(2, 0), self.own(2, 1), self.part(self.sib, 4, 2)],
            [self.out(KINDS[0]), self.out(KINDS[0])],
        )
        self.far_up, self.far_down = send(up, shift_y=1), send(down, shift_y=-1)

    def near(self):
        up, down = self.call(
            near_kernel, "near",
            [self.own(1, 0), self.own(1, 1), self.own(3, 0), self.own(3, 1), self.part(self.sib, 2, 2),
             self.part(self.sib, 6, 2), whole(self.far_up), whole(self.far_down)],
            [self.out(KINDS[1], 2), self.out(KINDS[1], 2)],
        )
        self.up, self.down = send(up, shift_y=1), send(down, shift_y=-1)

    def cross(self):
        self.mine, cross = self.call(
            cross_kernel, "cross",
            [self.own(0, 0), self.own(0, 1), self.part(self.sib, 0, 2), whole(self.up), whole(self.down)],
            [self.out(F32), self.out(KINDS[2])],
        )
        self.crossed = send(cross, flip_z=1)

    def encode(self, momentum, pos, basis, onto, before):
        rows, cols, i = self.rows, self.cols, self.index
        groups = rows // GROUP * (cols // WIDE)
        first = self.start // GROUP * (cols // WIDE)
        pos = pos[first:first + groups]
        height = rows // GROUP * (cols // GROUP) + sum(x.shape[0] for x in before)
        self.fresh, self.kept = self.call(
            encode_kernel, "encode",
            [whole(self.mine), whole(self.crossed), (momentum, pl.BlockSpec((rows, cols), lambda s, at: (i, 0))),
             whole(pos), whole(basis), *map(whole, before)],
            [(jax.ShapeDtypeStruct(momentum.shape, F32), pl.BlockSpec((rows, cols), lambda s, at: (i, 0))),
             (jax.ShapeDtypeStruct((height, KEPT), F32), pl.BlockSpec((height, KEPT), lambda s, at: (0, 0)))],
            onto=onto,
        )


CHUNKS = (256, 256)
PLAN = "P0 P1 F0 F1 N0 N1 X0 E0 X1 E1 G0,1 D0,1"
KINDS = (jnp.int16,) * 3
VMEM = 16 * 1024 * 1024


STEP = 128


def local(partial_grads, momentum, freq_index):
    rows, cols = momentum.shape
    basis = jnp.asarray(dct_constants())
    pos = freq_index.reshape(rows // GROUP * (cols // WIDE), KEPT)
    me, rep = lax.axis_index("fsdp"), lax.axis_index("rep")
    at = jnp.stack([me // 4, me // 2 % 2, me % 2, rep % 4]).astype(jnp.int32)
    lines = jnp.tile(freq_index.reshape(rows // GROUP * (cols // GROUP), K).astype(F32), (1, KEPT // K))
    lines = jnp.where(jnp.arange(KEPT)[None] // K == rep % 4, lines, F32(0.0))
    program = Program(at)
    starts = np.cumsum((0,) + CHUNKS)[:-1]
    work = [Chunk(program, partial_grads, int(s), r, cols) for s, r in zip(starts, CHUNKS)]
    per_step = STEP // GROUP * (cols // GROUP)
    fresh = update = None
    before = [lines]
    for step in PLAN.split():
        kind, which = step[0], [work[int(i)] for i in step[1:].split(",")]
        chunk = which[0]
        if kind == "P":
            chunk.pack(chunk is work[-1])
        elif kind == "F":
            chunk.far()
        elif kind == "N":
            chunk.near()
        elif kind == "X":
            chunk.cross()
        elif kind == "E":
            chunk.encode(momentum, pos, basis, fresh, before)
            fresh, before = chunk.fresh, [chunk.kept]
        elif kind == "G":
            sent = along_z(sum(along_x(before[0])))
        else:
            first, steps = chunk.start // STEP, rows // STEP
            val_spec = pl.BlockSpec((per_step, KEPT), lambda s, at: (steps + first + s, 0))
            pos_spec = pl.BlockSpec((per_step, KEPT), lambda s, at: (first + s, 0))
            update, = program.call(
                decode_kernel, "decode",
                [(x, val_spec) for x in sent] + [(x, pos_spec) for x in sent] + [whole(basis)],
                [(jax.ShapeDtypeStruct((rows, cols), F32), pl.BlockSpec((STEP, cols), lambda s, at: (first + s, 0)))],
                (sum(c.rows for c in which) // STEP,),
                onto=update,
            )
    return fresh, update


def solution(mesh):
    return jax.shard_map(
        local,
        mesh=mesh,
        in_specs=(P(("rep", "fsdp"), None, None), P("rep", "fsdp"), P("rep", None, "fsdp", None)),
        out_specs=(P("rep", "fsdp"), P(None, "fsdp")),
        check_vma=False,
    )
```

time: 178 us -> 112 us (0.63); the launches traced: 176 us -> 112 us
  waiting for transfers between devices: 94.6 us -> 37.7 us
  local copies, waits for them, and re-layouts: 24.2 us -> 13.9 us
  starting transfers between devices: 29.9 us -> 31.7 us
    all_to_all x1 -> x0, waiting for transfers between devices: 91.1 us -> none  [local(): terms = lax.all_to_all(slab, 'fsdp', 0, 0, tiled=True)]
    ppermute x12 -> x18, waiting for transfers between devices: 3.46 us -> 37.7 us  [the longest x12 29.1 us: send(): return lax.ppermute(x, 'fsdp', places(shift_y, flip_z, flip_core))]
    another operation x2, local copies, waits for them, and re-layouts: 12.4 us -> 0.72 us  [local(): jnp.tile(freq_index.reshape(rows // GROUP * (cols // GROUP), K).astype(F3...]
    ppermute x12 -> x18, starting transfers between devices: 23.8 us -> 31.7 us  [the longest x12 17.5 us: send(): return lax.ppermute(x, 'fsdp', places(shift_y, flip_z, flip_core))]
    all_to_all x1 -> x0, starting transfers between devices: 6.12 us -> none  [local(): terms = lax.all_to_all(slab, 'fsdp', 0, 0, tiled=True)]
    pallas_call x2 -> x11, Pallas kernels: 26.2 us -> 26.9 us  [call(): pl.pallas_call(kernel, grid_spec=pltpu.PrefetchScalarGridSpec(num_scalar_...]
    unnamed x7 -> x24, local copies, waits for them, and re-layouts: 11.7 us -> 11.7 us
  transfers between devices with their start and end apart: 13 -> 18, of which waited for: 4 -> 10; matrix products, arithmetic and copies ran while one was open for 0% -> 3% of each run, Pallas kernels for 5% -> 10%
where the time goes in v2:
time: 112 us
  waiting for transfers between devices  37.7 us (34%)
  starting transfers between devices  31.7 us (28%)
  Pallas kernels  26.9 us (24%)
  local copies, waits for them, and re-layouts  13.9 us (12%)
    ppermute x12, waiting for transfers between devices, send(): return lax.ppermute(x, 'fsdp', places(shift_y, flip_z, flip_core))  29.1 us
    pallas_call x11, Pallas kernels, call(): pl.pallas_call(kernel, grid_spec=pltpu.PrefetchScalarGridSpec(num_scalar_...  26.9 us
    ppermute x12, starting transfers between devices, send(): return lax.ppermute(x, 'fsdp', places(shift_y, flip_z, flip_core))  17.5 us
    unnamed x24, local copies, waits for them, and re-layouts  11.7 us
    ppermute x3, starting transfers between devices, along_z(): lax.ppermute(near, 'rep', across(4, 4, s, 0))  11.2 us
    ppermute x3, waiting for transfers between devices, along_x(): lax.ppermute(own, 'rep', across(4, 4, 0, s))  5.59 us
    ppermute x3, waiting for transfers between devices, along_z(): lax.ppermute(near, 'rep', across(4, 4, s, 0))  2.99 us
    ppermute x3, starting transfers between devices, along_x(): lax.ppermute(own, 'rep', across(4, 4, 0, s))  2.9 us
  transfers between devices with their start and end apart: 18, of which 10 were waited for; matrix products, arithmetic and copies ran while one was open for 3% of the time, Pallas kernels for 10%

profile of v2, /device:TPU:6, one launch (start us, length us, event | category | flops | bytes accessed | tf_op | source)
XLA Modules:
  0.0 111.9 jit_solution(3252657425576205165)
XLA Ops:
  0.7 0.1 pad_add_fusion.at_ref
  0.8 3.4 %copy-done.2 = bf16[1,512,8192]{2,1,0:T(8,128)(2,1)S(1)} copy-done((bf16[1,512,8192]{2,1,0:T(8,128)(2,1)S(1)}, bf16[1,512,8192]{2,1,0:T(8,128)(2,1)}, u32[]{:S(2)}) %copy-start.2) | copy-done | bytes 8388632
  4.1 1.4 %pack.2.refs_2_ = bf16[8,256,512]{2,1,0:T(8,128)(2,1)S(1)} custom-call(s32[4]{0:T(128)S(1)} %pad_add_fusion.at_ref, bf16[1,512,8192]{2,1,0:T(8,128)(2,1)S(1)} %copy-done.2), custom_call_target="tpu_custom_call" | custom-call | tf_op jit(solution)/shard_map/pack/pallas_call | solution.py:240
  5.5 0.1 collective-permute-start.1
  5.6 2.1 %pack.3 = (bf16[8,256,512]{2,1,0:T(8,128)(2,1)S(1)}, bf16[8,512,512]{2,1,0:T(8,128)(2,1)S(1)}) custom-call(s32[4]{0:T(128)S(1)} %pad_add_fusion.at_ref, bf16[1,512,8192]{2,1,0:T(8,128)(2,1)S(1)} %copy-done.2, bf16[1,512,8192]{2,1,0:T(8,128)(2,1)S(1)} %copy-done.2, bf16[8,256,512]{2,1,0:T(8,128)(2,1)S(1)} %pack.2.refs_2_), custom_call_target="tpu_custom_call" | custom-call | tf_op jit(solution)/shard_map/pack/pallas_call | solution.py:240
  7.7 0.6 collective-permute-start
  8.3 1.4 %collective-permute-done.1.refs_2_.refs_4_.refs_5_ = bf16[8,256,512]{2,1,0:T(8,128)(2,1)S(1)} collective-permute-done((bf16[8,256,512]{2,1,0:T(8,128)(2,1)S(1)}, bf16[8,256,512]{2,1,0:T(8,128)(2,1)S(1)}, u32[]{:S(2)}, u32[]{:S(2)}) %collective-permute-start.1) | collective-permute-done | bytes 2097184 | tf_op jit(solution)/shard_map/ppermute | solution.py:218
  9.8 0.8 far.2
  10.5 1.7 %collective-permute-start.4 = (s16[272,512]{1,0:T(8,128)(2,1)S(1)}, s16[272,512]{1,0:T(8,128)(2,1)S(1)}, u32[]{:S(2)}, u32[]{:S(2)}) collective-permute-start(s16[272,512]{1,0:T(8,128)(2,1)S(1)} %get-tuple-element.25), channel_id=1, source_target_pairs={{0,4},{1,5},{2,6},{3,7},{4,8},{5,9},{6,10},{7,11},{8,12},{9,13},{1... | collective-permute-start | bytes 835592 | tf_op jit(solution)/shard_map/ppermute | solution.py:218
  12.2 1.7 %collective-permute-start.5 = (s16[272,512]{1,0:T(8,128)(2,1)S(1)}, s16[272,512]{1,0:T(8,128)(2,1)S(1)}, u32[]{:S(2)}, u32[]{:S(2)}) collective-permute-start(s16[272,512]{1,0:T(8,128)(2,1)S(1)} %get-tuple-element.22.refs_3_), channel_id=1, source_target_pairs={{0,12},{1,13},{2,14},{3,15},{4,0},{5,1},{6,2},{7,3},{8,4},{9,5},{1... | collective-permute-start | bytes 835592 | tf_op jit(solution)/shard_map/ppermute | solution.py:218
  13.9 0.0 collective-permute-done.refs_2_.refs_4_.refs_5_
  13.9 0.8 far.3
  14.7 5.9 %collective-permute-done.4.refs_6_ = s16[272,512]{1,0:T(8,128)(2,1)S(1)} collective-permute-done((s16[272,512]{1,0:T(8,128)(2,1)S(1)}, s16[272,512]{1,0:T(8,128)(2,1)S(1)}, u32[]{:S(2)}, u32[]{:S(2)}) %collective-permute-start.4) | collective-permute-done | bytes 278560 | tf_op jit(solution)/shard_map/ppermute | solution.py:218
  20.6 0.0 collective-permute-done.5.refs_7_
  20.6 1.2 %near.2 = (s16[2,272,512]{2,1,0:T(8,128)(2,1)S(1)}, s16[2,272,512]{2,1,0:T(8,128)(2,1)S(1)}) custom-call(s32[4]{0:T(128)S(1)} %pad_add_fusion.at_ref, bf16[8,512,512]{2,1,0:T(8,128)(2,1)S(1)} %get-tuple-element.20.refs_0_.refs_1_.refs_3_.refs_2_, bf16[8,512,512]{2,1,0:T(8,128)(2,1)S(1)} %get-tuple-element.20.refs_0_.refs_1_.refs_3_.refs_2_, ...), custom_call_target="tpu_custom_call" | custom-call | tf_op jit(solution)/shard_map/near/pallas_call | solution.py:240
  21.8 1.7 %collective-permute-start.8 = (s16[2,272,512]{2,1,0:T(8,128)(2,1)S(1)}, s16[2,272,512]{2,1,0:T(8,128)(2,1)S(1)}, u32[]{:S(2)}, u32[]{:S(2)}) collective-permute-start(s16[2,272,512]{2,1,0:T(8,128)(2,1)S(1)} %get-tuple-element.29), channel_id=1, source_target_pairs={{0,4},{1,5},{2,6},{3,7},{4,8},{5,9},{6,10},{7,11},{8,12},{9,13},{1... | collective-permute-start | bytes 1671176 | tf_op jit(solution)/shard_map/ppermute | solution.py:218
  23.4 1.7 %collective-permute-start.9 = (s16[2,272,512]{2,1,0:T(8,128)(2,1)S(1)}, s16[2,272,512]{2,1,0:T(8,128)(2,1)S(1)}, u32[]{:S(2)}, u32[]{:S(2)}) collective-permute-start(s16[2,272,512]{2,1,0:T(8,128)(2,1)S(1)} %get-tuple-element.26.refs_8_), channel_id=1, source_target_pairs={{0,12},{1,13},{2,14},{3,15},{4,0},{5,1},{6,2},{7,3},{8,4},{9,5},{1... | collective-permute-start | bytes 1671176 | tf_op jit(solution)/shard_map/ppermute | solution.py:218
  25.1 0.4 collective-permute-start.2
  25.5 2.9 %collective-permute-start.3 = (s16[272,512]{1,0:T(8,128)(2,1)S(1)}, s16[272,512]{1,0:T(8,128)(2,1)S(1)}, u32[]{:S(2)}, u32[]{:S(2)}) collective-permute-start(s16[272,512]{1,0:T(8,128)(2,1)S(1)} %get-tuple-element.24.refs_8_), channel_id=1, source_target_pairs={{0,12},{1,13},{2,14},{3,15},{4,0},{5,1},{6,2},{7,3},{8,4},{9,5},{1... | collective-permute-start | bytes 835592 | tf_op jit(solution)/shard_map/ppermute | solution.py:218
  28.4 14.6 %collective-permute-done.2.refs_6_ = s16[272,512]{1,0:T(8,128)(2,1)S(1)} collective-permute-done((s16[272,512]{1,0:T(8,128)(2,1)S(1)}, s16[272,512]{1,0:T(8,128)(2,1)S(1)}, u32[]{:S(2)}, u32[]{:S(2)}) %collective-permute-start.2) | collective-permute-done | bytes 278560 | tf_op jit(solution)/shard_map/ppermute | solution.py:218
  42.9 0.0 collective-permute-done.3.refs_7_
  42.9 2.0 %near.3 = (s16[2,272,512]{2,1,0:T(8,128)(2,1)}, s16[2,272,512]{2,1,0:T(8,128)(2,1)}) custom-call(s32[4]{0:T(128)S(1)} %pad_add_fusion.at_ref, bf16[8,512,512]{2,1,0:T(8,128)(2,1)S(1)} %get-tuple-element.20.refs_0_.refs_1_.refs_3_.refs_2_, bf16[8,512,512]{2,1,0:T(8,128)(2,1)S(1)} %get-tuple-element.20.refs_0_.refs_1_.refs_3_.refs_2_, ...), custom_call_target="tpu_custom_call" | custom-call | tf_op jit(solution)/shard_map/near/pallas_call | solution.py:240
  44.9 1.0 collective-permute-start.6
  46.0 2.2 %collective-permute-start.7 = (s16[2,272,512]{2,1,0:T(8,128)(2,1)}, s16[2,272,512]{2,1,0:T(8,128)(2,1)}, u32[]{:S(2)}, u32[]{:S(2)}) collective-permute-start(s16[2,272,512]{2,1,0:T(8,128)(2,1)} %get-tuple-element.28.refs_5_), channel_id=1, source_target_pairs={{0,12},{1,13},{2,14},{3,15},{4,0},{5,1},{6,2},{7,3},{8,4},{9,5},{1... | collective-permute-start | bytes 1671176 | tf_op jit(solution)/shard_map/ppermute | solution.py:218
  48.2 0.6 fusion.1
  48.8 0.0 collective-permute-done.8.refs_3_
  48.8 0.0 collective-permute-done.9.refs_4_
  48.8 1.1 %cross.2 = (f32[256,512]{1,0:T(8,128)S(1)}, s16[272,512]{1,0:T(8,128)(2,1)S(1)}) custom-call(s32[4]{0:T(128)S(1)} %pad_add_fusion.at_ref, bf16[8,512,512]{2,1,0:T(8,128)(2,1)S(1)} %get-tuple-element.20.refs_0_.refs_1_.refs_3_.refs_2_, bf16[8,512,512]{2,1,0:T(8,128)(2,1)S(1)} %get-tuple-element.20.refs_0_.refs_1_.refs_3_.refs_2_, ...), custom_call_target="tpu_custom_call" | custom-call | tf_op jit(solution)/shard_map/cross/pallas_call | solution.py:240
  50.0 0.0 copy-start.8
  50.0 0.8 copy-done.8
  50.8 1.9 %collective-permute-start.10 = (s16[272,512]{1,0:T(8,128)(2,1)S(1)}, s16[272,512]{1,0:T(8,128)(2,1)}, u32[]{:S(2)}, u32[]{:S(2)}) collective-permute-start(s16[272,512]{1,0:T(8,128)(2,1)S(1)} %get-tuple-element.31.refs_6_), channel_id=1, source_target_pairs={{0,2},{1,3},{2,0},{3,1},{4,6},{5,7},{6,4},{7,5},{8,10},{9,11},{10,... | collective-permute-start | bytes 835592 | tf_op jit(solution)/shard_map/ppermute | solution.py:218
  52.7 0.1 copy.7
  52.8 0.7 copy.8
  53.5 0.8 slice.13.refs_3_
  54.3 0.8 broadcast_select_fusion.refs_5_
  55.0 2.4 %collective-permute-done.10.refs_1_ = s16[272,512]{1,0:T(8,128)(2,1)} collective-permute-done((s16[272,512]{1,0:T(8,128)(2,1)S(1)}, s16[272,512]{1,0:T(8,128)(2,1)}, u32[]{:S(2)}, u32[]{:S(2)}) %collective-permute-start.10) | collective-permute-done | bytes 278560 | tf_op jit(solution)/shard_map/ppermute | solution.py:218
  57.5 1.2 %copy-done.4 = f32[512,512]{1,0:T(8,128)S(1)} copy-done((f32[512,512]{1,0:T(8,128)S(1)}, f32[512,512]{1,0:T(8,128)}, u32[]{:S(2)}) %copy-start.4) | copy-done | bytes 1048600
  58.7 1.0 copy-done.9
  59.7 4.7 %encode.2 = (f32[512,512]{1,0:T(8,128)}, f32[96,128]{1,0:T(8,128)S(1)}) custom-call(s32[4]{0:T(128)S(1)} %pad_add_fusion.at_ref, f32[256,512]{1,0:T(8,128)S(1)} %copy-done.9, s16[272,512]{1,0:T(8,128)(2,1)} %collective-permute-done.10.refs_1_, f32[512,512]{1,0:T(8,128)S(1)} %copy-done.4, s32[8,128]{1,0:T(8,128)S(1)} %slice.13.refs_3_, ...), custom_call_target="tpu_custom_call" | custom-call | tf_op jit(solution)/shard_map/encode/pallas_call | solution.py:240
  64.4 0.0 collective-permute-done.6.refs_3_
  64.4 0.0 collective-permute-done.7.refs_4_
  64.4 2.2 %copy-done.1 = bf16[8,512,512]{2,1,0:T(8,128)(2,1)S(1)} copy-done((bf16[8,512,512]{2,1,0:T(8,128)(2,1)S(1)}, bf16[8,512,512]{2,1,0:T(8,128)(2,1)}, u32[]{:S(2)}) %copy-start.1) | copy-done | bytes 4194328
  66.6 2.2 %cross.3 = (f32[256,512]{1,0:T(8,128)S(1)}, s16[272,512]{1,0:T(8,128)(2,1)S(1)}) custom-call(s32[4]{0:T(128)S(1)} %pad_add_fusion.at_ref, bf16[8,512,512]{2,1,0:T(8,128)(2,1)S(1)} %copy-done.1, bf16[8,512,512]{2,1,0:T(8,128)(2,1)S(1)} %copy-done.1, bf16[8,256,512]{2,1,0:T(8,128)(2,1)S(1)} %collective-permute-done.refs_2_.refs_4_.refs_5_, ...), custom_call_target="tpu_custom_call" | custom-call | tf_op jit(solution)/shard_map/cross/pallas_call | solution.py:240
  68.8 0.0 copy-start.6
  68.8 0.8 copy-done.6
  69.6 1.9 %collective-permute-start.11 = (s16[272,512]{1,0:T(8,128)(2,1)S(1)}, s16[272,512]{1,0:T(8,128)(2,1)S(1)}, u32[]{:S(2)}, u32[]{:S(2)}) collective-permute-start(s16[272,512]{1,0:T(8,128)(2,1)S(1)} %get-tuple-element.34.refs_7_), channel_id=1, source_target_pairs={{0,2},{1,3},{2,0},{3,1},{4,6},{5,7},{6,4},{7,5},{8,10},{9,11},{10,... | collective-permute-start | bytes 835592 | tf_op jit(solution)/shard_map/ppermute | solution.py:218
  71.5 0.1 slice.15.refs_3_
  71.5 4.6 %collective-permute-done.11.refs_1_ = s16[272,512]{1,0:T(8,128)(2,1)S(1)} collective-permute-done((s16[272,512]{1,0:T(8,128)(2,1)S(1)}, s16[272,512]{1,0:T(8,128)(2,1)S(1)}, u32[]{:S(2)}, u32[]{:S(2)}) %collective-permute-start.11) | collective-permute-done | bytes 278560 | tf_op jit(solution)/shard_map/ppermute | solution.py:218
  76.2 1.2 %copy-done.5 = f32[512,512]{1,0:T(8,128)S(1)} copy-done((f32[512,512]{1,0:T(8,128)S(1)}, f32[512,512]{1,0:T(8,128)}, u32[]{:S(2)}) %copy-start.5) | copy-done | bytes 1048600
  77.4 1.0 copy-done.7
  78.4 3.7 %encode.3 = (f32[512,512]{1,0:T(8,128)}, f32[128,128]{1,0:T(8,128)S(1)}) custom-call(s32[4]{0:T(128)S(1)} %pad_add_fusion.at_ref, f32[256,512]{1,0:T(8,128)S(1)} %copy-done.7, s16[272,512]{1,0:T(8,128)(2,1)S(1)} %collective-permute-done.11.refs_1_, f32[512,512]{1,0:T(8,128)S(1)} %copy-done.5, ...), custom_call_target="tpu_custom_call", output_to_operand_aliasing={{0}: (7, {})} | custom-call | tf_op jit(solution)/shard_map/encode/pallas_call | solution.py:240
  82.1 2.0 %collective-permute-start.12 = (f32[128,128]{1,0:T(8,128)S(1)}, f32[128,128]{1,0:T(8,128)S(1)}, u32[]{:S(2)}, u32[]{:S(2)}) collective-permute-start(f32[128,128]{1,0:T(8,128)S(1)} %get-tuple-element.37.refs_9_), channel_id=1, source_target_pairs={{0,16},{16,32},{32,48},{48,0},{64,80},{80,96},{96,112},{112,64},{1... | collective-permute-start | bytes 196616 | tf_op jit(solution)/shard_map/ppermute | solution.py:201
  84.1 0.9 collective-permute-start.13
  85.0 0.0 collective-permute-start.14
  85.0 1.6 %collective-permute-done.12 = f32[128,128]{1,0:T(8,128)S(1)} collective-permute-done((f32[128,128]{1,0:T(8,128)S(1)}, f32[128,128]{1,0:T(8,128)S(1)}, u32[]{:S(2)}, u32[]{:S(2)}) %collective-permute-start.12) | collective-permute-done | bytes 65568 | tf_op jit(solution)/shard_map/ppermute | solution.py:201
  86.7 3.3 %collective-permute-done.13 = f32[128,128]{1,0:T(8,128)S(1)} collective-permute-done((f32[128,128]{1,0:T(8,128)S(1)}, f32[128,128]{1,0:T(8,128)S(1)}, u32[]{:S(2)}, u32[]{:S(2)}) %collective-permute-start.13) | collective-permute-done | bytes 65568 | tf_op jit(solution)/shard_map/ppermute | solution.py:201
  89.9 0.7 collective-permute-done.14
  90.6 3.2 %collective-permute-start.15 = (f32[128,128]{1,0:T(8,128)S(1)}, f32[128,128]{1,0:T(8,128)S(1)}, u32[]{:S(2)}, u32[]{:S(2)}) collective-permute-start(f32[128,128]{1,0:T(8,128)S(1)} %add_add_fusion.refs_0_.refs_4_), channel_id=1, source_target_pairs={{0,64},{16,80},{32,96},{48,112},{64,128},{80,144},{96,160},{112,17... | collective-permute-start | bytes 196616 | tf_op jit(solution)/shard_map/ppermute | solution.py:205
  93.9 5.3 %collective-permute-start.16 = (f32[128,128]{1,0:T(8,128)S(1)}, f32[128,128]{1,0:T(8,128)S(1)}, u32[]{:S(2)}, u32[]{:S(2)}) collective-permute-start(f32[128,128]{1,0:T(8,128)S(1)} %add_add_fusion.refs_0_.refs_4_), channel_id=1, source_target_pairs={{0,128},{16,144},{32,160},{48,176},{64,192},{80,208},{96,224},{112... | collective-permute-start | bytes 196616 | tf_op jit(solution)/shard_map/ppermute | solution.py:205
  99.2 2.7 %collective-permute-start.17 = (f32[128,128]{1,0:T(8,128)S(1)}, f32[128,128]{1,0:T(8,128)S(1)}, u32[]{:S(2)}, u32[]{:S(2)}) collective-permute-start(f32[128,128]{1,0:T(8,128)S(1)} %add_add_fusion.refs_0_.refs_4_), channel_id=1, source_target_pairs={{0,192},{16,208},{32,224},{48,240},{64,0},{80,16},{96,32},{112,48}... | collective-permute-start | bytes 196616 | tf_op jit(solution)/shard_map/ppermute | solution.py:205
  101.9 0.0 collective-permute-done.15.refs_1_.refs_5_
  101.9 0.4 collective-permute-done.16.refs_2_.refs_6_
  102.2 2.6 %collective-permute-done.17.refs_3_.refs_7_ = f32[128,128]{1,0:T(8,128)S(1)} collective-permute-done((f32[128,128]{1,0:T(8,128)S(1)}, f32[128,128]{1,0:T(8,128)S(1)}, u32[]{:S(2)}, u32[]{:S(2)}) %collective-permute-start.17) | collective-permute-done | bytes 65568 | tf_op jit(solution)/shard_map/ppermute | solution.py:205
  104.8 7.0 %decode.1 = f32[512,512]{1,0:T(8,128)} custom-call(s32[4]{0:T(128)S(1)} %pad_add_fusion.at_ref, f32[128,128]{1,0:T(8,128)S(1)} %add_add_fusion.refs_0_.refs_4_, f32[128,128]{1,0:T(8,128)S(1)} %collective-permute-done.15.refs_1_.refs_5_, f32[128,128]{1,0:T(8,128)S(1)} %collective-permute-done.16.refs_2_.refs_6_, ...), custom_call_target="tpu_custom_call" | custom-call | tf_op jit(solution)/shard_map/decode/pallas_call | solution.py:240
  (18 shorter events, 0.1 us)
Async XLA Ops:
  0.8 3.4 %copy-start.2 = (bf16[1,512,8192]{2,1,0:T(8,128)(2,1)S(1)}, bf16[1,512,8192]{2,1,0:T(8,128)(2,1)}, u32[]{:S(2)}) copy-start(bf16[1,512,8192]{2,1,0:T(8,128)(2,1)} %refs_1_.1) | copy-start | bytes 25165828
  5.5 4.2 %collective-permute-start.1 = (bf16[8,256,512]{2,1,0:T(8,128)(2,1)S(1)}, bf16[8,256,512]{2,1,0:T(8,128)(2,1)S(1)}, u32[]{:S(2)}, u32[]{:S(2)}) collective-permute-start(bf16[8,256,512]{2,1,0:T(8,128)(2,1)S(1)} %pack.2.refs_2_), channel_id=1, source_target_pairs={{0,1},{1,0},{2,3},{3,2},{4,5},{5,4},{6,7},{7,6},{8,9},{9,8},{10,11... | collective-permute-start | bytes 6291464 | tf_op jit(solution)/shard_map/ppermute | solution.py:218
  7.7 41.1 %copy-start = (bf16[8,512,512]{2,1,0:T(8,128)(2,1)}, bf16[8,512,512]{2,1,0:T(8,128)(2,1)S(1)}, u32[]{:S(2)}) copy-start(bf16[8,512,512]{2,1,0:T(8,128)(2,1)S(1)} %get-tuple-element.20.refs_0_.refs_1_.refs_3_.refs_2_) | copy-start | bytes 12582916
  7.7 6.1 %collective-permute-start = (bf16[8,256,512]{2,1,0:T(8,128)(2,1)S(1)}, bf16[8,256,512]{2,1,0:T(8,128)(2,1)S(1)}, u32[]{:S(2)}, u32[]{:S(2)}) collective-permute-start(bf16[8,256,512]{2,1,0:T(8,128)(2,1)S(1)} %get-tuple-element.21), channel_id=1, source_target_pairs={{0,1},{1,0},{2,3},{3,2},{4,5},{5,4},{6,7},{7,6},{8,9},{9,8},{10,11... | collective-permute-start | bytes 6291464 | tf_op jit(solution)/shard_map/ppermute | solution.py:218
  10.5 10.1 %collective-permute-start.4 = (s16[272,512]{1,0:T(8,128)(2,1)S(1)}, s16[272,512]{1,0:T(8,128)(2,1)S(1)}, u32[]{:S(2)}, u32[]{:S(2)}) collective-permute-start(s16[272,512]{1,0:T(8,128)(2,1)S(1)} %get-tuple-element.25), channel_id=1, source_target_pairs={{0,4},{1,5},{2,6},{3,7},{4,8},{5,9},{6,10},{7,11},{8,12},{9,13},{1... | collective-permute-start | bytes 835592 | tf_op jit(solution)/shard_map/ppermute | solution.py:218
  12.2 8.4 %collective-permute-start.5 = (s16[272,512]{1,0:T(8,128)(2,1)S(1)}, s16[272,512]{1,0:T(8,128)(2,1)S(1)}, u32[]{:S(2)}, u32[]{:S(2)}) collective-permute-start(s16[272,512]{1,0:T(8,128)(2,1)S(1)} %get-tuple-element.22.refs_3_), channel_id=1, source_target_pairs={{0,12},{1,13},{2,14},{3,15},{4,0},{5,1},{6,2},{7,3},{8,4},{9,5},{1... | collective-permute-start | bytes 835592 | tf_op jit(solution)/shard_map/ppermute | solution.py:218
  20.6 7.7 %copy-start.10 = (s32[1,8,8,32]{3,2,1,0:T(8,128)S(1)}, s32[1,8,8,32]{3,2,1,0:T(8,128)}, u32[]{:S(2)}) copy-start(s32[1,8,8,32]{3,2,1,0:T(8,128)} %param.6) | copy-start | bytes 24580
  21.8 27.0 %collective-permute-start.8 = (s16[2,272,512]{2,1,0:T(8,128)(2,1)S(1)}, s16[2,272,512]{2,1,0:T(8,128)(2,1)S(1)}, u32[]{:S(2)}, u32[]{:S(2)}) collective-permute-start(s16[2,272,512]{2,1,0:T(8,128)(2,1)S(1)} %get-tuple-element.29), channel_id=1, source_target_pairs={{0,4},{1,5},{2,6},{3,7},{4,8},{5,9},{6,10},{7,11},{8,12},{9,13},{1... | collective-permute-start | bytes 1671176 | tf_op jit(solution)/shard_map/ppermute | solution.py:218
  23.4 25.4 %collective-permute-start.9 = (s16[2,272,512]{2,1,0:T(8,128)(2,1)S(1)}, s16[2,272,512]{2,1,0:T(8,128)(2,1)S(1)}, u32[]{:S(2)}, u32[]{:S(2)}) collective-permute-start(s16[2,272,512]{2,1,0:T(8,128)(2,1)S(1)} %get-tuple-element.26.refs_8_), channel_id=1, source_target_pairs={{0,12},{1,13},{2,14},{3,15},{4,0},{5,1},{6,2},{7,3},{8,4},{9,5},{1... | collective-permute-start | bytes 1671176 | tf_op jit(solution)/shard_map/ppermute | solution.py:218
  25.1 17.8 %collective-permute-start.2 = (s16[272,512]{1,0:T(8,128)(2,1)S(1)}, s16[272,512]{1,0:T(8,128)(2,1)S(1)}, u32[]{:S(2)}, u32[]{:S(2)}) collective-permute-start(s16[272,512]{1,0:T(8,128)(2,1)S(1)} %get-tuple-element.23), channel_id=1, source_target_pairs={{0,4},{1,5},{2,6},{3,7},{4,8},{5,9},{6,10},{7,11},{8,12},{9,13},{1... | collective-permute-start | bytes 835592 | tf_op jit(solution)/shard_map/ppermute | solution.py:218
  25.5 17.5 %collective-permute-start.3 = (s16[272,512]{1,0:T(8,128)(2,1)S(1)}, s16[272,512]{1,0:T(8,128)(2,1)S(1)}, u32[]{:S(2)}, u32[]{:S(2)}) collective-permute-start(s16[272,512]{1,0:T(8,128)(2,1)S(1)} %get-tuple-element.24.refs_8_), channel_id=1, source_target_pairs={{0,12},{1,13},{2,14},{3,15},{4,0},{5,1},{6,2},{7,3},{8,4},{9,5},{1... | collective-permute-start | bytes 835592 | tf_op jit(solution)/shard_map/ppermute | solution.py:218
  44.9 19.4 %collective-permute-start.6 = (s16[2,272,512]{2,1,0:T(8,128)(2,1)}, s16[2,272,512]{2,1,0:T(8,128)(2,1)S(1)}, u32[]{:S(2)}, u32[]{:S(2)}) collective-permute-start(s16[2,272,512]{2,1,0:T(8,128)(2,1)} %get-tuple-element.27), channel_id=1, source_target_pairs={{0,4},{1,5},{2,6},{3,7},{4,8},{5,9},{6,10},{7,11},{8,12},{9,13},{1... | collective-permute-start | bytes 1671176 | tf_op jit(solution)/shard_map/ppermute | solution.py:218
  46.0 18.4 %collective-permute-start.7 = (s16[2,272,512]{2,1,0:T(8,128)(2,1)}, s16[2,272,512]{2,1,0:T(8,128)(2,1)}, u32[]{:S(2)}, u32[]{:S(2)}) collective-permute-start(s16[2,272,512]{2,1,0:T(8,128)(2,1)} %get-tuple-element.28.refs_5_), channel_id=1, source_target_pairs={{0,12},{1,13},{2,14},{3,15},{4,0},{5,1},{6,2},{7,3},{8,4},{9,5},{1... | collective-permute-start | bytes 1671176 | tf_op jit(solution)/shard_map/ppermute | solution.py:218
  48.8 8.7 %copy-start.3 = (bf16[2,2,256,256]{3,2,1,0:T(8,128)(2,1)S(1)}, bf16[2,2,256,256]{3,2,1,0:T(8,128)(2,1)}, u32[]{:S(2)}) copy-start(bf16[2,2,256,256]{3,2,1,0:T(8,128)(2,1)} %constant.74.clone.refs_4_.refs_8_) | copy-start | bytes 1572868
  50.0 0.8 copy-start.8
  50.8 6.7 %collective-permute-start.10 = (s16[272,512]{1,0:T(8,128)(2,1)S(1)}, s16[272,512]{1,0:T(8,128)(2,1)}, u32[]{:S(2)}, u32[]{:S(2)}) collective-permute-start(s16[272,512]{1,0:T(8,128)(2,1)S(1)} %get-tuple-element.31.refs_6_), channel_id=1, source_target_pairs={{0,2},{1,3},{2,0},{3,1},{4,6},{5,7},{6,4},{7,5},{8,10},{9,11},{10,... | collective-permute-start | bytes 835592 | tf_op jit(solution)/shard_map/ppermute | solution.py:218
  57.5 1.2 %copy-start.4 = (f32[512,512]{1,0:T(8,128)S(1)}, f32[512,512]{1,0:T(8,128)}, u32[]{:S(2)}) copy-start(f32[512,512]{1,0:T(8,128)} %refs_2_.3) | copy-start | bytes 3145732
  58.7 1.0 copy-start.9
  64.4 2.2 %copy-start.1 = (bf16[8,512,512]{2,1,0:T(8,128)(2,1)S(1)}, bf16[8,512,512]{2,1,0:T(8,128)(2,1)}, u32[]{:S(2)}) copy-start(bf16[8,512,512]{2,1,0:T(8,128)(2,1)} %copy-done) | copy-start | bytes 12582916
  66.6 4.9 %copy-start.11 = (s32[1,4,8,32]{3,2,1,0:T(8,128)S(1)}, s32[1,4,8,32]{3,2,1,0:T(8,128)}, u32[]{:S(2)}) copy-start(s32[1,4,8,32]{3,2,1,0:T(8,128)} %get-tuple-element.38) | copy-start | bytes 12292
  68.8 0.8 copy-start.6
  69.6 6.5 %collective-permute-start.11 = (s16[272,512]{1,0:T(8,128)(2,1)S(1)}, s16[272,512]{1,0:T(8,128)(2,1)S(1)}, u32[]{:S(2)}, u32[]{:S(2)}) collective-permute-start(s16[272,512]{1,0:T(8,128)(2,1)S(1)} %get-tuple-element.34.refs_7_), channel_id=1, source_target_pairs={{0,2},{1,3},{2,0},{3,1},{4,6},{5,7},{6,4},{7,5},{8,10},{9,11},{10,... | collective-permute-start | bytes 835592 | tf_op jit(solution)/shard_map/ppermute | solution.py:218
  76.2 1.2 %copy-start.5 = (f32[512,512]{1,0:T(8,128)S(1)}, f32[512,512]{1,0:T(8,128)}, u32[]{:S(2)}) copy-start(f32[512,512]{1,0:T(8,128)} %refs_2_.3) | copy-start | bytes 3145732
  77.4 1.0 copy-start.7
  82.1 4.5 %collective-permute-start.12 = (f32[128,128]{1,0:T(8,128)S(1)}, f32[128,128]{1,0:T(8,128)S(1)}, u32[]{:S(2)}, u32[]{:S(2)}) collective-permute-start(f32[128,128]{1,0:T(8,128)S(1)} %get-tuple-element.37.refs_9_), channel_id=1, source_target_pairs={{0,16},{16,32},{32,48},{48,0},{64,80},{80,96},{96,112},{112,64},{1... | collective-permute-start | bytes 196616 | tf_op jit(solution)/shard_map/ppermute | solution.py:201
  84.1 5.8 %collective-permute-start.13 = (f32[128,128]{1,0:T(8,128)S(1)}, f32[128,128]{1,0:T(8,128)S(1)}, u32[]{:S(2)}, u32[]{:S(2)}) collective-permute-start(f32[128,128]{1,0:T(8,128)S(1)} %get-tuple-element.37.refs_9_), channel_id=1, source_target_pairs={{0,32},{16,48},{32,0},{48,16},{64,96},{80,112},{96,64},{112,80},{1... | collective-permute-start | bytes 196616 | tf_op jit(solution)/shard_map/ppermute | solution.py:201
  85.0 5.6 %collective-permute-start.14 = (f32[128,128]{1,0:T(8,128)S(1)}, f32[128,128]{1,0:T(8,128)S(1)}, u32[]{:S(2)}, u32[]{:S(2)}) collective-permute-start(f32[128,128]{1,0:T(8,128)S(1)} %get-tuple-element.37.refs_9_), channel_id=1, source_target_pairs={{0,48},{16,0},{32,16},{48,32},{64,112},{80,64},{96,80},{112,96},{1... | collective-permute-start | bytes 196616 | tf_op jit(solution)/shard_map/ppermute | solution.py:201
  90.6 11.2 %collective-permute-start.15 = (f32[128,128]{1,0:T(8,128)S(1)}, f32[128,128]{1,0:T(8,128)S(1)}, u32[]{:S(2)}, u32[]{:S(2)}) collective-permute-start(f32[128,128]{1,0:T(8,128)S(1)} %add_add_fusion.refs_0_.refs_4_), channel_id=1, source_target_pairs={{0,64},{16,80},{32,96},{48,112},{64,128},{80,144},{96,160},{112,17... | collective-permute-start | bytes 196616 | tf_op jit(solution)/shard_map/ppermute | solution.py:205
  93.9 8.4 %collective-permute-start.16 = (f32[128,128]{1,0:T(8,128)S(1)}, f32[128,128]{1,0:T(8,128)S(1)}, u32[]{:S(2)}, u32[]{:S(2)}) collective-permute-start(f32[128,128]{1,0:T(8,128)S(1)} %add_add_fusion.refs_0_.refs_4_), channel_id=1, source_target_pairs={{0,128},{16,144},{32,160},{48,176},{64,192},{80,208},{96,224},{112... | collective-permute-start | bytes 196616 | tf_op jit(solution)/shard_map/ppermute | solution.py:205
  99.2 5.7 %collective-permute-start.17 = (f32[128,128]{1,0:T(8,128)S(1)}, f32[128,128]{1,0:T(8,128)S(1)}, u32[]{:S(2)}, u32[]{:S(2)}) collective-permute-start(f32[128,128]{1,0:T(8,128)S(1)} %add_add_fusion.refs_0_.refs_4_), channel_id=1, source_target_pairs={{0,192},{16,208},{32,224},{48,240},{64,0},{80,16},{96,32},{112,48}... | collective-permute-start | bytes 196616 | tf_op jit(solution)/shard_map/ppermute | solution.py:205

commit v3 on v2

--- a/solution.py
+++ b/solution.py
@@ -136,31 +136,48 @@
     return ref[:rows].astype(jnp.int32).astype(F32) * (scale * (1.0 / (LEVELS * STEPS)))
 
 
+def wide(*refs):
+    return sum(ref[0].astype(F32) for ref in refs)
+
+
 def pack_kernel(at_ref, *refs):
     for i in range(len(refs) // 2):
         refs[len(refs) // 2 + i][...] = refs[i][...]
 
 
-def far_kernel(at_ref, own0, own1, sib_ref, up_ref, down_ref):
-    put(up_ref, own0[0].astype(F32) + sib_ref[0].astype(F32))
-    put(down_ref, own1[0].astype(F32) + sib_ref[1].astype(F32))
-
-
-def near_kernel(at_ref, up0, up1, down0, down1, sib_up, sib_down, far_up, far_down, up_ref, down_ref):
-    put(up_ref.at[0], up0[0].astype(F32) + sib_up[0].astype(F32) + get(far_up))
-    put(up_ref.at[1], up1[0].astype(F32) + sib_up[1].astype(F32))
-    put(down_ref.at[0], down0[0].astype(F32) + sib_down[0].astype(F32))
-    put(down_ref.at[1], down1[0].astype(F32) + sib_down[1].astype(F32) + get(far_down))
-
-
-def cross_kernel(at_ref, own0, own1, sib_ref, up_ref, down_ref, own_ref, out_ref):
-    put(out_ref, own1[0].astype(F32) + sib_ref[1].astype(F32) + (get(up_ref.at[1]) + get(down_ref.at[1])))
-    own_ref[...] = own0[0].astype(F32) + sib_ref[0].astype(F32) + (get(up_ref.at[0]) + get(down_ref.at[0]))
-
-
-def encode_kernel(at_ref, own_ref, cross_ref, momentum_ref, pos_ref, basis_ref, *refs):
+def far_kernel(at_ref, own, sib, up_ref, down_ref):
+    x = wide(own, sib)
+    put(up_ref, x[:HALF])
+    put(down_ref, x[HALF:])
+
+
+def near_kernel(at_ref, own_up, sib_up, own_down, sib_down, far_up, far_down, up_ref, down_ref):
+    up, down = wide(own_up, sib_up), wide(own_down, sib_down)
+    put(up_ref, jnp.concatenate([up[:HALF] + get(far_up), up[HALF:]], axis=0))
+    put(down_ref, jnp.concatenate([down[:HALF], down[HALF:] + get(far_down)], axis=0))
+
+
+def near_top_kernel(at_ref, own_up, sib_up, own_down, sib_down, far_up, momentum, basis, up_ref, down_ref, decayed, held):
+    put(up_ref, wide(own_up, sib_up) + get(far_up))
+    put(down_ref, wide(own_down, sib_down))
+    decayed[...] = DECAY * momentum[...]
+    held[...] = basis[...]
+
+
+def near_low_kernel(at_ref, own_up, sib_up, own_down, sib_down, far_down, up_ref, down_ref):
+    put(up_ref, wide(own_up, sib_up))
+    put(down_ref, wide(own_down, sib_down) + get(far_down))
+
+
+def cross_kernel(at_ref, own, sib, up_ref, down_ref, top_ref, low_ref):
+    x = wide(own, sib) + (get(up_ref) + get(down_ref))
+    put(top_ref, x[:HALF])
+    put(low_ref, x[HALF:])
+
+
+def encode_kernel(at_ref, own, sib, up_ref, down_ref, cross_ref, momentum_ref, pos_ref, basis_ref, *refs):
     *before, fresh_ref, kept_ref = refs
-    field = DECAY * momentum_ref[...] + (own_ref[...] + get(cross_ref))
+    field = momentum_ref[...] + (wide(own, sib) + (get(up_ref) + get(down_ref)) + get(cross_ref))
     first = 0
     for ref in before:
         kept_ref[first:first + ref.shape[0]] = ref[...]
@@ -223,14 +240,15 @@
 
 
 class Program:
+
     def __init__(self, at):
         self.at = at
-        self.last = None
+        self.last = []
 
     def call(self, body, name, ins, outs, grid=(1,), onto=None):
         operands, specs = map(list, zip(*ins))
         count = len(operands)
-        extra = [x for x in (onto, self.last) if x is not None]
+        extra = ([] if onto is None else [onto]) + self.last
         operands += extra
         specs += [pl.BlockSpec(memory_space=pl.ANY)] * len(extra)
 
@@ -250,7 +268,7 @@
             compiler_params=pltpu.CompilerParams(vmem_limit_bytes=VMEM),
             name=name,
         )(self.at, *operands)
-        self.last = results[-1]
+        self.last = [results[-1]]
         return results
 
 
@@ -258,81 +276,8 @@
     return x, pl.BlockSpec(x.shape, lambda s, at: (0,) * x.ndim)
 
 
-class Chunk:
-    def __init__(self, program, slab, start, rows, cols):
-        self.program, self.call = program, program.call
-        self.slab, self.rows, self.cols = slab, rows, cols
-        self.start, self.index = start, start // rows
-
-    def own(self, dy, dz):
-        i, k = self.index, dy * 2 + dz
-        return self.program.own, pl.BlockSpec((1, self.rows, self.cols), lambda s, at: (k, i, 0))
-
-    def part(self, x, first, count):
-        return x, pl.BlockSpec((count, *x.shape[1:]), lambda s, at: (first // count, 0, 0))
-
-    def out(self, kind, *lead):
-        shape = (*lead, self.rows + (0 if kind == F32 else PAD), self.cols)
-        return jax.ShapeDtypeStruct(shape, kind), pl.BlockSpec(shape, lambda s, at: (0,) * len(shape))
-
-    def pack(self, own_too):
-        i, rows, cols, height = self.index, self.rows, self.cols, self.slab.shape[1]
-        slab_spec = pl.BlockSpec((1, rows, cols), lambda s, at: (0, i, piece(at, s // 2, s % 2, 1)))
-        out_spec = pl.BlockSpec((1, rows, cols), lambda s, at: (s, 0, 0))
-        ins = [(self.slab, slab_spec)]
-        outs = [(jax.ShapeDtypeStruct((8, rows, cols), BF), out_spec)]
-        if own_too:
-            ins.append((self.slab, pl.BlockSpec((1, height, cols), lambda s, at: (0, 0, piece(at, s // 2, s % 2)))))
-            outs.append((jax.ShapeDtypeStruct((8, height, cols), BF),
-                         pl.BlockSpec((1, height, cols), lambda s, at: (s, 0, 0))))
-        packed, *own = self.call(pack_kernel, "pack", ins, outs, (8,))
-        if own_too:
-            self.program.own = own[0]
-        self.sib = send(packed, flip_core=1)
-
-    def far(self):
-        up, down = self.call(
-            far_kernel, "far", [self.own(2, 0), self.own(2, 1), self.part(self.sib, 4, 2)],
-            [self.out(KINDS[0]), self.out(KINDS[0])],
-        )
-        self.far_up, self.far_down = send(up, shift_y=1), send(down, shift_y=-1)
-
-    def near(self):
-        up, down = self.call(
-            near_kernel, "near",
-            [self.own(1, 0), self.own(1, 1), self.own(3, 0), self.own(3, 1), self.part(self.sib, 2, 2),
-             self.part(self.sib, 6, 2), whole(self.far_up), whole(self.far_down)],
-            [self.out(KINDS[1], 2), self.out(KINDS[1], 2)],
-        )
-        self.up, self.down = send(up, shift_y=1), send(down, shift_y=-1)
-
-    def cross(self):
-        self.mine, cross = self.call(
-            cross_kernel, "cross",
-            [self.own(0, 0), self.own(0, 1), self.part(self.sib, 0, 2), whole(self.up), whole(self.down)],
-            [self.out(F32), self.out(KINDS[2])],
-        )
-        self.crossed = send(cross, flip_z=1)
-
-    def encode(self, momentum, pos, basis, onto, before):
-        rows, cols, i = self.rows, self.cols, self.index
-        groups = rows // GROUP * (cols // WIDE)
-        first = self.start // GROUP * (cols // WIDE)
-        pos = pos[first:first + groups]
-        height = rows // GROUP * (cols // GROUP) + sum(x.shape[0] for x in before)
-        self.fresh, self.kept = self.call(
-            encode_kernel, "encode",
-            [whole(self.mine), whole(self.crossed), (momentum, pl.BlockSpec((rows, cols), lambda s, at: (i, 0))),
-             whole(pos), whole(basis), *map(whole, before)],
-            [(jax.ShapeDtypeStruct(momentum.shape, F32), pl.BlockSpec((rows, cols), lambda s, at: (i, 0))),
-             (jax.ShapeDtypeStruct((height, KEPT), F32), pl.BlockSpec((height, KEPT), lambda s, at: (0, 0)))],
-            onto=onto,
-        )
-
-
-CHUNKS = (256, 256)
-PLAN = "P0 P1 F0 F1 N0 N1 X0 E0 X1 E1 G0,1 D0,1"
-KINDS = (jnp.int16,) * 3
+HALF = 256
+SENT = jnp.int16
 VMEM = 16 * 1024 * 1024
 
 
@@ -347,39 +292,78 @@
     at = jnp.stack([me // 4, me // 2 % 2, me % 2, rep % 4]).astype(jnp.int32)
     lines = jnp.tile(freq_index.reshape(rows // GROUP * (cols // GROUP), K).astype(F32), (1, KEPT // K))
     lines = jnp.where(jnp.arange(KEPT)[None] // K == rep % 4, lines, F32(0.0))
+    groups = HALF // GROUP * (cols // WIDE)
+    poss = [pos[i * groups:(i + 1) * groups] for i in range(rows // HALF)]
     program = Program(at)
-    starts = np.cumsum((0,) + CHUNKS)[:-1]
-    work = [Chunk(program, partial_grads, int(s), r, cols) for s, r in zip(starts, CHUNKS)]
-    per_step = STEP // GROUP * (cols // GROUP)
-    fresh = update = None
-    before = [lines]
-    for step in PLAN.split():
-        kind, which = step[0], [work[int(i)] for i in step[1:].split(",")]
-        chunk = which[0]
-        if kind == "P":
-            chunk.pack(chunk is work[-1])
-        elif kind == "F":
-            chunk.far()
-        elif kind == "N":
-            chunk.near()
-        elif kind == "X":
-            chunk.cross()
-        elif kind == "E":
-            chunk.encode(momentum, pos, basis, fresh, before)
-            fresh, before = chunk.fresh, [chunk.kept]
-        elif kind == "G":
-            sent = along_z(sum(along_x(before[0])))
-        else:
-            first, steps = chunk.start // STEP, rows // STEP
-            val_spec = pl.BlockSpec((per_step, KEPT), lambda s, at: (steps + first + s, 0))
-            pos_spec = pl.BlockSpec((per_step, KEPT), lambda s, at: (first + s, 0))
-            update, = program.call(
-                decode_kernel, "decode",
-                [(x, val_spec) for x in sent] + [(x, pos_spec) for x in sent] + [whole(basis)],
-                [(jax.ShapeDtypeStruct((rows, cols), F32), pl.BlockSpec((STEP, cols), lambda s, at: (first + s, 0)))],
-                (sum(c.rows for c in which) // STEP,),
-                onto=update,
-            )
+    call = program.call
+    quarter = jax.ShapeDtypeStruct((4, rows, cols), BF)
+
+    def slab(dz, flip_core):
+        return partial_grads, pl.BlockSpec((1, rows, cols), lambda s, at: (0, 0, piece(at, s, dz, flip_core)))
+
+    def packed():
+        return quarter, pl.BlockSpec((1, rows, cols), lambda s, at: (s, 0, 0))
+
+    def out(height):
+        shape = (height + (0 if SENT == F32 else PAD), cols)
+        return jax.ShapeDtypeStruct(shape, SENT), pl.BlockSpec(shape, lambda s, at: (0, 0))
+
+    def like(x):
+        return jax.ShapeDtypeStruct(x.shape, x.dtype), whole(x)[1]
+
+    own, sib = {}, {}
+    other, = call(pack_kernel, "pack", [slab(1, 1)], [packed()], (4,))
+    sib[1] = send(other, flip_core=1)
+    other, own[1], own[0] = call(
+        pack_kernel, "pack", [slab(0, 1), slab(1, 0), slab(0, 0)], [packed(), packed(), packed()], (4,))
+    sib[0] = send(other, flip_core=1)
+
+    def both(dz, dy, height=rows, i=0):
+        spec = pl.BlockSpec((1, height, cols), lambda s, at: (dy % 4, i, 0))
+        return [(own[dz], spec), (sib[dz], spec)]
+
+    def round_y(x):
+        return send(x[0], shift_y=1), send(x[1], shift_y=-1)
+
+    far = {}
+    for dz in (1, 0):
+        far[dz] = round_y(call(far_kernel, "far", both(dz, 2), [out(HALF)] * 2))
+        if dz:
+            program.last += [lines, *poss]
+    across_near = round_y(call(
+        near_kernel, "near", both(1, 1) + both(1, -1) + [whole(far[1][0]), whole(far[1][1])], [out(rows)] * 2))
+    *top, decayed, held = call(
+        near_top_kernel, "near",
+        both(0, 1, HALF, 0) + both(0, -1, HALF, 0) + [whole(far[0][0]), whole(momentum), whole(basis)],
+        [out(HALF)] * 2 + [like(momentum), like(basis)])
+    near = [round_y(top)]
+    crossing = call(
+        cross_kernel, "cross", both(1, 0) + [whole(across_near[0]), whole(across_near[1])], [out(HALF)] * 2)
+    crossed = [send(x, flip_z=1) for x in crossing]
+    near.append(round_y(call(
+        near_low_kernel, "near", both(0, 1, HALF, 1) + both(0, -1, HALF, 1) + [whole(far[0][1])], [out(HALF)] * 2)))
+    fresh, kept = None, lines
+    for i in range(rows // HALF):
+        height = kept.shape[0] + HALF // GROUP * (cols // GROUP)
+        half_spec = pl.BlockSpec((HALF, cols), lambda s, at, i=i: (i, 0))
+        fresh, kept = call(
+            encode_kernel, "encode",
+            [*both(0, 0, HALF, i), whole(near[i][0]), whole(near[i][1]), whole(crossed[i]), (decayed, half_spec),
+             whole(poss[i]), whole(held), whole(kept)],
+            [(jax.ShapeDtypeStruct((rows, cols), F32), half_spec),
+             (jax.ShapeDtypeStruct((height, KEPT), F32), pl.BlockSpec((height, KEPT), lambda s, at: (0, 0)))],
+            onto=fresh,
+        )
+    sent = along_z(sum(along_x(kept)))
+    per_step, steps = STEP // GROUP * (cols // GROUP), rows // STEP
+    val_spec = pl.BlockSpec((per_step, KEPT), lambda s, at: (steps + s, 0))
+    pos_spec = pl.BlockSpec((per_step, KEPT), lambda s, at: (s, 0))
+    update, = call(
+        decode_kernel, "decode",
+        [(x, val_spec) for x in sent] + [(x, pos_spec) for x in sent] + [whole(held)],
+        [(jax.ShapeDtypeStruct((rows, cols), F32), pl.BlockSpec((STEP, cols), lambda s, at: (s, 0)))],
+        (steps,),
+    )
     return fresh, update
 
 

time: 112 us -> 92.1 us (0.82)
  waiting for transfers between devices: 37.7 us -> 23 us
  local copies, waits for them, and re-layouts: 13.9 us -> 4.31 us
  Pallas kernels: 26.9 us -> 29.7 us
  starting transfers between devices: 31.7 us -> 33.9 us
    ppermute x12 -> x14, waiting for transfers between devices: 29.1 us -> 14.5 us  [send(): return lax.ppermute(x, 'fsdp', places(shift_y, flip_z, flip_core))]
    unnamed x24 -> x16, local copies, waits for them, and re-layouts: 11.7 us -> 4.01 us
    pallas_call x11, Pallas kernels: 26.9 us -> 29.7 us  [call(): pl.pallas_call(kernel, grid_spec=pltpu.PrefetchScalarGridSpec(num_scalar_...]
    ppermute x12 -> x14, starting transfers between devices: 17.5 us -> 19.7 us  [send(): return lax.ppermute(x, 'fsdp', places(shift_y, flip_z, flip_core))]
    slice x3, local copies, waits for them, and re-layouts: 1.46 us -> 0.16 us  [local(): poss = [pos[i * groups:(i + 1) * groups] for i in range(rows // HALF)]]
  transfers between devices with their start and end apart: 18 -> 20, of which waited for: 10 -> 10; matrix products, arithmetic and copies ran while one was open for 3% -> 0% of each run, Pallas kernels for 10% -> 18%
where the time goes in v3:
time: 92.1 us; the launch traced here: 91.8 us
  starting transfers between devices  33.9 us (37%)
  Pallas kernels  29.7 us (32%)
  waiting for transfers between devices  23 us (25%)
  local copies, waits for them, and re-layouts  4.31 us (5%)
    pallas_call x11, Pallas kernels, call(): pl.pallas_call(kernel, grid_spec=pltpu.PrefetchScalarGridSpec(num_scalar_...  29.7 us
    ppermute x14, starting transfers between devices, send(): return lax.ppermute(x, 'fsdp', places(shift_y, flip_z, flip_core))  19.7 us
    ppermute x14, waiting for transfers between devices, send(): return lax.ppermute(x, 'fsdp', places(shift_y, flip_z, flip_core))  14.5 us
    ppermute x3, starting transfers between devices, along_z(): lax.ppermute(near, 'rep', across(4, 4, s, 0))  11.2 us
    ppermute x3, waiting for transfers between devices, along_x(): lax.ppermute(own, 'rep', across(4, 4, 0, s))  5.53 us
    unnamed x16, local copies, waits for them, and re-layouts  4.01 us
    ppermute x3, waiting for transfers between devices, along_z(): lax.ppermute(near, 'rep', across(4, 4, s, 0))  2.99 us
    ppermute x3, starting transfers between devices, along_x(): lax.ppermute(own, 'rep', across(4, 4, 0, s))  2.91 us
  transfers between devices with their start and end apart: 20, of which 10 were waited for; matrix products, arithmetic and copies ran while one was open for 0% of the time, Pallas kernels for 18%

profile of v3, /device:TPU:6, one launch (start us, length us, event | category | flops | bytes accessed | tf_op | source)
XLA Modules:
  0.0 91.8 jit_solution(5334904983713785707)
XLA Ops:
  0.7 0.1 pad_add_fusion.at_ref
  0.8 3.4 %copy-done = bf16[1,512,8192]{2,1,0:T(8,128)(2,1)S(1)} copy-done((bf16[1,512,8192]{2,1,0:T(8,128)(2,1)S(1)}, bf16[1,512,8192]{2,1,0:T(8,128)(2,1)}, u32[]{:S(2)}) %copy-start) | copy-done | bytes 8388632
  4.1 1.1 %pack.2.refs_3_ = bf16[4,512,512]{2,1,0:T(8,128)(2,1)S(1)} custom-call(s32[4]{0:T(128)S(1)} %pad_add_fusion.at_ref, bf16[1,512,8192]{2,1,0:T(8,128)(2,1)S(1)} %copy-done), custom_call_target="tpu_custom_call" | custom-call | tf_op jit(solution)/shard_map/pack/pallas_call | solution.py:258
  5.2 0.0 copy-start.7
  5.2 0.1 collective-permute-start.1
  5.3 3.1 %pack.3 = (bf16[4,512,512]{2,1,0:T(8,128)(2,1)}, bf16[4,512,512]{2,1,0:T(8,128)(2,1)S(1)}, bf16[4,512,512]{2,1,0:T(8,128)(2,1)S(1)}) custom-call(s32[4]{0:T(128)S(1)} %pad_add_fusion.at_ref, bf16[1,512,8192]{2,1,0:T(8,128)(2,1)S(1)} %copy-done, bf16[1,512,8192]{2,1,0:T(8,128)(2,1)S(1)} %copy-done, bf16[1,512,8192]{2,1,0:T(8,128)(2,1)S(1)} %copy-done, ...), custom_call_target="tpu_custom_call" | custom-call | tf_op jit(solution)/shard_map/pack/pallas_call | solution.py:258
  8.4 0.5 collective-permute-start
  8.9 0.5 collective-permute-done.1.refs_1_.refs_3_
  9.5 0.8 far.2
  10.3 0.0 copy-done.3
  10.3 0.6 copy-done.1
  10.9 1.6 %collective-permute-start.3 = (s16[272,512]{1,0:T(8,128)(2,1)S(1)}, s16[272,512]{1,0:T(8,128)(2,1)S(1)}, u32[]{:S(2)}, u32[]{:S(2)}) collective-permute-start(s16[272,512]{1,0:T(8,128)(2,1)S(1)} %get-tuple-element.28), channel_id=1, source_target_pairs={{0,4},{1,5},{2,6},{3,7},{4,8},{5,9},{6,10},{7,11},{8,12},{9,13},{1... | collective-permute-start | bytes 835592 | tf_op jit(solution)/shard_map/ppermute | solution.py:235
  12.4 1.7 %collective-permute-start.4 = (s16[272,512]{1,0:T(8,128)(2,1)S(1)}, s16[272,512]{1,0:T(8,128)(2,1)S(1)}, u32[]{:S(2)}, u32[]{:S(2)}) collective-permute-start(s16[272,512]{1,0:T(8,128)(2,1)S(1)} %get-tuple-element.26.refs_2_), channel_id=1, source_target_pairs={{0,12},{1,13},{2,14},{3,15},{4,0},{5,1},{6,2},{7,3},{8,4},{9,5},{1... | collective-permute-start | bytes 835592 | tf_op jit(solution)/shard_map/ppermute | solution.py:235
  14.1 0.1 copy.7
  14.2 0.1 copy.8
  14.2 0.1 slice.13.refs_4_.refs_6_
  14.3 0.1 slice.15.refs_5_.refs_6_
  14.4 0.0 copy-start.2
  14.4 0.0 copy-start.4
  14.4 0.0 collective-permute-done.refs_1_.refs_3_
  14.4 2.1 %far.3 = (s16[272,512]{1,0:T(8,128)(2,1)S(1)}, s16[272,512]{1,0:T(8,128)(2,1)S(1)}) custom-call(s32[4]{0:T(128)S(1)} %pad_add_fusion.at_ref, bf16[4,512,512]{2,1,0:T(8,128)(2,1)S(1)} %get-tuple-element.23.refs_2_.refs_0_, bf16[4,512,512]{2,1,0:T(8,128)(2,1)} %collective-permute-done.refs_1_.refs_3_, s16[272,512]{1,0:T(8,128)(2,1)S(1)} %get-tuple-element.26.refs_2_, ...), custom_call_target="tpu_custom_call" | custom-call | tf_op jit(solution)/shard_map/far/pallas_call | solution.py:258
  16.6 0.4 collective-permute-start.7
  17.0 4.6 %collective-permute-done.3.refs_4_ = s16[272,512]{1,0:T(8,128)(2,1)S(1)} collective-permute-done((s16[272,512]{1,0:T(8,128)(2,1)S(1)}, s16[272,512]{1,0:T(8,128)(2,1)S(1)}, u32[]{:S(2)}, u32[]{:S(2)}) %collective-permute-start.3) | collective-permute-done | bytes 278560 | tf_op jit(solution)/shard_map/ppermute | solution.py:235
  21.6 0.0 collective-permute-done.4.refs_5_
  21.6 0.0 copy-start.5
  21.6 0.0 copy-start.6
  21.6 1.2 %near.3 = (s16[528,512]{1,0:T(8,128)(2,1)S(1)}, s16[528,512]{1,0:T(8,128)(2,1)S(1)}) custom-call(s32[4]{0:T(128)S(1)} %pad_add_fusion.at_ref, bf16[4,512,512]{2,1,0:T(8,128)(2,1)S(1)} %copy-done.4, bf16[4,512,512]{2,1,0:T(8,128)(2,1)S(1)} %copy-done.2, bf16[4,512,512]{2,1,0:T(8,128)(2,1)S(1)} %copy-done.4, bf16[4,512,512]{2,1,0:T(8,128)(2,1)S(1)} %copy-done.2, ...), custom_call_target="tpu_custom_call" | custom-call | tf_op jit(solution)/shard_map/near/pallas_call | solution.py:258
  22.8 0.9 %collective-permute-start.5 = (s16[528,512]{1,0:T(8,128)(2,1)S(1)}, s16[528,512]{1,0:T(8,128)(2,1)S(1)}, u32[]{:S(2)}, u32[]{:S(2)}) collective-permute-start(s16[528,512]{1,0:T(8,128)(2,1)S(1)} %get-tuple-element.29), channel_id=1, source_target_pairs={{0,4},{1,5},{2,6},{3,7},{4,8},{5,9},{6,10},{7,11},{8,12},{9,13},{1... | collective-permute-start | bytes 1622024 | tf_op jit(solution)/shard_map/ppermute | solution.py:235
  23.7 2.4 %collective-permute-start.6 = (s16[528,512]{1,0:T(8,128)(2,1)S(1)}, s16[528,512]{1,0:T(8,128)(2,1)S(1)}, u32[]{:S(2)}, u32[]{:S(2)}) collective-permute-start(s16[528,512]{1,0:T(8,128)(2,1)S(1)} %get-tuple-element.30.refs_7_), channel_id=1, source_target_pairs={{0,12},{1,13},{2,14},{3,15},{4,0},{5,1},{6,2},{7,3},{8,4},{9,5},{1... | collective-permute-start | bytes 1622024 | tf_op jit(solution)/shard_map/ppermute | solution.py:235
  26.1 1.0 %collective-permute-start.2 = (s16[272,512]{1,0:T(8,128)(2,1)S(1)}, s16[272,512]{1,0:T(8,128)(2,1)S(1)}, u32[]{:S(2)}, u32[]{:S(2)}) collective-permute-start(s16[272,512]{1,0:T(8,128)(2,1)S(1)} %get-tuple-element.27.refs_6_), channel_id=1, source_target_pairs={{0,12},{1,13},{2,14},{3,15},{4,0},{5,1},{6,2},{7,3},{8,4},{9,5},{1... | collective-permute-start | bytes 835592 | tf_op jit(solution)/shard_map/ppermute | solution.py:235
  27.1 0.4 collective-permute-done.7.refs_4_
  27.5 2.0 %near.4 = (s16[272,512]{1,0:T(8,128)(2,1)S(1)}, s16[272,512]{1,0:T(8,128)(2,1)S(1)}, f32[512,512]{1,0:T(8,128)S(1)}, bf16[2,2,256,256]{3,2,1,0:T(8,128)(2,1)S(1)}) custom-call(s32[4]{0:T(128)S(1)} %pad_add_fusion.at_ref, bf16[4,512,512]{2,1,0:T(8,128)(2,1)S(1)} %get-tuple-element.23.refs_2_.refs_0_, ...), custom_call_target="tpu_custom_call" | custom-call | tf_op jit(solution)/shard_map/near/pallas_call | solution.py:258
  29.5 0.7 collective-permute-start.11
  30.2 2.6 %collective-permute-start.12 = (s16[272,512]{1,0:T(8,128)(2,1)S(1)}, s16[272,512]{1,0:T(8,128)(2,1)S(1)}, u32[]{:S(2)}, u32[]{:S(2)}) collective-permute-start(s16[272,512]{1,0:T(8,128)(2,1)S(1)} %get-tuple-element.38), channel_id=1, source_target_pairs={{0,12},{1,13},{2,14},{3,15},{4,0},{5,1},{6,2},{7,3},{8,4},{9,5},{1... | collective-permute-start | bytes 835592 | tf_op jit(solution)/shard_map/ppermute | solution.py:235
  32.9 6.4 %collective-permute-done.5.refs_2_ = s16[528,512]{1,0:T(8,128)(2,1)S(1)} collective-permute-done((s16[528,512]{1,0:T(8,128)(2,1)S(1)}, s16[528,512]{1,0:T(8,128)(2,1)S(1)}, u32[]{:S(2)}, u32[]{:S(2)}) %collective-permute-start.5) | collective-permute-done | bytes 540704 | tf_op jit(solution)/shard_map/ppermute | solution.py:235
  39.3 0.0 collective-permute-done.6.refs_3_
  39.3 1.1 %cross.1 = (s16[272,512]{1,0:T(8,128)(2,1)S(1)}, s16[272,512]{1,0:T(8,128)(2,1)S(1)}) custom-call(s32[4]{0:T(128)S(1)} %pad_add_fusion.at_ref, bf16[4,512,512]{2,1,0:T(8,128)(2,1)S(1)} %copy-done.4, bf16[4,512,512]{2,1,0:T(8,128)(2,1)S(1)} %copy-done.2, s16[528,512]{1,0:T(8,128)(2,1)S(1)} %collective-permute-done.5.refs_2_, ...), custom_call_target="tpu_custom_call" | custom-call | tf_op jit(solution)/shard_map/cross/pallas_call | solution.py:258
  40.4 2.0 %collective-permute-start.13 = (s16[272,512]{1,0:T(8,128)(2,1)S(1)}, s16[272,512]{1,0:T(8,128)(2,1)S(1)}, u32[]{:S(2)}, u32[]{:S(2)}) collective-permute-start(s16[272,512]{1,0:T(8,128)(2,1)S(1)} %get-tuple-element.39), channel_id=1, source_target_pairs={{0,2},{1,3},{2,0},{3,1},{4,6},{5,7},{6,4},{7,5},{8,10},{9,11},{10,... | collective-permute-start | bytes 835592 | tf_op jit(solution)/shard_map/ppermute | solution.py:235
  42.4 2.5 %collective-permute-done.2.refs_4_ = s16[272,512]{1,0:T(8,128)(2,1)S(1)} collective-permute-done((s16[272,512]{1,0:T(8,128)(2,1)S(1)}, s16[272,512]{1,0:T(8,128)(2,1)S(1)}, u32[]{:S(2)}, u32[]{:S(2)}) %collective-permute-start.2) | collective-permute-done | bytes 278560 | tf_op jit(solution)/shard_map/ppermute | solution.py:235
  44.9 1.9 %near.5 = (s16[272,512]{1,0:T(8,128)(2,1)S(1)}, s16[272,512]{1,0:T(8,128)(2,1)S(1)}) custom-call(s32[4]{0:T(128)S(1)} %pad_add_fusion.at_ref, bf16[4,512,512]{2,1,0:T(8,128)(2,1)S(1)} %get-tuple-element.23.refs_2_.refs_0_, bf16[4,512,512]{2,1,0:T(8,128)(2,1)} %collective-permute-done.refs_1_.refs_3_, ...), custom_call_target="tpu_custom_call" | custom-call | tf_op jit(solution)/shard_map/near/pallas_call | solution.py:258
  46.8 1.4 %collective-permute-start.8 = (s16[272,512]{1,0:T(8,128)(2,1)S(1)}, s16[272,512]{1,0:T(8,128)(2,1)S(1)}, u32[]{:S(2)}, u32[]{:S(2)}) collective-permute-start(s16[272,512]{1,0:T(8,128)(2,1)S(1)} %get-tuple-element.34), channel_id=1, source_target_pairs={{0,4},{1,5},{2,6},{3,7},{4,8},{5,9},{6,10},{7,11},{8,12},{9,13},{1... | collective-permute-start | bytes 835592 | tf_op jit(solution)/shard_map/ppermute | solution.py:235
  48.1 2.6 %collective-permute-start.9 = (s16[272,512]{1,0:T(8,128)(2,1)S(1)}, s16[272,512]{1,0:T(8,128)(2,1)S(1)}, u32[]{:S(2)}, u32[]{:S(2)}) collective-permute-start(s16[272,512]{1,0:T(8,128)(2,1)S(1)} %get-tuple-element.35.refs_9_), channel_id=1, source_target_pairs={{0,12},{1,13},{2,14},{3,15},{4,0},{5,1},{6,2},{7,3},{8,4},{9,5},{1... | collective-permute-start | bytes 835592 | tf_op jit(solution)/shard_map/ppermute | solution.py:235
  50.7 0.0 collective-permute-done.11.refs_2_
  50.7 1.9 %collective-permute-start.10 = (s16[272,512]{1,0:T(8,128)(2,1)S(1)}, s16[272,512]{1,0:T(8,128)(2,1)S(1)}, u32[]{:S(2)}, u32[]{:S(2)}) collective-permute-start(s16[272,512]{1,0:T(8,128)(2,1)S(1)} %get-tuple-element.33.refs_5_), channel_id=1, source_target_pairs={{0,2},{1,3},{2,0},{3,1},{4,6},{5,7},{6,4},{7,5},{8,10},{9,11},{10,... | collective-permute-start | bytes 835592 | tf_op jit(solution)/shard_map/ppermute | solution.py:235
  52.7 0.0 collective-permute-done.12.refs_3_
  52.7 0.0 collective-permute-done.13.refs_4_
  52.7 4.7 %encode.2 = (f32[512,512]{1,0:T(8,128)}, f32[96,128]{1,0:T(8,128)S(1)}) custom-call(s32[4]{0:T(128)S(1)} %pad_add_fusion.at_ref, bf16[4,512,512]{2,1,0:T(8,128)(2,1)S(1)} %get-tuple-element.23.refs_2_.refs_0_, bf16[4,512,512]{2,1,0:T(8,128)(2,1)} %collective-permute-done.refs_1_.refs_3_, s16[272,512]{1,0:T(8,128)(2,1)S(1)} %collective-permute-done.11.refs_2_, ...), custom_call_target="tpu_custom_call" | custom-call | tf_op jit(solution)/shard_map/encode/pallas_call | solution.py:258
  57.4 0.0 collective-permute-done.8.refs_2_
  57.4 0.0 collective-permute-done.9.refs_3_
  57.4 0.0 collective-permute-done.10.refs_4_
  57.4 4.8 %encode.3 = (f32[512,512]{1,0:T(8,128)}, f32[128,128]{1,0:T(8,128)S(1)}) custom-call(s32[4]{0:T(128)S(1)} %pad_add_fusion.at_ref, bf16[4,512,512]{2,1,0:T(8,128)(2,1)S(1)} %get-tuple-element.23.refs_2_.refs_0_, bf16[4,512,512]{2,1,0:T(8,128)(2,1)} %collective-permute-done.refs_1_.refs_3_, ...), custom_call_target="tpu_custom_call", output_to_operand_aliasing={{0}: (10, {})} | custom-call | tf_op jit(solution)/shard_map/encode/pallas_call | solution.py:258
  62.2 2.0 %collective-permute-start.14 = (f32[128,128]{1,0:T(8,128)S(1)}, f32[128,128]{1,0:T(8,128)S(1)}, u32[]{:S(2)}, u32[]{:S(2)}) collective-permute-start(f32[128,128]{1,0:T(8,128)S(1)} %get-tuple-element.43.refs_9_), channel_id=1, source_target_pairs={{0,16},{16,32},{32,48},{48,0},{64,80},{80,96},{96,112},{112,64},{1... | collective-permute-start | bytes 196616 | tf_op jit(solution)/shard_map/ppermute | solution.py:218
  64.1 0.9 %collective-permute-start.15 = (f32[128,128]{1,0:T(8,128)S(1)}, f32[128,128]{1,0:T(8,128)S(1)}, u32[]{:S(2)}, u32[]{:S(2)}) collective-permute-start(f32[128,128]{1,0:T(8,128)S(1)} %get-tuple-element.43.refs_9_), channel_id=1, source_target_pairs={{0,32},{16,48},{32,0},{48,16},{64,96},{80,112},{96,64},{112,80},{1... | collective-permute-start | bytes 196616 | tf_op jit(solution)/shard_map/ppermute | solution.py:218
  65.1 0.0 collective-permute-start.16
  65.1 1.6 %collective-permute-done.14 = f32[128,128]{1,0:T(8,128)S(1)} collective-permute-done((f32[128,128]{1,0:T(8,128)S(1)}, f32[128,128]{1,0:T(8,128)S(1)}, u32[]{:S(2)}, u32[]{:S(2)}) %collective-permute-start.14) | collective-permute-done | bytes 65568 | tf_op jit(solution)/shard_map/ppermute | solution.py:218
  66.7 3.3 %collective-permute-done.15 = f32[128,128]{1,0:T(8,128)S(1)} collective-permute-done((f32[128,128]{1,0:T(8,128)S(1)}, f32[128,128]{1,0:T(8,128)S(1)}, u32[]{:S(2)}, u32[]{:S(2)}) %collective-permute-start.15) | collective-permute-done | bytes 65568 | tf_op jit(solution)/shard_map/ppermute | solution.py:218
  69.9 0.7 collective-permute-done.16
  70.6 3.3 %collective-permute-start.17 = (f32[128,128]{1,0:T(8,128)S(1)}, f32[128,128]{1,0:T(8,128)S(1)}, u32[]{:S(2)}, u32[]{:S(2)}) collective-permute-start(f32[128,128]{1,0:T(8,128)S(1)} %add_add_fusion.refs_0_.refs_4_), channel_id=1, source_target_pairs={{0,64},{16,80},{32,96},{48,112},{64,128},{80,144},{96,160},{112,17... | collective-permute-start | bytes 196616 | tf_op jit(solution)/shard_map/ppermute | solution.py:222
  73.9 5.3 %collective-permute-start.18 = (f32[128,128]{1,0:T(8,128)S(1)}, f32[128,128]{1,0:T(8,128)S(1)}, u32[]{:S(2)}, u32[]{:S(2)}) collective-permute-start(f32[128,128]{1,0:T(8,128)S(1)} %add_add_fusion.refs_0_.refs_4_), channel_id=1, source_target_pairs={{0,128},{16,144},{32,160},{48,176},{64,192},{80,208},{96,224},{112... | collective-permute-start | bytes 196616 | tf_op jit(solution)/shard_map/ppermute | solution.py:222
  79.2 2.7 %collective-permute-start.19 = (f32[128,128]{1,0:T(8,128)S(1)}, f32[128,128]{1,0:T(8,128)S(1)}, u32[]{:S(2)}, u32[]{:S(2)}) collective-permute-start(f32[128,128]{1,0:T(8,128)S(1)} %add_add_fusion.refs_0_.refs_4_), channel_id=1, source_target_pairs={{0,192},{16,208},{32,224},{48,240},{64,0},{80,16},{96,32},{112,48}... | collective-permute-start | bytes 196616 | tf_op jit(solution)/shard_map/ppermute | solution.py:222
  81.8 0.0 collective-permute-done.17.refs_1_.refs_5_
  81.8 0.4 collective-permute-done.18.refs_2_.refs_6_
  82.2 2.6 %collective-permute-done.19.refs_3_.refs_7_ = f32[128,128]{1,0:T(8,128)S(1)} collective-permute-done((f32[128,128]{1,0:T(8,128)S(1)}, f32[128,128]{1,0:T(8,128)S(1)}, u32[]{:S(2)}, u32[]{:S(2)}) %collective-permute-start.19) | collective-permute-done | bytes 65568 | tf_op jit(solution)/shard_map/ppermute | solution.py:222
  84.8 7.0 %decode.1 = f32[512,512]{1,0:T(8,128)} custom-call(s32[4]{0:T(128)S(1)} %pad_add_fusion.at_ref, f32[128,128]{1,0:T(8,128)S(1)} %add_add_fusion.refs_0_.refs_4_, f32[128,128]{1,0:T(8,128)S(1)} %collective-permute-done.17.refs_1_.refs_5_, f32[128,128]{1,0:T(8,128)S(1)} %collective-permute-done.18.refs_2_.refs_6_, ...), custom_call_target="tpu_custom_call" | custom-call | tf_op jit(solution)/shard_map/decode/pallas_call | solution.py:258
  (14 shorter events, 0.1 us)
Async XLA Ops:
  0.8 3.4 %copy-start = (bf16[1,512,8192]{2,1,0:T(8,128)(2,1)S(1)}, bf16[1,512,8192]{2,1,0:T(8,128)(2,1)}, u32[]{:S(2)}) copy-start(bf16[1,512,8192]{2,1,0:T(8,128)(2,1)} %refs_2_.1) | copy-start | bytes 25165828
  5.2 3.7 %copy-start.7 = (s32[1,8,8,32]{3,2,1,0:T(8,128)S(1)}, s32[1,8,8,32]{3,2,1,0:T(8,128)}, u32[]{:S(2)}) copy-start(s32[1,8,8,32]{3,2,1,0:T(8,128)} %param.6) | copy-start | bytes 24580
  5.2 4.2 %collective-permute-start.1 = (bf16[4,512,512]{2,1,0:T(8,128)(2,1)S(1)}, bf16[4,512,512]{2,1,0:T(8,128)(2,1)S(1)}, u32[]{:S(2)}, u32[]{:S(2)}) collective-permute-start(bf16[4,512,512]{2,1,0:T(8,128)(2,1)S(1)} %pack.2.refs_3_), channel_id=1, source_target_pairs={{0,1},{1,0},{2,3},{3,2},{4,5},{5,4},{6,7},{7,6},{8,9},{9,8},{10,11... | collective-permute-start | bytes 6291464 | tf_op jit(solution)/shard_map/ppermute | solution.py:235
  8.4 1.8 %copy-start.3 = (bf16[4,512,512]{2,1,0:T(8,128)(2,1)}, bf16[4,512,512]{2,1,0:T(8,128)(2,1)S(1)}, u32[]{:S(2)}) copy-start(bf16[4,512,512]{2,1,0:T(8,128)(2,1)S(1)} %get-tuple-element.25.refs_0_.refs_2_) | copy-start | bytes 6291460
  8.4 6.0 %collective-permute-start = (bf16[4,512,512]{2,1,0:T(8,128)(2,1)}, bf16[4,512,512]{2,1,0:T(8,128)(2,1)}, u32[]{:S(2)}, u32[]{:S(2)}) collective-permute-start(bf16[4,512,512]{2,1,0:T(8,128)(2,1)} %get-tuple-element.24), channel_id=1, source_target_pairs={{0,1},{1,0},{2,3},{3,2},{4,5},{5,4},{6,7},{7,6},{8,9},{9,8},{10,11... | collective-permute-start | bytes 6291464 | tf_op jit(solution)/shard_map/ppermute | solution.py:235
  9.5 1.4 %copy-start.1 = (bf16[4,512,512]{2,1,0:T(8,128)(2,1)}, bf16[4,512,512]{2,1,0:T(8,128)(2,1)S(1)}, u32[]{:S(2)}) copy-start(bf16[4,512,512]{2,1,0:T(8,128)(2,1)S(1)} %collective-permute-done.1.refs_1_.refs_3_) | copy-start | bytes 6291460
  10.9 10.7 %collective-permute-start.3 = (s16[272,512]{1,0:T(8,128)(2,1)S(1)}, s16[272,512]{1,0:T(8,128)(2,1)S(1)}, u32[]{:S(2)}, u32[]{:S(2)}) collective-permute-start(s16[272,512]{1,0:T(8,128)(2,1)S(1)} %get-tuple-element.28), channel_id=1, source_target_pairs={{0,4},{1,5},{2,6},{3,7},{4,8},{5,9},{6,10},{7,11},{8,12},{9,13},{1... | collective-permute-start | bytes 835592 | tf_op jit(solution)/shard_map/ppermute | solution.py:235
  12.4 9.1 %collective-permute-start.4 = (s16[272,512]{1,0:T(8,128)(2,1)S(1)}, s16[272,512]{1,0:T(8,128)(2,1)S(1)}, u32[]{:S(2)}, u32[]{:S(2)}) collective-permute-start(s16[272,512]{1,0:T(8,128)(2,1)S(1)} %get-tuple-element.26.refs_2_), channel_id=1, source_target_pairs={{0,12},{1,13},{2,14},{3,15},{4,0},{5,1},{6,2},{7,3},{8,4},{9,5},{1... | collective-permute-start | bytes 835592 | tf_op jit(solution)/shard_map/ppermute | solution.py:235
  14.4 7.2 %copy-start.2 = (bf16[4,512,512]{2,1,0:T(8,128)(2,1)S(1)}, bf16[4,512,512]{2,1,0:T(8,128)(2,1)}, u32[]{:S(2)}) copy-start(bf16[4,512,512]{2,1,0:T(8,128)(2,1)} %copy-done.1) | copy-start | bytes 6291460
  14.4 7.1 %copy-start.4 = (bf16[4,512,512]{2,1,0:T(8,128)(2,1)S(1)}, bf16[4,512,512]{2,1,0:T(8,128)(2,1)}, u32[]{:S(2)}) copy-start(bf16[4,512,512]{2,1,0:T(8,128)(2,1)} %copy-done.3) | copy-start | bytes 6291460
  16.6 11.0 %collective-permute-start.7 = (s16[272,512]{1,0:T(8,128)(2,1)S(1)}, s16[272,512]{1,0:T(8,128)(2,1)S(1)}, u32[]{:S(2)}, u32[]{:S(2)}) collective-permute-start(s16[272,512]{1,0:T(8,128)(2,1)S(1)} %get-tuple-element.31), channel_id=1, source_target_pairs={{0,4},{1,5},{2,6},{3,7},{4,8},{5,9},{6,10},{7,11},{8,12},{9,13},{1... | collective-permute-start | bytes 835592 | tf_op jit(solution)/shard_map/ppermute | solution.py:235
  21.6 6.0 %copy-start.5 = (f32[512,512]{1,0:T(8,128)S(1)}, f32[512,512]{1,0:T(8,128)}, u32[]{:S(2)}) copy-start(f32[512,512]{1,0:T(8,128)} %refs_5_.1) | copy-start | bytes 3145732
  21.6 6.0 %copy-start.6 = (bf16[2,2,256,256]{3,2,1,0:T(8,128)(2,1)S(1)}, bf16[2,2,256,256]{3,2,1,0:T(8,128)(2,1)}, u32[]{:S(2)}) copy-start(bf16[2,2,256,256]{3,2,1,0:T(8,128)(2,1)} %constant.74.clone.refs_6_) | copy-start | bytes 1572868
  22.8 16.5 %collective-permute-start.5 = (s16[528,512]{1,0:T(8,128)(2,1)S(1)}, s16[528,512]{1,0:T(8,128)(2,1)S(1)}, u32[]{:S(2)}, u32[]{:S(2)}) collective-permute-start(s16[528,512]{1,0:T(8,128)(2,1)S(1)} %get-tuple-element.29), channel_id=1, source_target_pairs={{0,4},{1,5},{2,6},{3,7},{4,8},{5,9},{6,10},{7,11},{8,12},{9,13},{1... | collective-permute-start | bytes 1622024 | tf_op jit(solution)/shard_map/ppermute | solution.py:235
  23.7 15.6 %collective-permute-start.6 = (s16[528,512]{1,0:T(8,128)(2,1)S(1)}, s16[528,512]{1,0:T(8,128)(2,1)S(1)}, u32[]{:S(2)}, u32[]{:S(2)}) collective-permute-start(s16[528,512]{1,0:T(8,128)(2,1)S(1)} %get-tuple-element.30.refs_7_), channel_id=1, source_target_pairs={{0,12},{1,13},{2,14},{3,15},{4,0},{5,1},{6,2},{7,3},{8,4},{9,5},{1... | collective-permute-start | bytes 1622024 | tf_op jit(solution)/shard_map/ppermute | solution.py:235
  26.1 18.8 %collective-permute-start.2 = (s16[272,512]{1,0:T(8,128)(2,1)S(1)}, s16[272,512]{1,0:T(8,128)(2,1)S(1)}, u32[]{:S(2)}, u32[]{:S(2)}) collective-permute-start(s16[272,512]{1,0:T(8,128)(2,1)S(1)} %get-tuple-element.27.refs_6_), channel_id=1, source_target_pairs={{0,12},{1,13},{2,14},{3,15},{4,0},{5,1},{6,2},{7,3},{8,4},{9,5},{1... | collective-permute-start | bytes 835592 | tf_op jit(solution)/shard_map/ppermute | solution.py:235
  29.5 21.2 %collective-permute-start.11 = (s16[272,512]{1,0:T(8,128)(2,1)S(1)}, s16[272,512]{1,0:T(8,128)(2,1)S(1)}, u32[]{:S(2)}, u32[]{:S(2)}) collective-permute-start(s16[272,512]{1,0:T(8,128)(2,1)S(1)} %get-tuple-element.37), channel_id=1, source_target_pairs={{0,4},{1,5},{2,6},{3,7},{4,8},{5,9},{6,10},{7,11},{8,12},{9,13},{1... | collective-permute-start | bytes 835592 | tf_op jit(solution)/shard_map/ppermute | solution.py:235
  30.2 22.4 %collective-permute-start.12 = (s16[272,512]{1,0:T(8,128)(2,1)S(1)}, s16[272,512]{1,0:T(8,128)(2,1)S(1)}, u32[]{:S(2)}, u32[]{:S(2)}) collective-permute-start(s16[272,512]{1,0:T(8,128)(2,1)S(1)} %get-tuple-element.38), channel_id=1, source_target_pairs={{0,12},{1,13},{2,14},{3,15},{4,0},{5,1},{6,2},{7,3},{8,4},{9,5},{1... | collective-permute-start | bytes 835592 | tf_op jit(solution)/shard_map/ppermute | solution.py:235
  40.4 12.3 %collective-permute-start.13 = (s16[272,512]{1,0:T(8,128)(2,1)S(1)}, s16[272,512]{1,0:T(8,128)(2,1)S(1)}, u32[]{:S(2)}, u32[]{:S(2)}) collective-permute-start(s16[272,512]{1,0:T(8,128)(2,1)S(1)} %get-tuple-element.39), channel_id=1, source_target_pairs={{0,2},{1,3},{2,0},{3,1},{4,6},{5,7},{6,4},{7,5},{8,10},{9,11},{10,... | collective-permute-start | bytes 835592 | tf_op jit(solution)/shard_map/ppermute | solution.py:235
  46.8 10.6 %collective-permute-start.8 = (s16[272,512]{1,0:T(8,128)(2,1)S(1)}, s16[272,512]{1,0:T(8,128)(2,1)S(1)}, u32[]{:S(2)}, u32[]{:S(2)}) collective-permute-start(s16[272,512]{1,0:T(8,128)(2,1)S(1)} %get-tuple-element.34), channel_id=1, source_target_pairs={{0,4},{1,5},{2,6},{3,7},{4,8},{5,9},{6,10},{7,11},{8,12},{9,13},{1... | collective-permute-start | bytes 835592 | tf_op jit(solution)/shard_map/ppermute | solution.py:235
  48.1 9.3 %collective-permute-start.9 = (s16[272,512]{1,0:T(8,128)(2,1)S(1)}, s16[272,512]{1,0:T(8,128)(2,1)S(1)}, u32[]{:S(2)}, u32[]{:S(2)}) collective-permute-start(s16[272,512]{1,0:T(8,128)(2,1)S(1)} %get-tuple-element.35.refs_9_), channel_id=1, source_target_pairs={{0,12},{1,13},{2,14},{3,15},{4,0},{5,1},{6,2},{7,3},{8,4},{9,5},{1... | collective-permute-start | bytes 835592 | tf_op jit(solution)/shard_map/ppermute | solution.py:235
  50.7 6.7 %collective-permute-start.10 = (s16[272,512]{1,0:T(8,128)(2,1)S(1)}, s16[272,512]{1,0:T(8,128)(2,1)S(1)}, u32[]{:S(2)}, u32[]{:S(2)}) collective-permute-start(s16[272,512]{1,0:T(8,128)(2,1)S(1)} %get-tuple-element.33.refs_5_), channel_id=1, source_target_pairs={{0,2},{1,3},{2,0},{3,1},{4,6},{5,7},{6,4},{7,5},{8,10},{9,11},{10,... | collective-permute-start | bytes 835592 | tf_op jit(solution)/shard_map/ppermute | solution.py:235
  62.2 4.5 %collective-permute-start.14 = (f32[128,128]{1,0:T(8,128)S(1)}, f32[128,128]{1,0:T(8,128)S(1)}, u32[]{:S(2)}, u32[]{:S(2)}) collective-permute-start(f32[128,128]{1,0:T(8,128)S(1)} %get-tuple-element.43.refs_9_), channel_id=1, source_target_pairs={{0,16},{16,32},{32,48},{48,0},{64,80},{80,96},{96,112},{112,64},{1... | collective-permute-start | bytes 196616 | tf_op jit(solution)/shard_map/ppermute | solution.py:218
  64.1 5.8 %collective-permute-start.15 = (f32[128,128]{1,0:T(8,128)S(1)}, f32[128,128]{1,0:T(8,128)S(1)}, u32[]{:S(2)}, u32[]{:S(2)}) collective-permute-start(f32[128,128]{1,0:T(8,128)S(1)} %get-tuple-element.43.refs_9_), channel_id=1, source_target_pairs={{0,32},{16,48},{32,0},{48,16},{64,96},{80,112},{96,64},{112,80},{1... | collective-permute-start | bytes 196616 | tf_op jit(solution)/shard_map/ppermute | solution.py:218
  65.1 5.5 %collective-permute-start.16 = (f32[128,128]{1,0:T(8,128)S(1)}, f32[128,128]{1,0:T(8,128)S(1)}, u32[]{:S(2)}, u32[]{:S(2)}) collective-permute-start(f32[128,128]{1,0:T(8,128)S(1)} %get-tuple-element.43.refs_9_), channel_id=1, source_target_pairs={{0,48},{16,0},{32,16},{48,32},{64,112},{80,64},{96,80},{112,96},{1... | collective-permute-start | bytes 196616 | tf_op jit(solution)/shard_map/ppermute | solution.py:218
  70.6 11.2 %collective-permute-start.17 = (f32[128,128]{1,0:T(8,128)S(1)}, f32[128,128]{1,0:T(8,128)S(1)}, u32[]{:S(2)}, u32[]{:S(2)}) collective-permute-start(f32[128,128]{1,0:T(8,128)S(1)} %add_add_fusion.refs_0_.refs_4_), channel_id=1, source_target_pairs={{0,64},{16,80},{32,96},{48,112},{64,128},{80,144},{96,160},{112,17... | collective-permute-start | bytes 196616 | tf_op jit(solution)/shard_map/ppermute | solution.py:222
  73.9 8.3 %collective-permute-start.18 = (f32[128,128]{1,0:T(8,128)S(1)}, f32[128,128]{1,0:T(8,128)S(1)}, u32[]{:S(2)}, u32[]{:S(2)}) collective-permute-start(f32[128,128]{1,0:T(8,128)S(1)} %add_add_fusion.refs_0_.refs_4_), channel_id=1, source_target_pairs={{0,128},{16,144},{32,160},{48,176},{64,192},{80,208},{96,224},{112... | collective-permute-start | bytes 196616 | tf_op jit(solution)/shard_map/ppermute | solution.py:222
  79.2 5.7 %collective-permute-start.19 = (f32[128,128]{1,0:T(8,128)S(1)}, f32[128,128]{1,0:T(8,128)S(1)}, u32[]{:S(2)}, u32[]{:S(2)}) collective-permute-start(f32[128,128]{1,0:T(8,128)S(1)} %add_add_fusion.refs_0_.refs_4_), channel_id=1, source_target_pairs={{0,192},{16,208},{32,224},{48,240},{64,0},{80,16},{96,32},{112,48}... | collective-permute-start | bytes 196616 | tf_op jit(solution)/shard_map/ppermute | solution.py:222

commit v4 on v3

--- a/solution.py
+++ b/solution.py
@@ -80,11 +80,9 @@
     return lax.dot_general(a, b, (((0,), (0,)), ((), ())), preferred_element_type=F32)
 
 
-def encode(field, pos_ref, basis, shift, fresh_ref, kept_ref):
+def encode(field, pos_ref, basis, fresh_ref, kept_ref):
     rows, cols = field.shape
     lane_block = lax.broadcasted_iota(jnp.int32, (1, KEPT), 1) // K
-    per_group = KEPT // K
-    kept = [None] * (rows // GROUP * (cols // WIDE))
     for half in range(cols // WIDE):
         span = slice(half * WIDE, (half + 1) * WIDE)
         part = field[:, span]
@@ -103,14 +101,8 @@
             three = jnp.concatenate([high, low, rest], axis=0)
             rows_of = by_rows(three, jnp.concatenate([row_one] * 3, axis=0))
             found = jnp.where(on_col, rows_of, F32(0.0))
-            lines = []
-            for q in range(per_group):
-                line = jnp.sum(found[q * GROUP:(q + 1) * GROUP], axis=0, keepdims=True)
-                lines.append(pltpu.roll(line, (KEPT - q * K) % KEPT, 1) if q else line)
-            kept[g] = jnp.concatenate(lines, axis=0)
+            kept_ref[g:g + 1] = jnp.sum(found, axis=0, keepdims=True)
         fresh_ref[:, span] = part - inverse(jnp.concatenate(dense, axis=0), basis)
-    kept = jnp.concatenate(kept, axis=0)
-    kept_ref[...] = pltpu.roll(kept, shift, 1)
 
 
 LEVELS = 32767.0
@@ -182,27 +174,38 @@
     for ref in before:
         kept_ref[first:first + ref.shape[0]] = ref[...]
         first += ref.shape[0]
-    encode(field, pos_ref, basis_ref, at_ref[3] * K, fresh_ref, kept_ref.at[first:])
+    encode(field, pos_ref, basis_ref, fresh_ref, kept_ref.at[first:])
+
+
+def spread_kernel(at_ref, *refs):
+    *sent, out_ref = refs
+    lane_block = lax.broadcasted_iota(jnp.int32, (1, KEPT), 1) // K
+    groups = out_ref.shape[1]
+    for q in range(KEPT // K):
+        total = None
+        for s in range(2 * len(sent)):
+            part = jnp.where(lane_block == q, sent[s // 2][s % 2], F32(0.0))
+            shift = (s - q) * K % KEPT
+            part = pltpu.roll(part, shift, 1) if shift else part
+            total = part if total is None else total + part
+        out_ref[2 * q] = total[:groups]
+        out_ref[2 * q + 1] = total[groups:]
 
 
 def decode_kernel(at_ref, *refs):
     *sent, basis, out_ref = refs
-    count = len(sent) // 2
-    vals, poss = sent[:count], sent[count:]
-    per_row = out_ref.shape[1] // GROUP
-    dense = []
-    for i in range(vals[0].shape[0]):
-        val = jnp.concatenate([ref[i:i + 1] for ref in vals], axis=1)
-        pos = jnp.concatenate([ref[i:i + 1] for ref in poss], axis=1).astype(jnp.int32)
-        high, low = cut(jnp.where(match(pos // GROUP, GROUP), val, F32(0.0)))
-        both = by_lanes(jnp.concatenate([high, low], axis=0), one(match(pos % GROUP, GROUP)))
-        dense.append(both[:GROUP] + both[GROUP:])
-    wide = WIDE // GROUP
-    for half in range(out_ref.shape[1] // WIDE):
-        lines = [
-            jnp.concatenate(dense[a + half * wide:a + (half + 1) * wide], axis=1)
-            for a in range(0, len(dense), per_row)
-        ]
+    halves = out_ref.shape[1] // WIDE
+    for half in range(halves):
+        lines = []
+        for g in range(half, sent[0].shape[1], halves):
+            dense = []
+            for q in range(WIDE // GROUP):
+                pos = jnp.concatenate([ref[2 * q, g:g + 1] for ref in sent], axis=1).astype(jnp.int32)
+                val = jnp.concatenate([ref[2 * q + 1, g:g + 1] for ref in sent], axis=1)
+                high, low = cut(jnp.where(match(pos // GROUP, GROUP), val, F32(0.0)))
+                both = by_lanes(jnp.concatenate([high, low], axis=0), one(match(pos % GROUP, GROUP)))
+                dense.append(both[:GROUP] + both[GROUP:])
+            lines.append(jnp.concatenate(dense, axis=1))
         out_ref[:, half * WIDE:(half + 1) * WIDE] = inverse(jnp.concatenate(lines, axis=0), basis)
 
 
@@ -218,8 +221,10 @@
     return [own] + [lax.ppermute(own, "rep", across(4, 4, 0, s)) for s in (1, 2, 3)]
 
 
-def along_z(near):
-    return [near] + [lax.ppermute(near, "rep", across(4, 4, s, 0)) for s in (1, 2, 3)]
+def along_z(own):
+    there = lax.ppermute(own, "rep", [(h * 4 + x, (h ^ 1) * 4 + x) for h in range(4) for x in range(4)])
+    two = jnp.stack([own, there])
+    return [two, lax.ppermute(two, "rep", [(h * 4 + x, (3 - h) * 4 + x) for h in range(4) for x in range(4)])]
 
 
 def places(shift_y, flip_z, flip_core):
@@ -278,22 +283,21 @@
 
 HALF = 256
 SENT = jnp.int16
-VMEM = 16 * 1024 * 1024
-
-
-STEP = 128
+VMEM = 10 * 1024 * 1024
+
+
+STEP = 256
 
 
 def local(partial_grads, momentum, freq_index):
     rows, cols = momentum.shape
     basis = jnp.asarray(dct_constants())
     pos = freq_index.reshape(rows // GROUP * (cols // WIDE), KEPT)
-    me, rep = lax.axis_index("fsdp"), lax.axis_index("rep")
-    at = jnp.stack([me // 4, me // 2 % 2, me % 2, rep % 4]).astype(jnp.int32)
-    lines = jnp.tile(freq_index.reshape(rows // GROUP * (cols // GROUP), K).astype(F32), (1, KEPT // K))
-    lines = jnp.where(jnp.arange(KEPT)[None] // K == rep % 4, lines, F32(0.0))
+    me = lax.axis_index("fsdp")
+    at = jnp.stack([me // 4, me // 2 % 2, me % 2]).astype(jnp.int32)
     groups = HALF // GROUP * (cols // WIDE)
     poss = [pos[i * groups:(i + 1) * groups] for i in range(rows // HALF)]
+    places_sent = pos.astype(F32)
     program = Program(at)
     call = program.call
     quarter = jax.ShapeDtypeStruct((4, rows, cols), BF)
@@ -329,9 +333,10 @@
     for dz in (1, 0):
         far[dz] = round_y(call(far_kernel, "far", both(dz, 2), [out(HALF)] * 2))
         if dz:
-            program.last += [lines, *poss]
+            program.last += [places_sent, *poss]
     across_near = round_y(call(
         near_kernel, "near", both(1, 1) + both(1, -1) + [whole(far[1][0]), whole(far[1][1])], [out(rows)] * 2))
+    program.last += far[0]
     *top, decayed, held = call(
         near_top_kernel, "near",
         both(0, 1, HALF, 0) + both(0, -1, HALF, 0) + [whole(far[0][0]), whole(momentum), whole(basis)],
@@ -342,9 +347,9 @@
     crossed = [send(x, flip_z=1) for x in crossing]
     near.append(round_y(call(
         near_low_kernel, "near", both(0, 1, HALF, 1) + both(0, -1, HALF, 1) + [whole(far[0][1])], [out(HALF)] * 2)))
-    fresh, kept = None, lines
+    fresh, kept = None, places_sent
     for i in range(rows // HALF):
-        height = kept.shape[0] + HALF // GROUP * (cols // GROUP)
+        height = kept.shape[0] + groups
         half_spec = pl.BlockSpec((HALF, cols), lambda s, at, i=i: (i, 0))
         fresh, kept = call(
             encode_kernel, "encode",
@@ -354,15 +359,17 @@
              (jax.ShapeDtypeStruct((height, KEPT), F32), pl.BlockSpec((height, KEPT), lambda s, at: (0, 0)))],
             onto=fresh,
         )
-    sent = along_z(sum(along_x(kept)))
-    per_step, steps = STEP // GROUP * (cols // GROUP), rows // STEP
-    val_spec = pl.BlockSpec((per_step, KEPT), lambda s, at: (steps + s, 0))
-    pos_spec = pl.BlockSpec((per_step, KEPT), lambda s, at: (s, 0))
+    sent = along_z(kept)
+    near_shape = (2 * (KEPT // K), pos.shape[0], KEPT)
+    lines, = call(
+        spread_kernel, "spread", [whole(x) for x in sent],
+        [(jax.ShapeDtypeStruct(near_shape, F32), pl.BlockSpec(near_shape, lambda s, at: (0, 0, 0)))])
+    sent = along_x(lines)
+    spec = pl.BlockSpec((near_shape[0], STEP // GROUP * (cols // WIDE), KEPT), lambda s, at: (0, s, 0))
     update, = call(
-        decode_kernel, "decode",
-        [(x, val_spec) for x in sent] + [(x, pos_spec) for x in sent] + [whole(held)],
+        decode_kernel, "decode", [(x, spec) for x in sent] + [whole(held)],
         [(jax.ShapeDtypeStruct((rows, cols), F32), pl.BlockSpec((STEP, cols), lambda s, at: (s, 0)))],
-        (steps,),
+        (rows // STEP,),
     )
     return fresh, update
 

time: 92.1 us -> 89.5 us (0.972)
  starting transfers between devices: 33.9 us -> 29.3 us
    ppermute x3 -> x2, starting transfers between devices: 11.2 us -> 8.32 us  [the longest x1 5.05 us: along_z(): lax.ppermute(two, 'rep', [(h * 4 + x, (3 - h) * 4 + x) for h in range(4)...]
    ppermute x14, starting transfers between devices: 19.7 us -> 18 us  [send(): return lax.ppermute(x, 'fsdp', places(shift_y, flip_z, flip_core))]
    pallas_call x11 -> x12, Pallas kernels: 29.7 us -> 30.5 us  [call(): pl.pallas_call(kernel, grid_spec=pltpu.PrefetchScalarGridSpec(num_scalar_...]
    ppermute x3 -> x2, waiting for transfers between devices: 2.99 us -> 3.61 us  [the longest x1 1.89 us: along_z(): lax.ppermute(two, 'rep', [(h * 4 + x, (3 - h) * 4 + x) for h in range(4)...]
  transfers between devices with their start and end apart: 20 -> 19, of which waited for: 10 -> 13; matrix products, arithmetic and copies ran while one was open for 0% -> 0% of each run, Pallas kernels for 18% -> 19%
where the time goes in v4:
time: 89.5 us; the launch traced here: 88.4 us
  Pallas kernels  30.5 us (34%)
  starting transfers between devices  29.3 us (33%)
  waiting for transfers between devices  23.6 us (26%)
  local copies, waits for them, and re-layouts  4.22 us (5%)
    pallas_call x12, Pallas kernels, call(): pl.pallas_call(kernel, grid_spec=pltpu.PrefetchScalarGridSpec(num_scalar_...  30.5 us
    ppermute x14, starting transfers between devices, send(): return lax.ppermute(x, 'fsdp', places(shift_y, flip_z, flip_core))  18 us
    ppermute x14, waiting for transfers between devices, send(): return lax.ppermute(x, 'fsdp', places(shift_y, flip_z, flip_core))  14.5 us
    ppermute x3, waiting for transfers between devices, along_x(): lax.ppermute(own, 'rep', across(4, 4, 0, s))  5.47 us
    ppermute x1, starting transfers between devices, along_z(): lax.ppermute(two, 'rep', [(h * 4 + x, (3 - h) * 4 + x) for h in range(4)...  5.05 us
    unnamed x16, local copies, waits for them, and re-layouts  4 us
    ppermute x1, starting transfers between devices, along_z(): lax.ppermute(own, 'rep', [(h * 4 + x, (h ^ 1) * 4 + x) for h in range(4)...  3.27 us
    ppermute x3, starting transfers between devices, along_x(): lax.ppermute(own, 'rep', across(4, 4, 0, s))  2.98 us
  transfers between devices with their start and end apart: 19, of which 13 were waited for; matrix products, arithmetic and copies ran while one was open for 0% of the time, Pallas kernels for 19%

profile of v4, /device:TPU:6, one launch (start us, length us, event | category | flops | bytes accessed | tf_op | source)
XLA Modules:
  0.0 88.4 jit_solution(16869324962336620744)
XLA Ops:
  0.7 0.1 pad_add_fusion.at_ref
  0.7 0.0 copy-start
  0.7 3.4 %copy-done = bf16[1,512,8192]{2,1,0:T(8,128)(2,1)S(1)} copy-done((bf16[1,512,8192]{2,1,0:T(8,128)(2,1)S(1)}, bf16[1,512,8192]{2,1,0:T(8,128)(2,1)}, u32[]{:S(2)}) %copy-start) | copy-done | bytes 8388632
  4.1 1.1 %pack.2.refs_3_ = bf16[4,512,512]{2,1,0:T(8,128)(2,1)S(1)} custom-call(s32[3]{0:T(128)S(1)} %pad_add_fusion.at_ref, bf16[1,512,8192]{2,1,0:T(8,128)(2,1)S(1)} %copy-done), custom_call_target="tpu_custom_call" | custom-call | tf_op jit(solution)/shard_map/pack/pallas_call | solution.py:263
  5.2 0.1 collective-permute-start.1
  5.3 3.1 %pack.3 = (bf16[4,512,512]{2,1,0:T(8,128)(2,1)}, bf16[4,512,512]{2,1,0:T(8,128)(2,1)S(1)}, bf16[4,512,512]{2,1,0:T(8,128)(2,1)S(1)}) custom-call(s32[3]{0:T(128)S(1)} %pad_add_fusion.at_ref, bf16[1,512,8192]{2,1,0:T(8,128)(2,1)S(1)} %copy-done, bf16[1,512,8192]{2,1,0:T(8,128)(2,1)S(1)} %copy-done, bf16[1,512,8192]{2,1,0:T(8,128)(2,1)S(1)} %copy-done, ...), custom_call_target="tpu_custom_call" | custom-call | tf_op jit(solution)/shard_map/pack/pallas_call | solution.py:263
  8.4 0.0 copy-start.3
  8.4 0.5 collective-permute-start
  8.9 0.5 collective-permute-done.1.refs_1_.refs_3_
  9.4 0.8 far.2
  10.2 0.0 copy-done.3
  10.2 0.6 copy-done.1
  10.8 1.6 %collective-permute-start.3 = (s16[272,512]{1,0:T(8,128)(2,1)S(1)}, s16[272,512]{1,0:T(8,128)(2,1)S(1)}, u32[]{:S(2)}, u32[]{:S(2)}) collective-permute-start(s16[272,512]{1,0:T(8,128)(2,1)S(1)} %get-tuple-element.28), channel_id=1, source_target_pairs={{0,4},{1,5},{2,6},{3,7},{4,8},{5,9},{6,10},{7,11},{8,12},{9,13},{1... | collective-permute-start | bytes 835592 | tf_op jit(solution)/shard_map/ppermute | solution.py:240
  12.4 1.7 %collective-permute-start.4 = (s16[272,512]{1,0:T(8,128)(2,1)S(1)}, s16[272,512]{1,0:T(8,128)(2,1)S(1)}, u32[]{:S(2)}, u32[]{:S(2)}) collective-permute-start(s16[272,512]{1,0:T(8,128)(2,1)S(1)} %get-tuple-element.26.refs_2_), channel_id=1, source_target_pairs={{0,12},{1,13},{2,14},{3,15},{4,0},{5,1},{6,2},{7,3},{8,4},{9,5},{1... | collective-permute-start | bytes 835592 | tf_op jit(solution)/shard_map/ppermute | solution.py:240
  14.1 0.0 copy-done.7
  14.1 0.1 slice.13.refs_4_.refs_6_
  14.2 0.1 slice.15.refs_5_.refs_6_
  14.2 0.1 convert_element_type.6.refs_3_.refs_8_
  14.3 0.0 collective-permute-done.refs_1_.refs_3_
  14.3 2.1 %far.3 = (s16[272,512]{1,0:T(8,128)(2,1)S(1)}, s16[272,512]{1,0:T(8,128)(2,1)S(1)}) custom-call(s32[3]{0:T(128)S(1)} %pad_add_fusion.at_ref, bf16[4,512,512]{2,1,0:T(8,128)(2,1)S(1)} %get-tuple-element.23.refs_2_.refs_0_, bf16[4,512,512]{2,1,0:T(8,128)(2,1)} %collective-permute-done.refs_1_.refs_3_, s16[272,512]{1,0:T(8,128)(2,1)S(1)} %get-tuple-element.26.refs_2_, ...), custom_call_target="tpu_custom_call" | custom-call | tf_op jit(solution)/shard_map/far/pallas_call | solution.py:263
  16.4 1.9 %collective-permute-start.2 = (s16[272,512]{1,0:T(8,128)(2,1)S(1)}, s16[272,512]{1,0:T(8,128)(2,1)S(1)}, u32[]{:S(2)}, u32[]{:S(2)}) collective-permute-start(s16[272,512]{1,0:T(8,128)(2,1)S(1)} %get-tuple-element.27.refs_6_), channel_id=1, source_target_pairs={{0,12},{1,13},{2,14},{3,15},{4,0},{5,1},{6,2},{7,3},{8,4},{9,5},{1... | collective-permute-start | bytes 835592 | tf_op jit(solution)/shard_map/ppermute | solution.py:240
  18.3 0.2 collective-permute-start.7
  18.5 2.3 %collective-permute-done.3.refs_4_ = s16[272,512]{1,0:T(8,128)(2,1)S(1)} collective-permute-done((s16[272,512]{1,0:T(8,128)(2,1)S(1)}, s16[272,512]{1,0:T(8,128)(2,1)S(1)}, u32[]{:S(2)}, u32[]{:S(2)}) %collective-permute-start.3) | collective-permute-done | bytes 278560 | tf_op jit(solution)/shard_map/ppermute | solution.py:240
  20.8 1.1 %collective-permute-done.4.refs_5_ = s16[272,512]{1,0:T(8,128)(2,1)S(1)} collective-permute-done((s16[272,512]{1,0:T(8,128)(2,1)S(1)}, s16[272,512]{1,0:T(8,128)(2,1)S(1)}, u32[]{:S(2)}, u32[]{:S(2)}) %collective-permute-start.4) | collective-permute-done | bytes 278560 | tf_op jit(solution)/shard_map/ppermute | solution.py:240
  22.0 0.0 copy-done.2
  22.0 0.0 copy-done.4
  22.0 1.2 %near.3 = (s16[528,512]{1,0:T(8,128)(2,1)S(1)}, s16[528,512]{1,0:T(8,128)(2,1)S(1)}) custom-call(s32[3]{0:T(128)S(1)} %pad_add_fusion.at_ref, bf16[4,512,512]{2,1,0:T(8,128)(2,1)S(1)} %copy-done.4, bf16[4,512,512]{2,1,0:T(8,128)(2,1)S(1)} %copy-done.2, bf16[4,512,512]{2,1,0:T(8,128)(2,1)S(1)} %copy-done.4, bf16[4,512,512]{2,1,0:T(8,128)(2,1)S(1)} %copy-done.2, ...), custom_call_target="tpu_custom_call" | custom-call | tf_op jit(solution)/shard_map/near/pallas_call | solution.py:263
  23.2 1.7 %collective-permute-start.5 = (s16[528,512]{1,0:T(8,128)(2,1)S(1)}, s16[528,512]{1,0:T(8,128)(2,1)S(1)}, u32[]{:S(2)}, u32[]{:S(2)}) collective-permute-start(s16[528,512]{1,0:T(8,128)(2,1)S(1)} %get-tuple-element.29), channel_id=1, source_target_pairs={{0,4},{1,5},{2,6},{3,7},{4,8},{5,9},{6,10},{7,11},{8,12},{9,13},{1... | collective-permute-start | bytes 1622024 | tf_op jit(solution)/shard_map/ppermute | solution.py:240
  24.8 1.7 %collective-permute-start.6 = (s16[528,512]{1,0:T(8,128)(2,1)S(1)}, s16[528,512]{1,0:T(8,128)(2,1)S(1)}, u32[]{:S(2)}, u32[]{:S(2)}) collective-permute-start(s16[528,512]{1,0:T(8,128)(2,1)S(1)} %get-tuple-element.30.refs_7_), channel_id=1, source_target_pairs={{0,12},{1,13},{2,14},{3,15},{4,0},{5,1},{6,2},{7,3},{8,4},{9,5},{1... | collective-permute-start | bytes 1622024 | tf_op jit(solution)/shard_map/ppermute | solution.py:240
  26.5 1.5 %collective-permute-done.2.refs_9_.refs_4_ = s16[272,512]{1,0:T(8,128)(2,1)S(1)} collective-permute-done((s16[272,512]{1,0:T(8,128)(2,1)S(1)}, s16[272,512]{1,0:T(8,128)(2,1)S(1)}, u32[]{:S(2)}, u32[]{:S(2)}) %collective-permute-start.2) | collective-permute-done | bytes 278560 | tf_op jit(solution)/shard_map/ppermute | solution.py:240
  27.9 1.2 %collective-permute-done.7.refs_4_.refs_8_ = s16[272,512]{1,0:T(8,128)(2,1)S(1)} collective-permute-done((s16[272,512]{1,0:T(8,128)(2,1)S(1)}, s16[272,512]{1,0:T(8,128)(2,1)S(1)}, u32[]{:S(2)}, u32[]{:S(2)}) %collective-permute-start.7) | collective-permute-done | bytes 278560 | tf_op jit(solution)/shard_map/ppermute | solution.py:240
  29.1 0.0 copy-done.5
  29.1 0.0 copy-done.6
  29.1 2.0 %near.4 = (s16[272,512]{1,0:T(8,128)(2,1)S(1)}, s16[272,512]{1,0:T(8,128)(2,1)S(1)}, f32[512,512]{1,0:T(8,128)S(1)}, bf16[2,2,256,256]{3,2,1,0:T(8,128)(2,1)S(1)}) custom-call(s32[3]{0:T(128)S(1)} %pad_add_fusion.at_ref, bf16[4,512,512]{2,1,0:T(8,128)(2,1)S(1)} %get-tuple-element.23.refs_2_.refs_0_, ...), custom_call_target="tpu_custom_call" | custom-call | tf_op jit(solution)/shard_map/near/pallas_call | solution.py:263
  31.1 0.5 collective-permute-start.11
  31.6 2.8 %collective-permute-start.12 = (s16[272,512]{1,0:T(8,128)(2,1)S(1)}, s16[272,512]{1,0:T(8,128)(2,1)S(1)}, u32[]{:S(2)}, u32[]{:S(2)}) collective-permute-start(s16[272,512]{1,0:T(8,128)(2,1)S(1)} %get-tuple-element.38), channel_id=1, source_target_pairs={{0,12},{1,13},{2,14},{3,15},{4,0},{5,1},{6,2},{7,3},{8,4},{9,5},{1... | collective-permute-start | bytes 835592 | tf_op jit(solution)/shard_map/ppermute | solution.py:240
  34.4 6.3 %collective-permute-done.5.refs_2_ = s16[528,512]{1,0:T(8,128)(2,1)S(1)} collective-permute-done((s16[528,512]{1,0:T(8,128)(2,1)S(1)}, s16[528,512]{1,0:T(8,128)(2,1)S(1)}, u32[]{:S(2)}, u32[]{:S(2)}) %collective-permute-start.5) | collective-permute-done | bytes 540704 | tf_op jit(solution)/shard_map/ppermute | solution.py:240
  40.7 0.0 collective-permute-done.6.refs_3_
  40.7 1.1 %cross.1 = (s16[272,512]{1,0:T(8,128)(2,1)S(1)}, s16[272,512]{1,0:T(8,128)(2,1)S(1)}) custom-call(s32[3]{0:T(128)S(1)} %pad_add_fusion.at_ref, bf16[4,512,512]{2,1,0:T(8,128)(2,1)S(1)} %copy-done.4, bf16[4,512,512]{2,1,0:T(8,128)(2,1)S(1)} %copy-done.2, s16[528,512]{1,0:T(8,128)(2,1)S(1)} %collective-permute-done.5.refs_2_, ...), custom_call_target="tpu_custom_call" | custom-call | tf_op jit(solution)/shard_map/cross/pallas_call | solution.py:263
  41.7 2.0 %collective-permute-start.13 = (s16[272,512]{1,0:T(8,128)(2,1)S(1)}, s16[272,512]{1,0:T(8,128)(2,1)S(1)}, u32[]{:S(2)}, u32[]{:S(2)}) collective-permute-start(s16[272,512]{1,0:T(8,128)(2,1)S(1)} %get-tuple-element.39), channel_id=1, source_target_pairs={{0,2},{1,3},{2,0},{3,1},{4,6},{5,7},{6,4},{7,5},{8,10},{9,11},{10,... | collective-permute-start | bytes 835592 | tf_op jit(solution)/shard_map/ppermute | solution.py:240
  43.7 1.9 %near.5 = (s16[272,512]{1,0:T(8,128)(2,1)S(1)}, s16[272,512]{1,0:T(8,128)(2,1)S(1)}) custom-call(s32[3]{0:T(128)S(1)} %pad_add_fusion.at_ref, bf16[4,512,512]{2,1,0:T(8,128)(2,1)S(1)} %get-tuple-element.23.refs_2_.refs_0_, bf16[4,512,512]{2,1,0:T(8,128)(2,1)} %collective-permute-done.refs_1_.refs_3_, ...), custom_call_target="tpu_custom_call" | custom-call | tf_op jit(solution)/shard_map/near/pallas_call | solution.py:263
  45.6 0.7 collective-permute-start.8
  46.3 2.6 %collective-permute-start.9 = (s16[272,512]{1,0:T(8,128)(2,1)S(1)}, s16[272,512]{1,0:T(8,128)(2,1)S(1)}, u32[]{:S(2)}, u32[]{:S(2)}) collective-permute-start(s16[272,512]{1,0:T(8,128)(2,1)S(1)} %get-tuple-element.35.refs_9_), channel_id=1, source_target_pairs={{0,12},{1,13},{2,14},{3,15},{4,0},{5,1},{6,2},{7,3},{8,4},{9,5},{1... | collective-permute-start | bytes 835592 | tf_op jit(solution)/shard_map/ppermute | solution.py:240
  49.0 0.0 collective-permute-done.11.refs_2_
  49.0 0.1 collective-permute-start.10
  49.1 0.0 collective-permute-done.12.refs_3_
  49.1 0.2 collective-permute-done.13.refs_4_
  49.3 4.8 %encode.2 = (f32[512,512]{1,0:T(8,128)}, f32[24,128]{1,0:T(8,128)S(1)}) custom-call(s32[3]{0:T(128)S(1)} %pad_add_fusion.at_ref, bf16[4,512,512]{2,1,0:T(8,128)(2,1)S(1)} %get-tuple-element.23.refs_2_.refs_0_, bf16[4,512,512]{2,1,0:T(8,128)(2,1)} %collective-permute-done.refs_1_.refs_3_, s16[272,512]{1,0:T(8,128)(2,1)S(1)} %collective-permute-done.11.refs_2_, ...), custom_call_target="tpu_custom_call" | custom-call | tf_op jit(solution)/shard_map/encode/pallas_call | solution.py:263
  54.0 0.0 collective-permute-done.8.refs_2_
  54.0 0.0 collective-permute-done.9.refs_3_
  54.0 1.5 %collective-permute-done.10.refs_4_ = s16[272,512]{1,0:T(8,128)(2,1)S(1)} collective-permute-done((s16[272,512]{1,0:T(8,128)(2,1)S(1)}, s16[272,512]{1,0:T(8,128)(2,1)S(1)}, u32[]{:S(2)}, u32[]{:S(2)}) %collective-permute-start.10) | collective-permute-done | bytes 278560 | tf_op jit(solution)/shard_map/ppermute | solution.py:240
  55.5 4.7 %encode.3 = (f32[512,512]{1,0:T(8,128)}, f32[32,128]{1,0:T(8,128)S(1)}) custom-call(s32[3]{0:T(128)S(1)} %pad_add_fusion.at_ref, bf16[4,512,512]{2,1,0:T(8,128)(2,1)S(1)} %get-tuple-element.23.refs_2_.refs_0_, bf16[4,512,512]{2,1,0:T(8,128)(2,1)} %collective-permute-done.refs_1_.refs_3_, ...), custom_call_target="tpu_custom_call", output_to_operand_aliasing={{0}: (10, {})} | custom-call | tf_op jit(solution)/shard_map/encode/pallas_call | solution.py:263
  60.2 3.3 %collective-permute-start.14 = (f32[32,128]{1,0:T(8,128)S(1)}, f32[32,128]{1,0:T(8,128)S(1)}, u32[]{:S(2)}, u32[]{:S(2)}) collective-permute-start(f32[32,128]{1,0:T(8,128)S(1)} %get-tuple-element.43.refs_2_), channel_id=1, source_target_pairs={{0,64},{16,80},{32,96},{48,112},{64,0},{80,16},{96,32},{112,48},{1... | collective-permute-start | bytes 49160 | tf_op jit(solution)/shard_map/ppermute | solution.py:225
  63.5 1.7 %collective-permute-done.14 = f32[32,128]{1,0:T(8,128)S(1)} collective-permute-done((f32[32,128]{1,0:T(8,128)S(1)}, f32[32,128]{1,0:T(8,128)S(1)}, u32[]{:S(2)}, u32[]{:S(2)}) %collective-permute-start.14) | collective-permute-done | bytes 16416 | tf_op jit(solution)/shard_map/ppermute | solution.py:225
  65.2 5.0 %collective-permute-start.15 = (f32[2,32,128]{2,1,0:T(8,128)S(1)}, f32[2,32,128]{2,1,0:T(8,128)S(1)}, u32[]{:S(2)}, u32[]{:S(2)}) collective-permute-start(f32[2,32,128]{2,1,0:T(8,128)S(1)} %pad_maximum_fusion.refs_0_), channel_id=1, source_target_pairs={{0,192},{16,208},{32,224},{48,240},{64,128},{80,144},{96,160},{112... | collective-permute-start | bytes 98312 | tf_op jit(solution)/shard_map/ppermute | solution.py:227
  70.3 1.9 %collective-permute-done.15.refs_1_ = f32[2,32,128]{2,1,0:T(8,128)S(1)} collective-permute-done((f32[2,32,128]{2,1,0:T(8,128)S(1)}, f32[2,32,128]{2,1,0:T(8,128)S(1)}, u32[]{:S(2)}, u32[]{:S(2)}) %collective-permute-start.15) | collective-permute-done | bytes 32800 | tf_op jit(solution)/shard_map/ppermute | solution.py:227
  72.2 0.7 spread.1.refs_0_.refs_5_
  72.8 0.6 collective-permute-start.16
  73.4 2.4 %collective-permute-start.17 = (f32[8,16,128]{2,1,0:T(8,128)S(1)}, f32[8,16,128]{2,1,0:T(8,128)S(1)}, u32[]{:S(2)}, u32[]{:S(2)}) collective-permute-start(f32[8,16,128]{2,1,0:T(8,128)S(1)} %spread.1.refs_0_.refs_5_), channel_id=1, source_target_pairs={{0,32},{16,48},{32,0},{48,16},{64,96},{80,112},{96,64},{112,80},{1... | collective-permute-start | bytes 196616 | tf_op jit(solution)/shard_map/ppermute | solution.py:221
  75.8 0.0 collective-permute-start.18
  75.8 1.4 %collective-permute-done.16.refs_1_ = f32[8,16,128]{2,1,0:T(8,128)S(1)} collective-permute-done((f32[8,16,128]{2,1,0:T(8,128)S(1)}, f32[8,16,128]{2,1,0:T(8,128)S(1)}, u32[]{:S(2)}, u32[]{:S(2)}) %collective-permute-start.16) | collective-permute-done | bytes 65568 | tf_op jit(solution)/shard_map/ppermute | solution.py:221
  77.2 2.0 %collective-permute-done.17.refs_2_ = f32[8,16,128]{2,1,0:T(8,128)S(1)} collective-permute-done((f32[8,16,128]{2,1,0:T(8,128)S(1)}, f32[8,16,128]{2,1,0:T(8,128)S(1)}, u32[]{:S(2)}, u32[]{:S(2)}) %collective-permute-start.17) | collective-permute-done | bytes 65568 | tf_op jit(solution)/shard_map/ppermute | solution.py:221
  79.2 2.1 %collective-permute-done.18.refs_3_ = f32[8,16,128]{2,1,0:T(8,128)S(1)} collective-permute-done((f32[8,16,128]{2,1,0:T(8,128)S(1)}, f32[8,16,128]{2,1,0:T(8,128)S(1)}, u32[]{:S(2)}, u32[]{:S(2)}) %collective-permute-start.18) | collective-permute-done | bytes 65568 | tf_op jit(solution)/shard_map/ppermute | solution.py:221
  81.3 7.1 %decode.1 = f32[512,512]{1,0:T(8,128)} custom-call(s32[3]{0:T(128)S(1)} %pad_add_fusion.at_ref, f32[8,16,128]{2,1,0:T(8,128)S(1)} %spread.1.refs_0_.refs_5_, f32[8,16,128]{2,1,0:T(8,128)S(1)} %collective-permute-done.16.refs_1_, f32[8,16,128]{2,1,0:T(8,128)S(1)} %collective-permute-done.17.refs_2_, f32[8,16,128]{2,1,0:T(8,128)S(1)} %collective-permute-done.18.refs_3_, ...), custom_call_target="tpu_custom_call" | custom-call | tf_op jit(solution)/shard_map/decode/pallas_call | solution.py:263
  (9 shorter events, 0.0 us)
Async XLA Ops:
  0.7 3.4 %copy-start = (bf16[1,512,8192]{2,1,0:T(8,128)(2,1)S(1)}, bf16[1,512,8192]{2,1,0:T(8,128)(2,1)}, u32[]{:S(2)}) copy-start(bf16[1,512,8192]{2,1,0:T(8,128)(2,1)} %refs_2_.1) | copy-start | bytes 25165828
  5.2 4.2 %collective-permute-start.1 = (bf16[4,512,512]{2,1,0:T(8,128)(2,1)S(1)}, bf16[4,512,512]{2,1,0:T(8,128)(2,1)S(1)}, u32[]{:S(2)}, u32[]{:S(2)}) collective-permute-start(bf16[4,512,512]{2,1,0:T(8,128)(2,1)S(1)} %pack.2.refs_3_), channel_id=1, source_target_pairs={{0,1},{1,0},{2,3},{3,2},{4,5},{5,4},{6,7},{7,6},{8,9},{9,8},{10,11... | collective-permute-start | bytes 6291464 | tf_op jit(solution)/shard_map/ppermute | solution.py:240
  8.4 1.8 %copy-start.3 = (bf16[4,512,512]{2,1,0:T(8,128)(2,1)}, bf16[4,512,512]{2,1,0:T(8,128)(2,1)S(1)}, u32[]{:S(2)}) copy-start(bf16[4,512,512]{2,1,0:T(8,128)(2,1)S(1)} %get-tuple-element.25.refs_0_.refs_2_) | copy-start | bytes 6291460
  8.4 5.9 %collective-permute-start = (bf16[4,512,512]{2,1,0:T(8,128)(2,1)}, bf16[4,512,512]{2,1,0:T(8,128)(2,1)}, u32[]{:S(2)}, u32[]{:S(2)}) collective-permute-start(bf16[4,512,512]{2,1,0:T(8,128)(2,1)} %get-tuple-element.24), channel_id=1, source_target_pairs={{0,1},{1,0},{2,3},{3,2},{4,5},{5,4},{6,7},{7,6},{8,9},{9,8},{10,11... | collective-permute-start | bytes 6291464 | tf_op jit(solution)/shard_map/ppermute | solution.py:240
  9.4 1.4 %copy-start.1 = (bf16[4,512,512]{2,1,0:T(8,128)(2,1)}, bf16[4,512,512]{2,1,0:T(8,128)(2,1)S(1)}, u32[]{:S(2)}) copy-start(bf16[4,512,512]{2,1,0:T(8,128)(2,1)S(1)} %collective-permute-done.1.refs_1_.refs_3_) | copy-start | bytes 6291460
  9.4 4.6 %copy-start.7 = (s32[1,8,8,32]{3,2,1,0:T(8,128)S(1)}, s32[1,8,8,32]{3,2,1,0:T(8,128)}, u32[]{:S(2)}) copy-start(s32[1,8,8,32]{3,2,1,0:T(8,128)} %param.6) | copy-start | bytes 24580
  10.8 10.0 %collective-permute-start.3 = (s16[272,512]{1,0:T(8,128)(2,1)S(1)}, s16[272,512]{1,0:T(8,128)(2,1)S(1)}, u32[]{:S(2)}, u32[]{:S(2)}) collective-permute-start(s16[272,512]{1,0:T(8,128)(2,1)S(1)} %get-tuple-element.28), channel_id=1, source_target_pairs={{0,4},{1,5},{2,6},{3,7},{4,8},{5,9},{6,10},{7,11},{8,12},{9,13},{1... | collective-permute-start | bytes 835592 | tf_op jit(solution)/shard_map/ppermute | solution.py:240
  12.4 9.5 %collective-permute-start.4 = (s16[272,512]{1,0:T(8,128)(2,1)S(1)}, s16[272,512]{1,0:T(8,128)(2,1)S(1)}, u32[]{:S(2)}, u32[]{:S(2)}) collective-permute-start(s16[272,512]{1,0:T(8,128)(2,1)S(1)} %get-tuple-element.26.refs_2_), channel_id=1, source_target_pairs={{0,12},{1,13},{2,14},{3,15},{4,0},{5,1},{6,2},{7,3},{8,4},{9,5},{1... | collective-permute-start | bytes 835592 | tf_op jit(solution)/shard_map/ppermute | solution.py:240
  14.3 7.7 %copy-start.2 = (bf16[4,512,512]{2,1,0:T(8,128)(2,1)S(1)}, bf16[4,512,512]{2,1,0:T(8,128)(2,1)}, u32[]{:S(2)}) copy-start(bf16[4,512,512]{2,1,0:T(8,128)(2,1)} %copy-done.1) | copy-start | bytes 6291460
  14.3 7.7 %copy-start.4 = (bf16[4,512,512]{2,1,0:T(8,128)(2,1)S(1)}, bf16[4,512,512]{2,1,0:T(8,128)(2,1)}, u32[]{:S(2)}) copy-start(bf16[4,512,512]{2,1,0:T(8,128)(2,1)} %copy-done.3) | copy-start | bytes 6291460
  16.4 11.5 %collective-permute-start.2 = (s16[272,512]{1,0:T(8,128)(2,1)S(1)}, s16[272,512]{1,0:T(8,128)(2,1)S(1)}, u32[]{:S(2)}, u32[]{:S(2)}) collective-permute-start(s16[272,512]{1,0:T(8,128)(2,1)S(1)} %get-tuple-element.27.refs_6_), channel_id=1, source_target_pairs={{0,12},{1,13},{2,14},{3,15},{4,0},{5,1},{6,2},{7,3},{8,4},{9,5},{1... | collective-permute-start | bytes 835592 | tf_op jit(solution)/shard_map/ppermute | solution.py:240
  18.3 10.8 %copy-start.5 = (f32[512,512]{1,0:T(8,128)S(1)}, f32[512,512]{1,0:T(8,128)}, u32[]{:S(2)}) copy-start(f32[512,512]{1,0:T(8,128)} %refs_5_.1) | copy-start | bytes 3145732
  18.3 10.8 %copy-start.6 = (bf16[2,2,256,256]{3,2,1,0:T(8,128)(2,1)S(1)}, bf16[2,2,256,256]{3,2,1,0:T(8,128)(2,1)}, u32[]{:S(2)}) copy-start(bf16[2,2,256,256]{3,2,1,0:T(8,128)(2,1)} %constant.44.clone.refs_6_) | copy-start | bytes 1572868
  18.3 10.8 %collective-permute-start.7 = (s16[272,512]{1,0:T(8,128)(2,1)S(1)}, s16[272,512]{1,0:T(8,128)(2,1)S(1)}, u32[]{:S(2)}, u32[]{:S(2)}) collective-permute-start(s16[272,512]{1,0:T(8,128)(2,1)S(1)} %get-tuple-element.31), channel_id=1, source_target_pairs={{0,4},{1,5},{2,6},{3,7},{4,8},{5,9},{6,10},{7,11},{8,12},{9,13},{1... | collective-permute-start | bytes 835592 | tf_op jit(solution)/shard_map/ppermute | solution.py:240
  23.2 17.5 %collective-permute-start.5 = (s16[528,512]{1,0:T(8,128)(2,1)S(1)}, s16[528,512]{1,0:T(8,128)(2,1)S(1)}, u32[]{:S(2)}, u32[]{:S(2)}) collective-permute-start(s16[528,512]{1,0:T(8,128)(2,1)S(1)} %get-tuple-element.29), channel_id=1, source_target_pairs={{0,4},{1,5},{2,6},{3,7},{4,8},{5,9},{6,10},{7,11},{8,12},{9,13},{1... | collective-permute-start | bytes 1622024 | tf_op jit(solution)/shard_map/ppermute | solution.py:240
  24.8 15.9 %collective-permute-start.6 = (s16[528,512]{1,0:T(8,128)(2,1)S(1)}, s16[528,512]{1,0:T(8,128)(2,1)S(1)}, u32[]{:S(2)}, u32[]{:S(2)}) collective-permute-start(s16[528,512]{1,0:T(8,128)(2,1)S(1)} %get-tuple-element.30.refs_7_), channel_id=1, source_target_pairs={{0,12},{1,13},{2,14},{3,15},{4,0},{5,1},{6,2},{7,3},{8,4},{9,5},{1... | collective-permute-start | bytes 1622024 | tf_op jit(solution)/shard_map/ppermute | solution.py:240
  31.1 17.9 %collective-permute-start.11 = (s16[272,512]{1,0:T(8,128)(2,1)S(1)}, s16[272,512]{1,0:T(8,128)(2,1)S(1)}, u32[]{:S(2)}, u32[]{:S(2)}) collective-permute-start(s16[272,512]{1,0:T(8,128)(2,1)S(1)} %get-tuple-element.37), channel_id=1, source_target_pairs={{0,4},{1,5},{2,6},{3,7},{4,8},{5,9},{6,10},{7,11},{8,12},{9,13},{1... | collective-permute-start | bytes 835592 | tf_op jit(solution)/shard_map/ppermute | solution.py:240
  31.6 17.5 %collective-permute-start.12 = (s16[272,512]{1,0:T(8,128)(2,1)S(1)}, s16[272,512]{1,0:T(8,128)(2,1)S(1)}, u32[]{:S(2)}, u32[]{:S(2)}) collective-permute-start(s16[272,512]{1,0:T(8,128)(2,1)S(1)} %get-tuple-element.38), channel_id=1, source_target_pairs={{0,12},{1,13},{2,14},{3,15},{4,0},{5,1},{6,2},{7,3},{8,4},{9,5},{1... | collective-permute-start | bytes 835592 | tf_op jit(solution)/shard_map/ppermute | solution.py:240
  41.7 7.5 %collective-permute-start.13 = (s16[272,512]{1,0:T(8,128)(2,1)S(1)}, s16[272,512]{1,0:T(8,128)(2,1)S(1)}, u32[]{:S(2)}, u32[]{:S(2)}) collective-permute-start(s16[272,512]{1,0:T(8,128)(2,1)S(1)} %get-tuple-element.39), channel_id=1, source_target_pairs={{0,2},{1,3},{2,0},{3,1},{4,6},{5,7},{6,4},{7,5},{8,10},{9,11},{10,... | collective-permute-start | bytes 835592 | tf_op jit(solution)/shard_map/ppermute | solution.py:240
  45.6 8.4 %collective-permute-start.8 = (s16[272,512]{1,0:T(8,128)(2,1)S(1)}, s16[272,512]{1,0:T(8,128)(2,1)S(1)}, u32[]{:S(2)}, u32[]{:S(2)}) collective-permute-start(s16[272,512]{1,0:T(8,128)(2,1)S(1)} %get-tuple-element.34), channel_id=1, source_target_pairs={{0,4},{1,5},{2,6},{3,7},{4,8},{5,9},{6,10},{7,11},{8,12},{9,13},{1... | collective-permute-start | bytes 835592 | tf_op jit(solution)/shard_map/ppermute | solution.py:240
  46.3 7.7 %collective-permute-start.9 = (s16[272,512]{1,0:T(8,128)(2,1)S(1)}, s16[272,512]{1,0:T(8,128)(2,1)S(1)}, u32[]{:S(2)}, u32[]{:S(2)}) collective-permute-start(s16[272,512]{1,0:T(8,128)(2,1)S(1)} %get-tuple-element.35.refs_9_), channel_id=1, source_target_pairs={{0,12},{1,13},{2,14},{3,15},{4,0},{5,1},{6,2},{7,3},{8,4},{9,5},{1... | collective-permute-start | bytes 835592 | tf_op jit(solution)/shard_map/ppermute | solution.py:240
  49.0 6.5 %collective-permute-start.10 = (s16[272,512]{1,0:T(8,128)(2,1)S(1)}, s16[272,512]{1,0:T(8,128)(2,1)S(1)}, u32[]{:S(2)}, u32[]{:S(2)}) collective-permute-start(s16[272,512]{1,0:T(8,128)(2,1)S(1)} %get-tuple-element.33.refs_5_), channel_id=1, source_target_pairs={{0,2},{1,3},{2,0},{3,1},{4,6},{5,7},{6,4},{7,5},{8,10},{9,11},{10,... | collective-permute-start | bytes 835592 | tf_op jit(solution)/shard_map/ppermute | solution.py:240
  60.2 5.0 %collective-permute-start.14 = (f32[32,128]{1,0:T(8,128)S(1)}, f32[32,128]{1,0:T(8,128)S(1)}, u32[]{:S(2)}, u32[]{:S(2)}) collective-permute-start(f32[32,128]{1,0:T(8,128)S(1)} %get-tuple-element.43.refs_2_), channel_id=1, source_target_pairs={{0,64},{16,80},{32,96},{48,112},{64,0},{80,16},{96,32},{112,48},{1... | collective-permute-start | bytes 49160 | tf_op jit(solution)/shard_map/ppermute | solution.py:225
  65.2 6.9 %collective-permute-start.15 = (f32[2,32,128]{2,1,0:T(8,128)S(1)}, f32[2,32,128]{2,1,0:T(8,128)S(1)}, u32[]{:S(2)}, u32[]{:S(2)}) collective-permute-start(f32[2,32,128]{2,1,0:T(8,128)S(1)} %pad_maximum_fusion.refs_0_), channel_id=1, source_target_pairs={{0,192},{16,208},{32,224},{48,240},{64,128},{80,144},{96,160},{112... | collective-permute-start | bytes 98312 | tf_op jit(solution)/shard_map/ppermute | solution.py:227
  72.8 4.3 %collective-permute-start.16 = (f32[8,16,128]{2,1,0:T(8,128)S(1)}, f32[8,16,128]{2,1,0:T(8,128)S(1)}, u32[]{:S(2)}, u32[]{:S(2)}) collective-permute-start(f32[8,16,128]{2,1,0:T(8,128)S(1)} %spread.1.refs_0_.refs_5_), channel_id=1, source_target_pairs={{0,16},{16,32},{32,48},{48,0},{64,80},{80,96},{96,112},{112,64},{1... | collective-permute-start | bytes 196616 | tf_op jit(solution)/shard_map/ppermute | solution.py:221
  73.4 5.8 %collective-permute-start.17 = (f32[8,16,128]{2,1,0:T(8,128)S(1)}, f32[8,16,128]{2,1,0:T(8,128)S(1)}, u32[]{:S(2)}, u32[]{:S(2)}) collective-permute-start(f32[8,16,128]{2,1,0:T(8,128)S(1)} %spread.1.refs_0_.refs_5_), channel_id=1, source_target_pairs={{0,32},{16,48},{32,0},{48,16},{64,96},{80,112},{96,64},{112,80},{1... | collective-permute-start | bytes 196616 | tf_op jit(solution)/shard_map/ppermute | solution.py:221
  75.8 5.5 %collective-permute-start.18 = (f32[8,16,128]{2,1,0:T(8,128)S(1)}, f32[8,16,128]{2,1,0:T(8,128)S(1)}, u32[]{:S(2)}, u32[]{:S(2)}) collective-permute-start(f32[8,16,128]{2,1,0:T(8,128)S(1)} %spread.1.refs_0_.refs_5_), channel_id=1, source_target_pairs={{0,48},{16,0},{32,16},{48,32},{64,112},{80,64},{96,80},{112,96},{1... | collective-permute-start | bytes 196616 | tf_op jit(solution)/shard_map/ppermute | solution.py:221

commit v5 on v4

--- a/solution.py
+++ b/solution.py
@@ -9,6 +9,7 @@
 from jax.sharding import PartitionSpec as P
 
 GROUP = 64
+SHIFT = 6
 K = 32
 WIDE = 256
 KEPT = 128
@@ -83,6 +84,8 @@
 def encode(field, pos_ref, basis, fresh_ref, kept_ref):
     rows, cols = field.shape
     lane_block = lax.broadcasted_iota(jnp.int32, (1, KEPT), 1) // K
+    row = pos_ref[...] >> SHIFT
+    wide_col = (pos_ref[...] & (GROUP - 1)) + lane_block * GROUP
     for half in range(cols // WIDE):
         span = slice(half * WIDE, (half + 1) * WIDE)
         part = field[:, span]
@@ -91,9 +94,8 @@
         for a in range(rows // GROUP):
             g = a * (cols // WIDE) + half
             block = coef[a * GROUP:(a + 1) * GROUP]
-            pos = pos_ref[g:g + 1]
-            on_col = match(pos % GROUP + lane_block * GROUP, WIDE)
-            row_one = one(match(pos // GROUP, GROUP))
+            on_col = match(wide_col[g:g + 1], WIDE)
+            row_one = one(match(row[g:g + 1], GROUP))
             chosen = by_lanes(row_one, one(on_col))
             dense.append(jnp.where(chosen > 0.5, block, F32(0.0)))
             high, low = cut(block)
@@ -149,10 +151,12 @@
     put(down_ref, jnp.concatenate([down[:HALF], down[HALF:] + get(far_down)], axis=0))
 
 
-def near_top_kernel(at_ref, own_up, sib_up, own_down, sib_down, far_up, momentum, basis, up_ref, down_ref, decayed, held):
+def near_top_kernel(
+    at_ref, own_up, sib_up, own_down, sib_down, far_up, own, sib, momentum, basis, up_ref, down_ref, started, held
+):
     put(up_ref, wide(own_up, sib_up) + get(far_up))
     put(down_ref, wide(own_down, sib_down))
-    decayed[...] = DECAY * momentum[...]
+    started[...] = DECAY * momentum[...] + wide(own, sib)
     held[...] = basis[...]
 
 
@@ -167,9 +171,9 @@
     put(low_ref, x[HALF:])
 
 
-def encode_kernel(at_ref, own, sib, up_ref, down_ref, cross_ref, momentum_ref, pos_ref, basis_ref, *refs):
+def encode_kernel(at_ref, up_ref, down_ref, cross_ref, started_ref, pos_ref, basis_ref, *refs):
     *before, fresh_ref, kept_ref = refs
-    field = momentum_ref[...] + (wide(own, sib) + (get(up_ref) + get(down_ref)) + get(cross_ref))
+    field = started_ref[...] + (get(up_ref) + get(down_ref) + get(cross_ref))
     first = 0
     for ref in before:
         kept_ref[first:first + ref.shape[0]] = ref[...]
@@ -195,15 +199,21 @@
 def decode_kernel(at_ref, *refs):
     *sent, basis, out_ref = refs
     halves = out_ref.shape[1] // WIDE
+    parts = []
+    for q in range(WIDE // GROUP):
+        pos = jnp.concatenate([ref[2 * q] for ref in sent], axis=1).astype(jnp.int32)
+        val = jnp.concatenate([ref[2 * q + 1] for ref in sent], axis=1)
+        high = val.astype(BF).astype(F32)
+        parts.append((pos >> SHIFT, pos & (GROUP - 1), high, val - high))
     for half in range(halves):
         lines = []
         for g in range(half, sent[0].shape[1], halves):
             dense = []
-            for q in range(WIDE // GROUP):
-                pos = jnp.concatenate([ref[2 * q, g:g + 1] for ref in sent], axis=1).astype(jnp.int32)
-                val = jnp.concatenate([ref[2 * q + 1, g:g + 1] for ref in sent], axis=1)
-                high, low = cut(jnp.where(match(pos // GROUP, GROUP), val, F32(0.0)))
-                both = by_lanes(jnp.concatenate([high, low], axis=0), one(match(pos % GROUP, GROUP)))
+            for part in parts:
+                row, col, high, low = [x[g:g + 1] for x in part]
+                on_row = match(row, GROUP)
+                left = [jnp.where(on_row, x, F32(0.0)).astype(BF) for x in (high, low)]
+                both = by_lanes(jnp.concatenate(left, axis=0), one(match(col, GROUP)))
                 dense.append(both[:GROUP] + both[GROUP:])
             lines.append(jnp.concatenate(dense, axis=1))
         out_ref[:, half * WIDE:(half + 1) * WIDE] = inverse(jnp.concatenate(lines, axis=0), basis)
@@ -337,9 +347,9 @@
     across_near = round_y(call(
         near_kernel, "near", both(1, 1) + both(1, -1) + [whole(far[1][0]), whole(far[1][1])], [out(rows)] * 2))
     program.last += far[0]
-    *top, decayed, held = call(
+    *top, started, held = call(
         near_top_kernel, "near",
-        both(0, 1, HALF, 0) + both(0, -1, HALF, 0) + [whole(far[0][0]), whole(momentum), whole(basis)],
+        both(0, 1, HALF, 0) + both(0, -1, HALF, 0) + [whole(far[0][0])] + both(0, 0) + [whole(momentum), whole(basis)],
         [out(HALF)] * 2 + [like(momentum), like(basis)])
     near = [round_y(top)]
     crossing = call(
@@ -353,7 +363,7 @@
         half_spec = pl.BlockSpec((HALF, cols), lambda s, at, i=i: (i, 0))
         fresh, kept = call(
             encode_kernel, "encode",
-            [*both(0, 0, HALF, i), whole(near[i][0]), whole(near[i][1]), whole(crossed[i]), (decayed, half_spec),
+            [whole(near[i][0]), whole(near[i][1]), whole(crossed[i]), (started, half_spec),
              whole(poss[i]), whole(held), whole(kept)],
             [(jax.ShapeDtypeStruct((rows, cols), F32), half_spec),
              (jax.ShapeDtypeStruct((height, KEPT), F32), pl.BlockSpec((height, KEPT), lambda s, at: (0, 0)))],

time: 89.5 us -> 86.9 us (0.971); the launches traced: 88.4 us -> 86.7 us
  Pallas kernels: 30.5 us -> 28.2 us
    pallas_call x12, Pallas kernels: 30.5 us -> 28.2 us  [call(): pl.pallas_call(kernel, grid_spec=pltpu.PrefetchScalarGridSpec(num_scalar_...]
  transfers between devices with their start and end apart: 19 -> 19, of which waited for: 13 -> 14; matrix products, arithmetic and copies ran while one was open for 0% -> 0% of each run, Pallas kernels for 19% -> 19%
where the time goes in v5:
time: 86.9 us; the launch traced here: 86.7 us
  starting transfers between devices  29.3 us (34%)
  Pallas kernels  28.2 us (32%)
  waiting for transfers between devices  24.2 us (28%)
  local copies, waits for them, and re-layouts  4.22 us (5%)
    pallas_call x12, Pallas kernels, call(): pl.pallas_call(kernel, grid_spec=pltpu.PrefetchScalarGridSpec(num_scalar_...  28.2 us
    ppermute x14, starting transfers between devices, send(): return lax.ppermute(x, 'fsdp', places(shift_y, flip_z, flip_core))  18 us
    ppermute x14, waiting for transfers between devices, send(): return lax.ppermute(x, 'fsdp', places(shift_y, flip_z, flip_core))  15.1 us
    ppermute x3, waiting for transfers between devices, along_x(): lax.ppermute(own, 'rep', across(4, 4, 0, s))  5.47 us
    ppermute x1, starting transfers between devices, along_z(): lax.ppermute(two, 'rep', [(h * 4 + x, (3 - h) * 4 + x) for h in range(4)...  5.05 us
    unnamed x16, local copies, waits for them, and re-layouts  4 us
    ppermute x1, starting transfers between devices, along_z(): lax.ppermute(own, 'rep', [(h * 4 + x, (h ^ 1) * 4 + x) for h in range(4)...  3.27 us
    ppermute x3, starting transfers between devices, along_x(): lax.ppermute(own, 'rep', across(4, 4, 0, s))  2.97 us
  transfers between devices with their start and end apart: 19, of which 14 were waited for; matrix products, arithmetic and copies ran while one was open for 0% of the time, Pallas kernels for 19%

profile of v5, /device:TPU:6, one launch (start us, length us, event | category | flops | bytes accessed | tf_op | source)
XLA Modules:
  0.0 86.7 jit_solution(2590987332072559444)
XLA Ops:
  0.7 0.1 pad_add_fusion.at_ref
  0.7 0.0 copy-start
  0.7 3.4 %copy-done = bf16[1,512,8192]{2,1,0:T(8,128)(2,1)S(1)} copy-done((bf16[1,512,8192]{2,1,0:T(8,128)(2,1)S(1)}, bf16[1,512,8192]{2,1,0:T(8,128)(2,1)}, u32[]{:S(2)}) %copy-start) | copy-done | bytes 8388632
  4.1 1.1 %pack.2.refs_3_ = bf16[4,512,512]{2,1,0:T(8,128)(2,1)S(1)} custom-call(s32[3]{0:T(128)S(1)} %pad_add_fusion.at_ref, bf16[1,512,8192]{2,1,0:T(8,128)(2,1)S(1)} %copy-done), custom_call_target="tpu_custom_call" | custom-call | tf_op jit(solution)/shard_map/pack/pallas_call | solution.py:273
  5.2 0.1 collective-permute-start.1
  5.3 3.1 %pack.3 = (bf16[4,512,512]{2,1,0:T(8,128)(2,1)}, bf16[4,512,512]{2,1,0:T(8,128)(2,1)S(1)}, bf16[4,512,512]{2,1,0:T(8,128)(2,1)S(1)}) custom-call(s32[3]{0:T(128)S(1)} %pad_add_fusion.at_ref, bf16[1,512,8192]{2,1,0:T(8,128)(2,1)S(1)} %copy-done, bf16[1,512,8192]{2,1,0:T(8,128)(2,1)S(1)} %copy-done, bf16[1,512,8192]{2,1,0:T(8,128)(2,1)S(1)} %copy-done, ...), custom_call_target="tpu_custom_call" | custom-call | tf_op jit(solution)/shard_map/pack/pallas_call | solution.py:273
  8.4 0.0 copy-start.3
  8.4 0.5 collective-permute-start
  8.9 0.5 collective-permute-done.1.refs_1_.refs_3_
  9.4 0.8 far.2
  10.2 0.0 copy-done.3
  10.2 0.6 copy-done.1
  10.8 1.6 %collective-permute-start.3 = (s16[272,512]{1,0:T(8,128)(2,1)S(1)}, s16[272,512]{1,0:T(8,128)(2,1)S(1)}, u32[]{:S(2)}, u32[]{:S(2)}) collective-permute-start(s16[272,512]{1,0:T(8,128)(2,1)S(1)} %get-tuple-element.28), channel_id=1, source_target_pairs={{0,4},{1,5},{2,6},{3,7},{4,8},{5,9},{6,10},{7,11},{8,12},{9,13},{1... | collective-permute-start | bytes 835592 | tf_op jit(solution)/shard_map/ppermute | solution.py:250
  12.4 1.7 %collective-permute-start.4 = (s16[272,512]{1,0:T(8,128)(2,1)S(1)}, s16[272,512]{1,0:T(8,128)(2,1)S(1)}, u32[]{:S(2)}, u32[]{:S(2)}) collective-permute-start(s16[272,512]{1,0:T(8,128)(2,1)S(1)} %get-tuple-element.26.refs_2_), channel_id=1, source_target_pairs={{0,12},{1,13},{2,14},{3,15},{4,0},{5,1},{6,2},{7,3},{8,4},{9,5},{1... | collective-permute-start | bytes 835592 | tf_op jit(solution)/shard_map/ppermute | solution.py:250
  14.1 0.0 copy-done.7
  14.1 0.1 slice.13.refs_4_
  14.2 0.1 slice.15.refs_5_.refs_4_
  14.2 0.1 convert_element_type.6.refs_3_.refs_6_
  14.3 0.0 collective-permute-done.refs_1_.refs_3_.refs_6_
  14.3 2.1 %far.3 = (s16[272,512]{1,0:T(8,128)(2,1)S(1)}, s16[272,512]{1,0:T(8,128)(2,1)S(1)}) custom-call(s32[3]{0:T(128)S(1)} %pad_add_fusion.at_ref, bf16[4,512,512]{2,1,0:T(8,128)(2,1)S(1)} %get-tuple-element.23.refs_2_.refs_0_.refs_5_, bf16[4,512,512]{2,1,0:T(8,128)(2,1)} %collective-permute-done.refs_1_.refs_3_.refs_6_, ...), custom_call_target="tpu_custom_call" | custom-call | tf_op jit(solution)/shard_map/far/pallas_call | solution.py:273
  16.4 1.9 %collective-permute-start.2 = (s16[272,512]{1,0:T(8,128)(2,1)S(1)}, s16[272,512]{1,0:T(8,128)(2,1)S(1)}, u32[]{:S(2)}, u32[]{:S(2)}) collective-permute-start(s16[272,512]{1,0:T(8,128)(2,1)S(1)} %get-tuple-element.27.refs_6_), channel_id=1, source_target_pairs={{0,12},{1,13},{2,14},{3,15},{4,0},{5,1},{6,2},{7,3},{8,4},{9,5},{1... | collective-permute-start | bytes 835592 | tf_op jit(solution)/shard_map/ppermute | solution.py:250
  18.3 0.2 collective-permute-start.7
  18.5 2.3 %collective-permute-done.3.refs_4_ = s16[272,512]{1,0:T(8,128)(2,1)S(1)} collective-permute-done((s16[272,512]{1,0:T(8,128)(2,1)S(1)}, s16[272,512]{1,0:T(8,128)(2,1)S(1)}, u32[]{:S(2)}, u32[]{:S(2)}) %collective-permute-start.3) | collective-permute-done | bytes 278560 | tf_op jit(solution)/shard_map/ppermute | solution.py:250
  20.8 1.1 %collective-permute-done.4.refs_5_ = s16[272,512]{1,0:T(8,128)(2,1)S(1)} collective-permute-done((s16[272,512]{1,0:T(8,128)(2,1)S(1)}, s16[272,512]{1,0:T(8,128)(2,1)S(1)}, u32[]{:S(2)}, u32[]{:S(2)}) %collective-permute-start.4) | collective-permute-done | bytes 278560 | tf_op jit(solution)/shard_map/ppermute | solution.py:250
  22.0 0.0 copy-done.2
  22.0 0.0 copy-done.4
  22.0 1.2 %near.3 = (s16[528,512]{1,0:T(8,128)(2,1)S(1)}, s16[528,512]{1,0:T(8,128)(2,1)S(1)}) custom-call(s32[3]{0:T(128)S(1)} %pad_add_fusion.at_ref, bf16[4,512,512]{2,1,0:T(8,128)(2,1)S(1)} %copy-done.4, bf16[4,512,512]{2,1,0:T(8,128)(2,1)S(1)} %copy-done.2, bf16[4,512,512]{2,1,0:T(8,128)(2,1)S(1)} %copy-done.4, bf16[4,512,512]{2,1,0:T(8,128)(2,1)S(1)} %copy-done.2, ...), custom_call_target="tpu_custom_call" | custom-call | tf_op jit(solution)/shard_map/near/pallas_call | solution.py:273
  23.2 1.7 %collective-permute-start.5 = (s16[528,512]{1,0:T(8,128)(2,1)S(1)}, s16[528,512]{1,0:T(8,128)(2,1)S(1)}, u32[]{:S(2)}, u32[]{:S(2)}) collective-permute-start(s16[528,512]{1,0:T(8,128)(2,1)S(1)} %get-tuple-element.29), channel_id=1, source_target_pairs={{0,4},{1,5},{2,6},{3,7},{4,8},{5,9},{6,10},{7,11},{8,12},{9,13},{1... | collective-permute-start | bytes 1622024 | tf_op jit(solution)/shard_map/ppermute | solution.py:250
  24.8 1.7 %collective-permute-start.6 = (s16[528,512]{1,0:T(8,128)(2,1)S(1)}, s16[528,512]{1,0:T(8,128)(2,1)S(1)}, u32[]{:S(2)}, u32[]{:S(2)}) collective-permute-start(s16[528,512]{1,0:T(8,128)(2,1)S(1)} %get-tuple-element.30.refs_9_), channel_id=1, source_target_pairs={{0,12},{1,13},{2,14},{3,15},{4,0},{5,1},{6,2},{7,3},{8,4},{9,5},{1... | collective-permute-start | bytes 1622024 | tf_op jit(solution)/shard_map/ppermute | solution.py:250
  26.5 1.5 %collective-permute-done.2.refs_11_.refs_4_ = s16[272,512]{1,0:T(8,128)(2,1)S(1)} collective-permute-done((s16[272,512]{1,0:T(8,128)(2,1)S(1)}, s16[272,512]{1,0:T(8,128)(2,1)S(1)}, u32[]{:S(2)}, u32[]{:S(2)}) %collective-permute-start.2) | collective-permute-done | bytes 278560 | tf_op jit(solution)/shard_map/ppermute | solution.py:250
  27.9 1.2 %collective-permute-done.7.refs_4_.refs_10_ = s16[272,512]{1,0:T(8,128)(2,1)S(1)} collective-permute-done((s16[272,512]{1,0:T(8,128)(2,1)S(1)}, s16[272,512]{1,0:T(8,128)(2,1)S(1)}, u32[]{:S(2)}, u32[]{:S(2)}) %collective-permute-start.7) | collective-permute-done | bytes 278560 | tf_op jit(solution)/shard_map/ppermute | solution.py:250
  29.1 0.0 copy-done.5
  29.1 0.0 copy-done.6
  29.1 2.5 %near.4 = (s16[272,512]{1,0:T(8,128)(2,1)S(1)}, s16[272,512]{1,0:T(8,128)(2,1)S(1)}, f32[512,512]{1,0:T(8,128)S(1)}, bf16[2,2,256,256]{3,2,1,0:T(8,128)(2,1)S(1)}) custom-call(s32[3]{0:T(128)S(1)} %pad_add_fusion.at_ref, bf16[4,512,512]{2,1,0:T(8,128)(2,1)S(1)} %get-tuple-element.23.refs_2_.refs_0_.refs_5_, ...), custom_call_target="tpu_custom_call" | custom-call | tf_op jit(solution)/shard_map/near/pallas_call | solution.py:273
  31.5 0.5 collective-permute-start.11
  32.1 2.8 %collective-permute-start.12 = (s16[272,512]{1,0:T(8,128)(2,1)S(1)}, s16[272,512]{1,0:T(8,128)(2,1)S(1)}, u32[]{:S(2)}, u32[]{:S(2)}) collective-permute-start(s16[272,512]{1,0:T(8,128)(2,1)S(1)} %get-tuple-element.38), channel_id=1, source_target_pairs={{0,12},{1,13},{2,14},{3,15},{4,0},{5,1},{6,2},{7,3},{8,4},{9,5},{1... | collective-permute-start | bytes 835592 | tf_op jit(solution)/shard_map/ppermute | solution.py:250
  34.9 5.8 %collective-permute-done.5.refs_2_ = s16[528,512]{1,0:T(8,128)(2,1)S(1)} collective-permute-done((s16[528,512]{1,0:T(8,128)(2,1)S(1)}, s16[528,512]{1,0:T(8,128)(2,1)S(1)}, u32[]{:S(2)}, u32[]{:S(2)}) %collective-permute-start.5) | collective-permute-done | bytes 540704 | tf_op jit(solution)/shard_map/ppermute | solution.py:250
  40.7 0.0 collective-permute-done.6.refs_3_
  40.7 1.1 %cross.1 = (s16[272,512]{1,0:T(8,128)(2,1)S(1)}, s16[272,512]{1,0:T(8,128)(2,1)S(1)}) custom-call(s32[3]{0:T(128)S(1)} %pad_add_fusion.at_ref, bf16[4,512,512]{2,1,0:T(8,128)(2,1)S(1)} %copy-done.4, bf16[4,512,512]{2,1,0:T(8,128)(2,1)S(1)} %copy-done.2, s16[528,512]{1,0:T(8,128)(2,1)S(1)} %collective-permute-done.5.refs_2_, ...), custom_call_target="tpu_custom_call" | custom-call | tf_op jit(solution)/shard_map/cross/pallas_call | solution.py:273
  41.7 2.0 %collective-permute-start.13 = (s16[272,512]{1,0:T(8,128)(2,1)S(1)}, s16[272,512]{1,0:T(8,128)(2,1)S(1)}, u32[]{:S(2)}, u32[]{:S(2)}) collective-permute-start(s16[272,512]{1,0:T(8,128)(2,1)S(1)} %get-tuple-element.39), channel_id=1, source_target_pairs={{0,2},{1,3},{2,0},{3,1},{4,6},{5,7},{6,4},{7,5},{8,10},{9,11},{10,... | collective-permute-start | bytes 835592 | tf_op jit(solution)/shard_map/ppermute | solution.py:250
  43.7 1.9 %near.5 = (s16[272,512]{1,0:T(8,128)(2,1)S(1)}, s16[272,512]{1,0:T(8,128)(2,1)S(1)}) custom-call(s32[3]{0:T(128)S(1)} %pad_add_fusion.at_ref, bf16[4,512,512]{2,1,0:T(8,128)(2,1)S(1)} %get-tuple-element.23.refs_2_.refs_0_.refs_5_, bf16[4,512,512]{2,1,0:T(8,128)(2,1)} %collective-permute-done.refs_1_.refs_3_.refs_6_, ...), custom_call_target="tpu_custom_call" | custom-call | tf_op jit(solution)/shard_map/near/pallas_call | solution.py:273
  45.6 0.7 collective-permute-start.8
  46.3 2.6 %collective-permute-start.9 = (s16[272,512]{1,0:T(8,128)(2,1)S(1)}, s16[272,512]{1,0:T(8,128)(2,1)S(1)}, u32[]{:S(2)}, u32[]{:S(2)}) collective-permute-start(s16[272,512]{1,0:T(8,128)(2,1)S(1)} %get-tuple-element.35.refs_7_), channel_id=1, source_target_pairs={{0,12},{1,13},{2,14},{3,15},{4,0},{5,1},{6,2},{7,3},{8,4},{9,5},{1... | collective-permute-start | bytes 835592 | tf_op jit(solution)/shard_map/ppermute | solution.py:250
  49.0 0.0 collective-permute-done.11.refs_0_
  49.0 0.1 collective-permute-start.10
  49.1 0.0 collective-permute-done.12.refs_1_
  49.1 0.2 collective-permute-done.13.refs_2_
  49.3 3.7 %encode.2 = (f32[512,512]{1,0:T(8,128)}, f32[24,128]{1,0:T(8,128)S(1)}) custom-call(s32[3]{0:T(128)S(1)} %pad_add_fusion.at_ref, s16[272,512]{1,0:T(8,128)(2,1)S(1)} %collective-permute-done.11.refs_0_, s16[272,512]{1,0:T(8,128)(2,1)S(1)} %collective-permute-done.12.refs_1_, s16[272,512]{1,0:T(8,128)(2,1)S(1)} %collective-permute-done.13.refs_2_, ...), custom_call_target="tpu_custom_call" | custom-call | tf_op jit(solution)/shard_map/encode/pallas_call | solution.py:273
  53.0 0.5 collective-permute-done.8.refs_0_
  53.5 0.0 collective-permute-done.9.refs_1_
  53.5 2.0 %collective-permute-done.10.refs_2_ = s16[272,512]{1,0:T(8,128)(2,1)S(1)} collective-permute-done((s16[272,512]{1,0:T(8,128)(2,1)S(1)}, s16[272,512]{1,0:T(8,128)(2,1)S(1)}, u32[]{:S(2)}, u32[]{:S(2)}) %collective-permute-start.10) | collective-permute-done | bytes 278560 | tf_op jit(solution)/shard_map/ppermute | solution.py:250
  55.5 3.7 %encode.3 = (f32[512,512]{1,0:T(8,128)}, f32[32,128]{1,0:T(8,128)S(1)}) custom-call(s32[3]{0:T(128)S(1)} %pad_add_fusion.at_ref, s16[272,512]{1,0:T(8,128)(2,1)S(1)} %collective-permute-done.8.refs_0_, s16[272,512]{1,0:T(8,128)(2,1)S(1)} %collective-permute-done.9.refs_1_, ...), custom_call_target="tpu_custom_call", output_to_operand_aliasing={{0}: (8, {})} | custom-call | tf_op jit(solution)/shard_map/encode/pallas_call | solution.py:273
  59.2 3.3 %collective-permute-start.14 = (f32[32,128]{1,0:T(8,128)S(1)}, f32[32,128]{1,0:T(8,128)S(1)}, u32[]{:S(2)}, u32[]{:S(2)}) collective-permute-start(f32[32,128]{1,0:T(8,128)S(1)} %get-tuple-element.43.refs_2_), channel_id=1, source_target_pairs={{0,64},{16,80},{32,96},{48,112},{64,0},{80,16},{96,32},{112,48},{1... | collective-permute-start | bytes 49160 | tf_op jit(solution)/shard_map/ppermute | solution.py:235
  62.5 1.7 %collective-permute-done.14 = f32[32,128]{1,0:T(8,128)S(1)} collective-permute-done((f32[32,128]{1,0:T(8,128)S(1)}, f32[32,128]{1,0:T(8,128)S(1)}, u32[]{:S(2)}, u32[]{:S(2)}) %collective-permute-start.14) | collective-permute-done | bytes 16416 | tf_op jit(solution)/shard_map/ppermute | solution.py:235
  64.2 5.1 %collective-permute-start.15 = (f32[2,32,128]{2,1,0:T(8,128)S(1)}, f32[2,32,128]{2,1,0:T(8,128)S(1)}, u32[]{:S(2)}, u32[]{:S(2)}) collective-permute-start(f32[2,32,128]{2,1,0:T(8,128)S(1)} %pad_maximum_fusion.refs_0_), channel_id=1, source_target_pairs={{0,192},{16,208},{32,224},{48,240},{64,128},{80,144},{96,160},{112... | collective-permute-start | bytes 98312 | tf_op jit(solution)/shard_map/ppermute | solution.py:237
  69.3 1.9 %collective-permute-done.15.refs_1_ = f32[2,32,128]{2,1,0:T(8,128)S(1)} collective-permute-done((f32[2,32,128]{2,1,0:T(8,128)S(1)}, f32[2,32,128]{2,1,0:T(8,128)S(1)}, u32[]{:S(2)}, u32[]{:S(2)}) %collective-permute-start.15) | collective-permute-done | bytes 32800 | tf_op jit(solution)/shard_map/ppermute | solution.py:237
  71.1 0.7 spread.1.refs_0_.refs_5_
  71.8 0.6 collective-permute-start.16
  72.4 2.4 %collective-permute-start.17 = (f32[8,16,128]{2,1,0:T(8,128)S(1)}, f32[8,16,128]{2,1,0:T(8,128)S(1)}, u32[]{:S(2)}, u32[]{:S(2)}) collective-permute-start(f32[8,16,128]{2,1,0:T(8,128)S(1)} %spread.1.refs_0_.refs_5_), channel_id=1, source_target_pairs={{0,32},{16,48},{32,0},{48,16},{64,96},{80,112},{96,64},{112,80},{1... | collective-permute-start | bytes 196616 | tf_op jit(solution)/shard_map/ppermute | solution.py:231
  74.8 0.0 collective-permute-start.18
  74.8 1.4 %collective-permute-done.16.refs_1_ = f32[8,16,128]{2,1,0:T(8,128)S(1)} collective-permute-done((f32[8,16,128]{2,1,0:T(8,128)S(1)}, f32[8,16,128]{2,1,0:T(8,128)S(1)}, u32[]{:S(2)}, u32[]{:S(2)}) %collective-permute-start.16) | collective-permute-done | bytes 65568 | tf_op jit(solution)/shard_map/ppermute | solution.py:231
  76.2 2.0 %collective-permute-done.17.refs_2_ = f32[8,16,128]{2,1,0:T(8,128)S(1)} collective-permute-done((f32[8,16,128]{2,1,0:T(8,128)S(1)}, f32[8,16,128]{2,1,0:T(8,128)S(1)}, u32[]{:S(2)}, u32[]{:S(2)}) %collective-permute-start.17) | collective-permute-done | bytes 65568 | tf_op jit(solution)/shard_map/ppermute | solution.py:231
  78.1 2.1 %collective-permute-done.18.refs_3_ = f32[8,16,128]{2,1,0:T(8,128)S(1)} collective-permute-done((f32[8,16,128]{2,1,0:T(8,128)S(1)}, f32[8,16,128]{2,1,0:T(8,128)S(1)}, u32[]{:S(2)}, u32[]{:S(2)}) %collective-permute-start.18) | collective-permute-done | bytes 65568 | tf_op jit(solution)/shard_map/ppermute | solution.py:231
  80.3 6.5 %decode.1 = f32[512,512]{1,0:T(8,128)} custom-call(s32[3]{0:T(128)S(1)} %pad_add_fusion.at_ref, f32[8,16,128]{2,1,0:T(8,128)S(1)} %spread.1.refs_0_.refs_5_, f32[8,16,128]{2,1,0:T(8,128)S(1)} %collective-permute-done.16.refs_1_, f32[8,16,128]{2,1,0:T(8,128)S(1)} %collective-permute-done.17.refs_2_, f32[8,16,128]{2,1,0:T(8,128)S(1)} %collective-permute-done.18.refs_3_, ...), custom_call_target="tpu_custom_call" | custom-call | tf_op jit(solution)/shard_map/decode/pallas_call | solution.py:273
  (9 shorter events, 0.0 us)
Async XLA Ops:
  0.7 3.4 %copy-start = (bf16[1,512,8192]{2,1,0:T(8,128)(2,1)S(1)}, bf16[1,512,8192]{2,1,0:T(8,128)(2,1)}, u32[]{:S(2)}) copy-start(bf16[1,512,8192]{2,1,0:T(8,128)(2,1)} %refs_2_.1) | copy-start | bytes 25165828
  5.2 4.2 %collective-permute-start.1 = (bf16[4,512,512]{2,1,0:T(8,128)(2,1)S(1)}, bf16[4,512,512]{2,1,0:T(8,128)(2,1)S(1)}, u32[]{:S(2)}, u32[]{:S(2)}) collective-permute-start(bf16[4,512,512]{2,1,0:T(8,128)(2,1)S(1)} %pack.2.refs_3_), channel_id=1, source_target_pairs={{0,1},{1,0},{2,3},{3,2},{4,5},{5,4},{6,7},{7,6},{8,9},{9,8},{10,11... | collective-permute-start | bytes 6291464 | tf_op jit(solution)/shard_map/ppermute | solution.py:250
  8.4 1.8 %copy-start.3 = (bf16[4,512,512]{2,1,0:T(8,128)(2,1)}, bf16[4,512,512]{2,1,0:T(8,128)(2,1)S(1)}, u32[]{:S(2)}) copy-start(bf16[4,512,512]{2,1,0:T(8,128)(2,1)S(1)} %get-tuple-element.25.refs_0_.refs_2_) | copy-start | bytes 6291460
  8.4 5.9 %collective-permute-start = (bf16[4,512,512]{2,1,0:T(8,128)(2,1)}, bf16[4,512,512]{2,1,0:T(8,128)(2,1)}, u32[]{:S(2)}, u32[]{:S(2)}) collective-permute-start(bf16[4,512,512]{2,1,0:T(8,128)(2,1)} %get-tuple-element.24), channel_id=1, source_target_pairs={{0,1},{1,0},{2,3},{3,2},{4,5},{5,4},{6,7},{7,6},{8,9},{9,8},{10,11... | collective-permute-start | bytes 6291464 | tf_op jit(solution)/shard_map/ppermute | solution.py:250
  9.4 1.4 %copy-start.1 = (bf16[4,512,512]{2,1,0:T(8,128)(2,1)}, bf16[4,512,512]{2,1,0:T(8,128)(2,1)S(1)}, u32[]{:S(2)}) copy-start(bf16[4,512,512]{2,1,0:T(8,128)(2,1)S(1)} %collective-permute-done.1.refs_1_.refs_3_) | copy-start | bytes 6291460
  9.4 4.6 %copy-start.7 = (s32[1,8,8,32]{3,2,1,0:T(8,128)S(1)}, s32[1,8,8,32]{3,2,1,0:T(8,128)}, u32[]{:S(2)}) copy-start(s32[1,8,8,32]{3,2,1,0:T(8,128)} %param.6) | copy-start | bytes 24580
  10.8 10.0 %collective-permute-start.3 = (s16[272,512]{1,0:T(8,128)(2,1)S(1)}, s16[272,512]{1,0:T(8,128)(2,1)S(1)}, u32[]{:S(2)}, u32[]{:S(2)}) collective-permute-start(s16[272,512]{1,0:T(8,128)(2,1)S(1)} %get-tuple-element.28), channel_id=1, source_target_pairs={{0,4},{1,5},{2,6},{3,7},{4,8},{5,9},{6,10},{7,11},{8,12},{9,13},{1... | collective-permute-start | bytes 835592 | tf_op jit(solution)/shard_map/ppermute | solution.py:250
  12.4 9.5 %collective-permute-start.4 = (s16[272,512]{1,0:T(8,128)(2,1)S(1)}, s16[272,512]{1,0:T(8,128)(2,1)S(1)}, u32[]{:S(2)}, u32[]{:S(2)}) collective-permute-start(s16[272,512]{1,0:T(8,128)(2,1)S(1)} %get-tuple-element.26.refs_2_), channel_id=1, source_target_pairs={{0,12},{1,13},{2,14},{3,15},{4,0},{5,1},{6,2},{7,3},{8,4},{9,5},{1... | collective-permute-start | bytes 835592 | tf_op jit(solution)/shard_map/ppermute | solution.py:250
  14.3 7.7 %copy-start.2 = (bf16[4,512,512]{2,1,0:T(8,128)(2,1)S(1)}, bf16[4,512,512]{2,1,0:T(8,128)(2,1)}, u32[]{:S(2)}) copy-start(bf16[4,512,512]{2,1,0:T(8,128)(2,1)} %copy-done.1) | copy-start | bytes 6291460
  14.3 7.7 %copy-start.4 = (bf16[4,512,512]{2,1,0:T(8,128)(2,1)S(1)}, bf16[4,512,512]{2,1,0:T(8,128)(2,1)}, u32[]{:S(2)}) copy-start(bf16[4,512,512]{2,1,0:T(8,128)(2,1)} %copy-done.3) | copy-start | bytes 6291460
  16.4 11.5 %collective-permute-start.2 = (s16[272,512]{1,0:T(8,128)(2,1)S(1)}, s16[272,512]{1,0:T(8,128)(2,1)S(1)}, u32[]{:S(2)}, u32[]{:S(2)}) collective-permute-start(s16[272,512]{1,0:T(8,128)(2,1)S(1)} %get-tuple-element.27.refs_6_), channel_id=1, source_target_pairs={{0,12},{1,13},{2,14},{3,15},{4,0},{5,1},{6,2},{7,3},{8,4},{9,5},{1... | collective-permute-start | bytes 835592 | tf_op jit(solution)/shard_map/ppermute | solution.py:250
  18.3 10.8 %copy-start.5 = (f32[512,512]{1,0:T(8,128)S(1)}, f32[512,512]{1,0:T(8,128)}, u32[]{:S(2)}) copy-start(f32[512,512]{1,0:T(8,128)} %refs_7_.1) | copy-start | bytes 3145732
  18.3 10.8 %copy-start.6 = (bf16[2,2,256,256]{3,2,1,0:T(8,128)(2,1)S(1)}, bf16[2,2,256,256]{3,2,1,0:T(8,128)(2,1)}, u32[]{:S(2)}) copy-start(bf16[2,2,256,256]{3,2,1,0:T(8,128)(2,1)} %constant.44.clone.refs_8_) | copy-start | bytes 1572868
  18.3 10.8 %collective-permute-start.7 = (s16[272,512]{1,0:T(8,128)(2,1)S(1)}, s16[272,512]{1,0:T(8,128)(2,1)S(1)}, u32[]{:S(2)}, u32[]{:S(2)}) collective-permute-start(s16[272,512]{1,0:T(8,128)(2,1)S(1)} %get-tuple-element.31), channel_id=1, source_target_pairs={{0,4},{1,5},{2,6},{3,7},{4,8},{5,9},{6,10},{7,11},{8,12},{9,13},{1... | collective-permute-start | bytes 835592 | tf_op jit(solution)/shard_map/ppermute | solution.py:250
  23.2 17.5 %collective-permute-start.5 = (s16[528,512]{1,0:T(8,128)(2,1)S(1)}, s16[528,512]{1,0:T(8,128)(2,1)S(1)}, u32[]{:S(2)}, u32[]{:S(2)}) collective-permute-start(s16[528,512]{1,0:T(8,128)(2,1)S(1)} %get-tuple-element.29), channel_id=1, source_target_pairs={{0,4},{1,5},{2,6},{3,7},{4,8},{5,9},{6,10},{7,11},{8,12},{9,13},{1... | collective-permute-start | bytes 1622024 | tf_op jit(solution)/shard_map/ppermute | solution.py:250
  24.8 15.9 %collective-permute-start.6 = (s16[528,512]{1,0:T(8,128)(2,1)S(1)}, s16[528,512]{1,0:T(8,128)(2,1)S(1)}, u32[]{:S(2)}, u32[]{:S(2)}) collective-permute-start(s16[528,512]{1,0:T(8,128)(2,1)S(1)} %get-tuple-element.30.refs_9_), channel_id=1, source_target_pairs={{0,12},{1,13},{2,14},{3,15},{4,0},{5,1},{6,2},{7,3},{8,4},{9,5},{1... | collective-permute-start | bytes 1622024 | tf_op jit(solution)/shard_map/ppermute | solution.py:250
  31.5 17.4 %collective-permute-start.11 = (s16[272,512]{1,0:T(8,128)(2,1)S(1)}, s16[272,512]{1,0:T(8,128)(2,1)S(1)}, u32[]{:S(2)}, u32[]{:S(2)}) collective-permute-start(s16[272,512]{1,0:T(8,128)(2,1)S(1)} %get-tuple-element.37), channel_id=1, source_target_pairs={{0,4},{1,5},{2,6},{3,7},{4,8},{5,9},{6,10},{7,11},{8,12},{9,13},{1... | collective-permute-start | bytes 835592 | tf_op jit(solution)/shard_map/ppermute | solution.py:250
  32.1 17.0 %collective-permute-start.12 = (s16[272,512]{1,0:T(8,128)(2,1)S(1)}, s16[272,512]{1,0:T(8,128)(2,1)S(1)}, u32[]{:S(2)}, u32[]{:S(2)}) collective-permute-start(s16[272,512]{1,0:T(8,128)(2,1)S(1)} %get-tuple-element.38), channel_id=1, source_target_pairs={{0,12},{1,13},{2,14},{3,15},{4,0},{5,1},{6,2},{7,3},{8,4},{9,5},{1... | collective-permute-start | bytes 835592 | tf_op jit(solution)/shard_map/ppermute | solution.py:250
  41.7 7.5 %collective-permute-start.13 = (s16[272,512]{1,0:T(8,128)(2,1)S(1)}, s16[272,512]{1,0:T(8,128)(2,1)S(1)}, u32[]{:S(2)}, u32[]{:S(2)}) collective-permute-start(s16[272,512]{1,0:T(8,128)(2,1)S(1)} %get-tuple-element.39), channel_id=1, source_target_pairs={{0,2},{1,3},{2,0},{3,1},{4,6},{5,7},{6,4},{7,5},{8,10},{9,11},{10,... | collective-permute-start | bytes 835592 | tf_op jit(solution)/shard_map/ppermute | solution.py:250
  45.6 7.8 %collective-permute-start.8 = (s16[272,512]{1,0:T(8,128)(2,1)S(1)}, s16[272,512]{1,0:T(8,128)(2,1)S(1)}, u32[]{:S(2)}, u32[]{:S(2)}) collective-permute-start(s16[272,512]{1,0:T(8,128)(2,1)S(1)} %get-tuple-element.34), channel_id=1, source_target_pairs={{0,4},{1,5},{2,6},{3,7},{4,8},{5,9},{6,10},{7,11},{8,12},{9,13},{1... | collective-permute-start | bytes 835592 | tf_op jit(solution)/shard_map/ppermute | solution.py:250
  46.3 7.1 %collective-permute-start.9 = (s16[272,512]{1,0:T(8,128)(2,1)S(1)}, s16[272,512]{1,0:T(8,128)(2,1)S(1)}, u32[]{:S(2)}, u32[]{:S(2)}) collective-permute-start(s16[272,512]{1,0:T(8,128)(2,1)S(1)} %get-tuple-element.35.refs_7_), channel_id=1, source_target_pairs={{0,12},{1,13},{2,14},{3,15},{4,0},{5,1},{6,2},{7,3},{8,4},{9,5},{1... | collective-permute-start | bytes 835592 | tf_op jit(solution)/shard_map/ppermute | solution.py:250
  49.0 6.5 %collective-permute-start.10 = (s16[272,512]{1,0:T(8,128)(2,1)S(1)}, s16[272,512]{1,0:T(8,128)(2,1)S(1)}, u32[]{:S(2)}, u32[]{:S(2)}) collective-permute-start(s16[272,512]{1,0:T(8,128)(2,1)S(1)} %get-tuple-element.33.refs_5_), channel_id=1, source_target_pairs={{0,2},{1,3},{2,0},{3,1},{4,6},{5,7},{6,4},{7,5},{8,10},{9,11},{10,... | collective-permute-start | bytes 835592 | tf_op jit(solution)/shard_map/ppermute | solution.py:250
  59.2 5.0 %collective-permute-start.14 = (f32[32,128]{1,0:T(8,128)S(1)}, f32[32,128]{1,0:T(8,128)S(1)}, u32[]{:S(2)}, u32[]{:S(2)}) collective-permute-start(f32[32,128]{1,0:T(8,128)S(1)} %get-tuple-element.43.refs_2_), channel_id=1, source_target_pairs={{0,64},{16,80},{32,96},{48,112},{64,0},{80,16},{96,32},{112,48},{1... | collective-permute-start | bytes 49160 | tf_op jit(solution)/shard_map/ppermute | solution.py:235
  64.2 6.9 %collective-permute-start.15 = (f32[2,32,128]{2,1,0:T(8,128)S(1)}, f32[2,32,128]{2,1,0:T(8,128)S(1)}, u32[]{:S(2)}, u32[]{:S(2)}) collective-permute-start(f32[2,32,128]{2,1,0:T(8,128)S(1)} %pad_maximum_fusion.refs_0_), channel_id=1, source_target_pairs={{0,192},{16,208},{32,224},{48,240},{64,128},{80,144},{96,160},{112... | collective-permute-start | bytes 98312 | tf_op jit(solution)/shard_map/ppermute | solution.py:237
  71.8 4.3 %collective-permute-start.16 = (f32[8,16,128]{2,1,0:T(8,128)S(1)}, f32[8,16,128]{2,1,0:T(8,128)S(1)}, u32[]{:S(2)}, u32[]{:S(2)}) collective-permute-start(f32[8,16,128]{2,1,0:T(8,128)S(1)} %spread.1.refs_0_.refs_5_), channel_id=1, source_target_pairs={{0,16},{16,32},{32,48},{48,0},{64,80},{80,96},{96,112},{112,64},{1... | collective-permute-start | bytes 196616 | tf_op jit(solution)/shard_map/ppermute | solution.py:231
  72.4 5.8 %collective-permute-start.17 = (f32[8,16,128]{2,1,0:T(8,128)S(1)}, f32[8,16,128]{2,1,0:T(8,128)S(1)}, u32[]{:S(2)}, u32[]{:S(2)}) collective-permute-start(f32[8,16,128]{2,1,0:T(8,128)S(1)} %spread.1.refs_0_.refs_5_), channel_id=1, source_target_pairs={{0,32},{16,48},{32,0},{48,16},{64,96},{80,112},{96,64},{112,80},{1... | collective-permute-start | bytes 196616 | tf_op jit(solution)/shard_map/ppermute | solution.py:231
  74.8 5.5 %collective-permute-start.18 = (f32[8,16,128]{2,1,0:T(8,128)S(1)}, f32[8,16,128]{2,1,0:T(8,128)S(1)}, u32[]{:S(2)}, u32[]{:S(2)}) collective-permute-start(f32[8,16,128]{2,1,0:T(8,128)S(1)} %spread.1.refs_0_.refs_5_), channel_id=1, source_target_pairs={{0,48},{16,0},{32,16},{48,32},{64,112},{80,64},{96,80},{112,96},{1... | collective-permute-start | bytes 196616 | tf_op jit(solution)/shard_map/ppermute | solution.py:231

commit v6 on v5

--- a/solution.py
+++ b/solution.py
@@ -296,7 +296,7 @@
 VMEM = 10 * 1024 * 1024
 
 
-STEP = 256
+STEP = 512
 
 
 def local(partial_grads, momentum, freq_index):

time: 86.9 us -> 86.3 us (level)
  no operation moved by 1% of the time
where the time goes in v6:
time: 86.3 us; the launch traced here: 86.1 us
  starting transfers between devices  29.3 us (34%)
  Pallas kernels  27.5 us (32%)
  waiting for transfers between devices  24.2 us (28%)
  local copies, waits for them, and re-layouts  4.22 us (5%)
    pallas_call x12, Pallas kernels, call(): pl.pallas_call(kernel, grid_spec=pltpu.PrefetchScalarGridSpec(num_scalar_...  27.5 us
    ppermute x14, starting transfers between devices, send(): return lax.ppermute(x, 'fsdp', places(shift_y, flip_z, flip_core))  18 us
    ppermute x14, waiting for transfers between devices, send(): return lax.ppermute(x, 'fsdp', places(shift_y, flip_z, flip_core))  15.1 us
    ppermute x3, waiting for transfers between devices, along_x(): lax.ppermute(own, 'rep', across(4, 4, 0, s))  5.47 us
    ppermute x1, starting transfers between devices, along_z(): lax.ppermute(two, 'rep', [(h * 4 + x, (3 - h) * 4 + x) for h in range(4)...  5.05 us
    unnamed x16, local copies, waits for them, and re-layouts  4 us
    ppermute x1, starting transfers between devices, along_z(): lax.ppermute(own, 'rep', [(h * 4 + x, (h ^ 1) * 4 + x) for h in range(4)...  3.27 us
    ppermute x3, starting transfers between devices, along_x(): lax.ppermute(own, 'rep', across(4, 4, 0, s))  2.97 us
  transfers between devices with their start and end apart: 19, of which 14 were waited for; matrix products, arithmetic and copies ran while one was open for 0% of the time, Pallas kernels for 19%

profile of v6, /device:TPU:6, one launch (start us, length us, event | category | flops | bytes accessed | tf_op | source)
XLA Modules:
  0.0 86.1 jit_solution(18037433821195044499)
XLA Ops:
  0.7 0.1 pad_add_fusion.at_ref
  0.7 0.0 copy-start
  0.7 3.4 %copy-done = bf16[1,512,8192]{2,1,0:T(8,128)(2,1)S(1)} copy-done((bf16[1,512,8192]{2,1,0:T(8,128)(2,1)S(1)}, bf16[1,512,8192]{2,1,0:T(8,128)(2,1)}, u32[]{:S(2)}) %copy-start) | copy-done | bytes 8388632
  4.1 1.1 %pack.2.refs_3_ = bf16[4,512,512]{2,1,0:T(8,128)(2,1)S(1)} custom-call(s32[3]{0:T(128)S(1)} %pad_add_fusion.at_ref, bf16[1,512,8192]{2,1,0:T(8,128)(2,1)S(1)} %copy-done), custom_call_target="tpu_custom_call" | custom-call | tf_op jit(solution)/shard_map/pack/pallas_call | solution.py:273
  5.2 0.1 collective-permute-start.1
  5.3 3.1 %pack.3 = (bf16[4,512,512]{2,1,0:T(8,128)(2,1)}, bf16[4,512,512]{2,1,0:T(8,128)(2,1)S(1)}, bf16[4,512,512]{2,1,0:T(8,128)(2,1)S(1)}) custom-call(s32[3]{0:T(128)S(1)} %pad_add_fusion.at_ref, bf16[1,512,8192]{2,1,0:T(8,128)(2,1)S(1)} %copy-done, bf16[1,512,8192]{2,1,0:T(8,128)(2,1)S(1)} %copy-done, bf16[1,512,8192]{2,1,0:T(8,128)(2,1)S(1)} %copy-done, ...), custom_call_target="tpu_custom_call" | custom-call | tf_op jit(solution)/shard_map/pack/pallas_call | solution.py:273
  8.4 0.0 copy-start.3
  8.4 0.5 collective-permute-start
  8.9 0.5 collective-permute-done.1.refs_1_.refs_3_
  9.4 0.8 far.2
  10.2 0.0 copy-done.3
  10.2 0.6 copy-done.1
  10.8 1.6 %collective-permute-start.3 = (s16[272,512]{1,0:T(8,128)(2,1)S(1)}, s16[272,512]{1,0:T(8,128)(2,1)S(1)}, u32[]{:S(2)}, u32[]{:S(2)}) collective-permute-start(s16[272,512]{1,0:T(8,128)(2,1)S(1)} %get-tuple-element.28), channel_id=1, source_target_pairs={{0,4},{1,5},{2,6},{3,7},{4,8},{5,9},{6,10},{7,11},{8,12},{9,13},{1... | collective-permute-start | bytes 835592 | tf_op jit(solution)/shard_map/ppermute | solution.py:250
  12.4 1.7 %collective-permute-start.4 = (s16[272,512]{1,0:T(8,128)(2,1)S(1)}, s16[272,512]{1,0:T(8,128)(2,1)S(1)}, u32[]{:S(2)}, u32[]{:S(2)}) collective-permute-start(s16[272,512]{1,0:T(8,128)(2,1)S(1)} %get-tuple-element.26.refs_2_), channel_id=1, source_target_pairs={{0,12},{1,13},{2,14},{3,15},{4,0},{5,1},{6,2},{7,3},{8,4},{9,5},{1... | collective-permute-start | bytes 835592 | tf_op jit(solution)/shard_map/ppermute | solution.py:250
  14.1 0.0 copy-done.7
  14.1 0.1 slice.13.refs_4_
  14.2 0.1 slice.15.refs_5_.refs_4_
  14.2 0.1 convert_element_type.6.refs_3_.refs_6_
  14.3 0.0 collective-permute-done.refs_1_.refs_3_.refs_6_
  14.3 2.1 %far.3 = (s16[272,512]{1,0:T(8,128)(2,1)S(1)}, s16[272,512]{1,0:T(8,128)(2,1)S(1)}) custom-call(s32[3]{0:T(128)S(1)} %pad_add_fusion.at_ref, bf16[4,512,512]{2,1,0:T(8,128)(2,1)S(1)} %get-tuple-element.23.refs_2_.refs_0_.refs_5_, bf16[4,512,512]{2,1,0:T(8,128)(2,1)} %collective-permute-done.refs_1_.refs_3_.refs_6_, ...), custom_call_target="tpu_custom_call" | custom-call | tf_op jit(solution)/shard_map/far/pallas_call | solution.py:273
  16.4 1.9 %collective-permute-start.2 = (s16[272,512]{1,0:T(8,128)(2,1)S(1)}, s16[272,512]{1,0:T(8,128)(2,1)S(1)}, u32[]{:S(2)}, u32[]{:S(2)}) collective-permute-start(s16[272,512]{1,0:T(8,128)(2,1)S(1)} %get-tuple-element.27.refs_6_), channel_id=1, source_target_pairs={{0,12},{1,13},{2,14},{3,15},{4,0},{5,1},{6,2},{7,3},{8,4},{9,5},{1... | collective-permute-start | bytes 835592 | tf_op jit(solution)/shard_map/ppermute | solution.py:250
  18.3 0.2 collective-permute-start.7
  18.5 2.3 %collective-permute-done.3.refs_4_ = s16[272,512]{1,0:T(8,128)(2,1)S(1)} collective-permute-done((s16[272,512]{1,0:T(8,128)(2,1)S(1)}, s16[272,512]{1,0:T(8,128)(2,1)S(1)}, u32[]{:S(2)}, u32[]{:S(2)}) %collective-permute-start.3) | collective-permute-done | bytes 278560 | tf_op jit(solution)/shard_map/ppermute | solution.py:250
  20.8 1.1 %collective-permute-done.4.refs_5_ = s16[272,512]{1,0:T(8,128)(2,1)S(1)} collective-permute-done((s16[272,512]{1,0:T(8,128)(2,1)S(1)}, s16[272,512]{1,0:T(8,128)(2,1)S(1)}, u32[]{:S(2)}, u32[]{:S(2)}) %collective-permute-start.4) | collective-permute-done | bytes 278560 | tf_op jit(solution)/shard_map/ppermute | solution.py:250
  22.0 0.0 copy-done.2
  22.0 0.0 copy-done.4
  22.0 1.2 %near.3 = (s16[528,512]{1,0:T(8,128)(2,1)S(1)}, s16[528,512]{1,0:T(8,128)(2,1)S(1)}) custom-call(s32[3]{0:T(128)S(1)} %pad_add_fusion.at_ref, bf16[4,512,512]{2,1,0:T(8,128)(2,1)S(1)} %copy-done.4, bf16[4,512,512]{2,1,0:T(8,128)(2,1)S(1)} %copy-done.2, bf16[4,512,512]{2,1,0:T(8,128)(2,1)S(1)} %copy-done.4, bf16[4,512,512]{2,1,0:T(8,128)(2,1)S(1)} %copy-done.2, ...), custom_call_target="tpu_custom_call" | custom-call | tf_op jit(solution)/shard_map/near/pallas_call | solution.py:273
  23.2 1.7 %collective-permute-start.5 = (s16[528,512]{1,0:T(8,128)(2,1)S(1)}, s16[528,512]{1,0:T(8,128)(2,1)S(1)}, u32[]{:S(2)}, u32[]{:S(2)}) collective-permute-start(s16[528,512]{1,0:T(8,128)(2,1)S(1)} %get-tuple-element.29), channel_id=1, source_target_pairs={{0,4},{1,5},{2,6},{3,7},{4,8},{5,9},{6,10},{7,11},{8,12},{9,13},{1... | collective-permute-start | bytes 1622024 | tf_op jit(solution)/shard_map/ppermute | solution.py:250
  24.8 1.7 %collective-permute-start.6 = (s16[528,512]{1,0:T(8,128)(2,1)S(1)}, s16[528,512]{1,0:T(8,128)(2,1)S(1)}, u32[]{:S(2)}, u32[]{:S(2)}) collective-permute-start(s16[528,512]{1,0:T(8,128)(2,1)S(1)} %get-tuple-element.30.refs_9_), channel_id=1, source_target_pairs={{0,12},{1,13},{2,14},{3,15},{4,0},{5,1},{6,2},{7,3},{8,4},{9,5},{1... | collective-permute-start | bytes 1622024 | tf_op jit(solution)/shard_map/ppermute | solution.py:250
  26.5 1.5 %collective-permute-done.2.refs_11_.refs_4_ = s16[272,512]{1,0:T(8,128)(2,1)S(1)} collective-permute-done((s16[272,512]{1,0:T(8,128)(2,1)S(1)}, s16[272,512]{1,0:T(8,128)(2,1)S(1)}, u32[]{:S(2)}, u32[]{:S(2)}) %collective-permute-start.2) | collective-permute-done | bytes 278560 | tf_op jit(solution)/shard_map/ppermute | solution.py:250
  27.9 1.2 %collective-permute-done.7.refs_4_.refs_10_ = s16[272,512]{1,0:T(8,128)(2,1)S(1)} collective-permute-done((s16[272,512]{1,0:T(8,128)(2,1)S(1)}, s16[272,512]{1,0:T(8,128)(2,1)S(1)}, u32[]{:S(2)}, u32[]{:S(2)}) %collective-permute-start.7) | collective-permute-done | bytes 278560 | tf_op jit(solution)/shard_map/ppermute | solution.py:250
  29.1 0.0 copy-done.5
  29.1 0.0 copy-done.6
  29.1 2.5 %near.4 = (s16[272,512]{1,0:T(8,128)(2,1)S(1)}, s16[272,512]{1,0:T(8,128)(2,1)S(1)}, f32[512,512]{1,0:T(8,128)S(1)}, bf16[2,2,256,256]{3,2,1,0:T(8,128)(2,1)S(1)}) custom-call(s32[3]{0:T(128)S(1)} %pad_add_fusion.at_ref, bf16[4,512,512]{2,1,0:T(8,128)(2,1)S(1)} %get-tuple-element.23.refs_2_.refs_0_.refs_5_, ...), custom_call_target="tpu_custom_call" | custom-call | tf_op jit(solution)/shard_map/near/pallas_call | solution.py:273
  31.5 0.5 collective-permute-start.11
  32.1 2.8 %collective-permute-start.12 = (s16[272,512]{1,0:T(8,128)(2,1)S(1)}, s16[272,512]{1,0:T(8,128)(2,1)S(1)}, u32[]{:S(2)}, u32[]{:S(2)}) collective-permute-start(s16[272,512]{1,0:T(8,128)(2,1)S(1)} %get-tuple-element.38), channel_id=1, source_target_pairs={{0,12},{1,13},{2,14},{3,15},{4,0},{5,1},{6,2},{7,3},{8,4},{9,5},{1... | collective-permute-start | bytes 835592 | tf_op jit(solution)/shard_map/ppermute | solution.py:250
  34.9 5.8 %collective-permute-done.5.refs_2_ = s16[528,512]{1,0:T(8,128)(2,1)S(1)} collective-permute-done((s16[528,512]{1,0:T(8,128)(2,1)S(1)}, s16[528,512]{1,0:T(8,128)(2,1)S(1)}, u32[]{:S(2)}, u32[]{:S(2)}) %collective-permute-start.5) | collective-permute-done | bytes 540704 | tf_op jit(solution)/shard_map/ppermute | solution.py:250
  40.7 0.0 collective-permute-done.6.refs_3_
  40.7 1.1 %cross.1 = (s16[272,512]{1,0:T(8,128)(2,1)S(1)}, s16[272,512]{1,0:T(8,128)(2,1)S(1)}) custom-call(s32[3]{0:T(128)S(1)} %pad_add_fusion.at_ref, bf16[4,512,512]{2,1,0:T(8,128)(2,1)S(1)} %copy-done.4, bf16[4,512,512]{2,1,0:T(8,128)(2,1)S(1)} %copy-done.2, s16[528,512]{1,0:T(8,128)(2,1)S(1)} %collective-permute-done.5.refs_2_, ...), custom_call_target="tpu_custom_call" | custom-call | tf_op jit(solution)/shard_map/cross/pallas_call | solution.py:273
  41.7 2.0 %collective-permute-start.13 = (s16[272,512]{1,0:T(8,128)(2,1)S(1)}, s16[272,512]{1,0:T(8,128)(2,1)S(1)}, u32[]{:S(2)}, u32[]{:S(2)}) collective-permute-start(s16[272,512]{1,0:T(8,128)(2,1)S(1)} %get-tuple-element.39), channel_id=1, source_target_pairs={{0,2},{1,3},{2,0},{3,1},{4,6},{5,7},{6,4},{7,5},{8,10},{9,11},{10,... | collective-permute-start | bytes 835592 | tf_op jit(solution)/shard_map/ppermute | solution.py:250
  43.7 1.9 %near.5 = (s16[272,512]{1,0:T(8,128)(2,1)S(1)}, s16[272,512]{1,0:T(8,128)(2,1)S(1)}) custom-call(s32[3]{0:T(128)S(1)} %pad_add_fusion.at_ref, bf16[4,512,512]{2,1,0:T(8,128)(2,1)S(1)} %get-tuple-element.23.refs_2_.refs_0_.refs_5_, bf16[4,512,512]{2,1,0:T(8,128)(2,1)} %collective-permute-done.refs_1_.refs_3_.refs_6_, ...), custom_call_target="tpu_custom_call" | custom-call | tf_op jit(solution)/shard_map/near/pallas_call | solution.py:273
  45.6 0.7 collective-permute-start.8
  46.3 2.6 %collective-permute-start.9 = (s16[272,512]{1,0:T(8,128)(2,1)S(1)}, s16[272,512]{1,0:T(8,128)(2,1)S(1)}, u32[]{:S(2)}, u32[]{:S(2)}) collective-permute-start(s16[272,512]{1,0:T(8,128)(2,1)S(1)} %get-tuple-element.35.refs_7_), channel_id=1, source_target_pairs={{0,12},{1,13},{2,14},{3,15},{4,0},{5,1},{6,2},{7,3},{8,4},{9,5},{1... | collective-permute-start | bytes 835592 | tf_op jit(solution)/shard_map/ppermute | solution.py:250
  49.0 0.0 collective-permute-done.11.refs_0_
  49.0 0.1 collective-permute-start.10
  49.1 0.0 collective-permute-done.12.refs_1_
  49.1 0.2 collective-permute-done.13.refs_2_
  49.3 3.7 %encode.2 = (f32[512,512]{1,0:T(8,128)}, f32[24,128]{1,0:T(8,128)S(1)}) custom-call(s32[3]{0:T(128)S(1)} %pad_add_fusion.at_ref, s16[272,512]{1,0:T(8,128)(2,1)S(1)} %collective-permute-done.11.refs_0_, s16[272,512]{1,0:T(8,128)(2,1)S(1)} %collective-permute-done.12.refs_1_, s16[272,512]{1,0:T(8,128)(2,1)S(1)} %collective-permute-done.13.refs_2_, ...), custom_call_target="tpu_custom_call" | custom-call | tf_op jit(solution)/shard_map/encode/pallas_call | solution.py:273
  53.0 0.5 collective-permute-done.8.refs_0_
  53.5 0.0 collective-permute-done.9.refs_1_
  53.5 2.0 %collective-permute-done.10.refs_2_ = s16[272,512]{1,0:T(8,128)(2,1)S(1)} collective-permute-done((s16[272,512]{1,0:T(8,128)(2,1)S(1)}, s16[272,512]{1,0:T(8,128)(2,1)S(1)}, u32[]{:S(2)}, u32[]{:S(2)}) %collective-permute-start.10) | collective-permute-done | bytes 278560 | tf_op jit(solution)/shard_map/ppermute | solution.py:250
  55.5 3.7 %encode.3 = (f32[512,512]{1,0:T(8,128)}, f32[32,128]{1,0:T(8,128)S(1)}) custom-call(s32[3]{0:T(128)S(1)} %pad_add_fusion.at_ref, s16[272,512]{1,0:T(8,128)(2,1)S(1)} %collective-permute-done.8.refs_0_, s16[272,512]{1,0:T(8,128)(2,1)S(1)} %collective-permute-done.9.refs_1_, ...), custom_call_target="tpu_custom_call", output_to_operand_aliasing={{0}: (8, {})} | custom-call | tf_op jit(solution)/shard_map/encode/pallas_call | solution.py:273
  59.2 3.3 %collective-permute-start.14 = (f32[32,128]{1,0:T(8,128)S(1)}, f32[32,128]{1,0:T(8,128)S(1)}, u32[]{:S(2)}, u32[]{:S(2)}) collective-permute-start(f32[32,128]{1,0:T(8,128)S(1)} %get-tuple-element.43.refs_2_), channel_id=1, source_target_pairs={{0,64},{16,80},{32,96},{48,112},{64,0},{80,16},{96,32},{112,48},{1... | collective-permute-start | bytes 49160 | tf_op jit(solution)/shard_map/ppermute | solution.py:235
  62.5 1.7 %collective-permute-done.14 = f32[32,128]{1,0:T(8,128)S(1)} collective-permute-done((f32[32,128]{1,0:T(8,128)S(1)}, f32[32,128]{1,0:T(8,128)S(1)}, u32[]{:S(2)}, u32[]{:S(2)}) %collective-permute-start.14) | collective-permute-done | bytes 16416 | tf_op jit(solution)/shard_map/ppermute | solution.py:235
  64.2 5.1 %collective-permute-start.15 = (f32[2,32,128]{2,1,0:T(8,128)S(1)}, f32[2,32,128]{2,1,0:T(8,128)S(1)}, u32[]{:S(2)}, u32[]{:S(2)}) collective-permute-start(f32[2,32,128]{2,1,0:T(8,128)S(1)} %pad_maximum_fusion.refs_0_), channel_id=1, source_target_pairs={{0,192},{16,208},{32,224},{48,240},{64,128},{80,144},{96,160},{112... | collective-permute-start | bytes 98312 | tf_op jit(solution)/shard_map/ppermute | solution.py:237
  69.3 1.9 %collective-permute-done.15.refs_1_ = f32[2,32,128]{2,1,0:T(8,128)S(1)} collective-permute-done((f32[2,32,128]{2,1,0:T(8,128)S(1)}, f32[2,32,128]{2,1,0:T(8,128)S(1)}, u32[]{:S(2)}, u32[]{:S(2)}) %collective-permute-start.15) | collective-permute-done | bytes 32800 | tf_op jit(solution)/shard_map/ppermute | solution.py:237
  71.1 0.7 spread.1.refs_0_.refs_5_
  71.8 0.6 collective-permute-start.16
  72.4 2.4 %collective-permute-start.17 = (f32[8,16,128]{2,1,0:T(8,128)S(1)}, f32[8,16,128]{2,1,0:T(8,128)S(1)}, u32[]{:S(2)}, u32[]{:S(2)}) collective-permute-start(f32[8,16,128]{2,1,0:T(8,128)S(1)} %spread.1.refs_0_.refs_5_), channel_id=1, source_target_pairs={{0,32},{16,48},{32,0},{48,16},{64,96},{80,112},{96,64},{112,80},{1... | collective-permute-start | bytes 196616 | tf_op jit(solution)/shard_map/ppermute | solution.py:231
  74.8 0.0 collective-permute-start.18
  74.8 1.4 %collective-permute-done.16.refs_1_ = f32[8,16,128]{2,1,0:T(8,128)S(1)} collective-permute-done((f32[8,16,128]{2,1,0:T(8,128)S(1)}, f32[8,16,128]{2,1,0:T(8,128)S(1)}, u32[]{:S(2)}, u32[]{:S(2)}) %collective-permute-start.16) | collective-permute-done | bytes 65568 | tf_op jit(solution)/shard_map/ppermute | solution.py:231
  76.2 2.0 %collective-permute-done.17.refs_2_ = f32[8,16,128]{2,1,0:T(8,128)S(1)} collective-permute-done((f32[8,16,128]{2,1,0:T(8,128)S(1)}, f32[8,16,128]{2,1,0:T(8,128)S(1)}, u32[]{:S(2)}, u32[]{:S(2)}) %collective-permute-start.17) | collective-permute-done | bytes 65568 | tf_op jit(solution)/shard_map/ppermute | solution.py:231
  78.1 2.1 %collective-permute-done.18.refs_3_ = f32[8,16,128]{2,1,0:T(8,128)S(1)} collective-permute-done((f32[8,16,128]{2,1,0:T(8,128)S(1)}, f32[8,16,128]{2,1,0:T(8,128)S(1)}, u32[]{:S(2)}, u32[]{:S(2)}) %collective-permute-start.18) | collective-permute-done | bytes 65568 | tf_op jit(solution)/shard_map/ppermute | solution.py:231
  80.3 5.8 %decode.1 = f32[512,512]{1,0:T(8,128)} custom-call(s32[3]{0:T(128)S(1)} %pad_add_fusion.at_ref, f32[8,16,128]{2,1,0:T(8,128)S(1)} %spread.1.refs_0_.refs_5_, f32[8,16,128]{2,1,0:T(8,128)S(1)} %collective-permute-done.16.refs_1_, f32[8,16,128]{2,1,0:T(8,128)S(1)} %collective-permute-done.17.refs_2_, f32[8,16,128]{2,1,0:T(8,128)S(1)} %collective-permute-done.18.refs_3_, ...), custom_call_target="tpu_custom_call" | custom-call | tf_op jit(solution)/shard_map/decode/pallas_call | solution.py:273
  (9 shorter events, 0.0 us)
Async XLA Ops:
  0.7 3.4 %copy-start = (bf16[1,512,8192]{2,1,0:T(8,128)(2,1)S(1)}, bf16[1,512,8192]{2,1,0:T(8,128)(2,1)}, u32[]{:S(2)}) copy-start(bf16[1,512,8192]{2,1,0:T(8,128)(2,1)} %refs_2_.1) | copy-start | bytes 25165828
  5.2 4.2 %collective-permute-start.1 = (bf16[4,512,512]{2,1,0:T(8,128)(2,1)S(1)}, bf16[4,512,512]{2,1,0:T(8,128)(2,1)S(1)}, u32[]{:S(2)}, u32[]{:S(2)}) collective-permute-start(bf16[4,512,512]{2,1,0:T(8,128)(2,1)S(1)} %pack.2.refs_3_), channel_id=1, source_target_pairs={{0,1},{1,0},{2,3},{3,2},{4,5},{5,4},{6,7},{7,6},{8,9},{9,8},{10,11... | collective-permute-start | bytes 6291464 | tf_op jit(solution)/shard_map/ppermute | solution.py:250
  8.4 1.8 %copy-start.3 = (bf16[4,512,512]{2,1,0:T(8,128)(2,1)}, bf16[4,512,512]{2,1,0:T(8,128)(2,1)S(1)}, u32[]{:S(2)}) copy-start(bf16[4,512,512]{2,1,0:T(8,128)(2,1)S(1)} %get-tuple-element.25.refs_0_.refs_2_) | copy-start | bytes 6291460
  8.4 5.9 %collective-permute-start = (bf16[4,512,512]{2,1,0:T(8,128)(2,1)}, bf16[4,512,512]{2,1,0:T(8,128)(2,1)}, u32[]{:S(2)}, u32[]{:S(2)}) collective-permute-start(bf16[4,512,512]{2,1,0:T(8,128)(2,1)} %get-tuple-element.24), channel_id=1, source_target_pairs={{0,1},{1,0},{2,3},{3,2},{4,5},{5,4},{6,7},{7,6},{8,9},{9,8},{10,11... | collective-permute-start | bytes 6291464 | tf_op jit(solution)/shard_map/ppermute | solution.py:250
  9.4 1.4 %copy-start.1 = (bf16[4,512,512]{2,1,0:T(8,128)(2,1)}, bf16[4,512,512]{2,1,0:T(8,128)(2,1)S(1)}, u32[]{:S(2)}) copy-start(bf16[4,512,512]{2,1,0:T(8,128)(2,1)S(1)} %collective-permute-done.1.refs_1_.refs_3_) | copy-start | bytes 6291460
  9.4 4.6 %copy-start.7 = (s32[1,8,8,32]{3,2,1,0:T(8,128)S(1)}, s32[1,8,8,32]{3,2,1,0:T(8,128)}, u32[]{:S(2)}) copy-start(s32[1,8,8,32]{3,2,1,0:T(8,128)} %param.6) | copy-start | bytes 24580
  10.8 10.0 %collective-permute-start.3 = (s16[272,512]{1,0:T(8,128)(2,1)S(1)}, s16[272,512]{1,0:T(8,128)(2,1)S(1)}, u32[]{:S(2)}, u32[]{:S(2)}) collective-permute-start(s16[272,512]{1,0:T(8,128)(2,1)S(1)} %get-tuple-element.28), channel_id=1, source_target_pairs={{0,4},{1,5},{2,6},{3,7},{4,8},{5,9},{6,10},{7,11},{8,12},{9,13},{1... | collective-permute-start | bytes 835592 | tf_op jit(solution)/shard_map/ppermute | solution.py:250
  12.4 9.5 %collective-permute-start.4 = (s16[272,512]{1,0:T(8,128)(2,1)S(1)}, s16[272,512]{1,0:T(8,128)(2,1)S(1)}, u32[]{:S(2)}, u32[]{:S(2)}) collective-permute-start(s16[272,512]{1,0:T(8,128)(2,1)S(1)} %get-tuple-element.26.refs_2_), channel_id=1, source_target_pairs={{0,12},{1,13},{2,14},{3,15},{4,0},{5,1},{6,2},{7,3},{8,4},{9,5},{1... | collective-permute-start | bytes 835592 | tf_op jit(solution)/shard_map/ppermute | solution.py:250
  14.3 7.7 %copy-start.2 = (bf16[4,512,512]{2,1,0:T(8,128)(2,1)S(1)}, bf16[4,512,512]{2,1,0:T(8,128)(2,1)}, u32[]{:S(2)}) copy-start(bf16[4,512,512]{2,1,0:T(8,128)(2,1)} %copy-done.1) | copy-start | bytes 6291460
  14.3 7.7 %copy-start.4 = (bf16[4,512,512]{2,1,0:T(8,128)(2,1)S(1)}, bf16[4,512,512]{2,1,0:T(8,128)(2,1)}, u32[]{:S(2)}) copy-start(bf16[4,512,512]{2,1,0:T(8,128)(2,1)} %copy-done.3) | copy-start | bytes 6291460
  16.4 11.5 %collective-permute-start.2 = (s16[272,512]{1,0:T(8,128)(2,1)S(1)}, s16[272,512]{1,0:T(8,128)(2,1)S(1)}, u32[]{:S(2)}, u32[]{:S(2)}) collective-permute-start(s16[272,512]{1,0:T(8,128)(2,1)S(1)} %get-tuple-element.27.refs_6_), channel_id=1, source_target_pairs={{0,12},{1,13},{2,14},{3,15},{4,0},{5,1},{6,2},{7,3},{8,4},{9,5},{1... | collective-permute-start | bytes 835592 | tf_op jit(solution)/shard_map/ppermute | solution.py:250
  18.3 10.8 %copy-start.5 = (f32[512,512]{1,0:T(8,128)S(1)}, f32[512,512]{1,0:T(8,128)}, u32[]{:S(2)}) copy-start(f32[512,512]{1,0:T(8,128)} %refs_7_.1) | copy-start | bytes 3145732
  18.3 10.8 %copy-start.6 = (bf16[2,2,256,256]{3,2,1,0:T(8,128)(2,1)S(1)}, bf16[2,2,256,256]{3,2,1,0:T(8,128)(2,1)}, u32[]{:S(2)}) copy-start(bf16[2,2,256,256]{3,2,1,0:T(8,128)(2,1)} %constant.44.clone.refs_8_) | copy-start | bytes 1572868
  18.3 10.8 %collective-permute-start.7 = (s16[272,512]{1,0:T(8,128)(2,1)S(1)}, s16[272,512]{1,0:T(8,128)(2,1)S(1)}, u32[]{:S(2)}, u32[]{:S(2)}) collective-permute-start(s16[272,512]{1,0:T(8,128)(2,1)S(1)} %get-tuple-element.31), channel_id=1, source_target_pairs={{0,4},{1,5},{2,6},{3,7},{4,8},{5,9},{6,10},{7,11},{8,12},{9,13},{1... | collective-permute-start | bytes 835592 | tf_op jit(solution)/shard_map/ppermute | solution.py:250
  23.2 17.5 %collective-permute-start.5 = (s16[528,512]{1,0:T(8,128)(2,1)S(1)}, s16[528,512]{1,0:T(8,128)(2,1)S(1)}, u32[]{:S(2)}, u32[]{:S(2)}) collective-permute-start(s16[528,512]{1,0:T(8,128)(2,1)S(1)} %get-tuple-element.29), channel_id=1, source_target_pairs={{0,4},{1,5},{2,6},{3,7},{4,8},{5,9},{6,10},{7,11},{8,12},{9,13},{1... | collective-permute-start | bytes 1622024 | tf_op jit(solution)/shard_map/ppermute | solution.py:250
  24.8 15.9 %collective-permute-start.6 = (s16[528,512]{1,0:T(8,128)(2,1)S(1)}, s16[528,512]{1,0:T(8,128)(2,1)S(1)}, u32[]{:S(2)}, u32[]{:S(2)}) collective-permute-start(s16[528,512]{1,0:T(8,128)(2,1)S(1)} %get-tuple-element.30.refs_9_), channel_id=1, source_target_pairs={{0,12},{1,13},{2,14},{3,15},{4,0},{5,1},{6,2},{7,3},{8,4},{9,5},{1... | collective-permute-start | bytes 1622024 | tf_op jit(solution)/shard_map/ppermute | solution.py:250
  31.5 17.4 %collective-permute-start.11 = (s16[272,512]{1,0:T(8,128)(2,1)S(1)}, s16[272,512]{1,0:T(8,128)(2,1)S(1)}, u32[]{:S(2)}, u32[]{:S(2)}) collective-permute-start(s16[272,512]{1,0:T(8,128)(2,1)S(1)} %get-tuple-element.37), channel_id=1, source_target_pairs={{0,4},{1,5},{2,6},{3,7},{4,8},{5,9},{6,10},{7,11},{8,12},{9,13},{1... | collective-permute-start | bytes 835592 | tf_op jit(solution)/shard_map/ppermute | solution.py:250
  32.1 17.0 %collective-permute-start.12 = (s16[272,512]{1,0:T(8,128)(2,1)S(1)}, s16[272,512]{1,0:T(8,128)(2,1)S(1)}, u32[]{:S(2)}, u32[]{:S(2)}) collective-permute-start(s16[272,512]{1,0:T(8,128)(2,1)S(1)} %get-tuple-element.38), channel_id=1, source_target_pairs={{0,12},{1,13},{2,14},{3,15},{4,0},{5,1},{6,2},{7,3},{8,4},{9,5},{1... | collective-permute-start | bytes 835592 | tf_op jit(solution)/shard_map/ppermute | solution.py:250
  41.7 7.5 %collective-permute-start.13 = (s16[272,512]{1,0:T(8,128)(2,1)S(1)}, s16[272,512]{1,0:T(8,128)(2,1)S(1)}, u32[]{:S(2)}, u32[]{:S(2)}) collective-permute-start(s16[272,512]{1,0:T(8,128)(2,1)S(1)} %get-tuple-element.39), channel_id=1, source_target_pairs={{0,2},{1,3},{2,0},{3,1},{4,6},{5,7},{6,4},{7,5},{8,10},{9,11},{10,... | collective-permute-start | bytes 835592 | tf_op jit(solution)/shard_map/ppermute | solution.py:250
  45.6 7.8 %collective-permute-start.8 = (s16[272,512]{1,0:T(8,128)(2,1)S(1)}, s16[272,512]{1,0:T(8,128)(2,1)S(1)}, u32[]{:S(2)}, u32[]{:S(2)}) collective-permute-start(s16[272,512]{1,0:T(8,128)(2,1)S(1)} %get-tuple-element.34), channel_id=1, source_target_pairs={{0,4},{1,5},{2,6},{3,7},{4,8},{5,9},{6,10},{7,11},{8,12},{9,13},{1... | collective-permute-start | bytes 835592 | tf_op jit(solution)/shard_map/ppermute | solution.py:250
  46.3 7.1 %collective-permute-start.9 = (s16[272,512]{1,0:T(8,128)(2,1)S(1)}, s16[272,512]{1,0:T(8,128)(2,1)S(1)}, u32[]{:S(2)}, u32[]{:S(2)}) collective-permute-start(s16[272,512]{1,0:T(8,128)(2,1)S(1)} %get-tuple-element.35.refs_7_), channel_id=1, source_target_pairs={{0,12},{1,13},{2,14},{3,15},{4,0},{5,1},{6,2},{7,3},{8,4},{9,5},{1... | collective-permute-start | bytes 835592 | tf_op jit(solution)/shard_map/ppermute | solution.py:250
  49.0 6.5 %collective-permute-start.10 = (s16[272,512]{1,0:T(8,128)(2,1)S(1)}, s16[272,512]{1,0:T(8,128)(2,1)S(1)}, u32[]{:S(2)}, u32[]{:S(2)}) collective-permute-start(s16[272,512]{1,0:T(8,128)(2,1)S(1)} %get-tuple-element.33.refs_5_), channel_id=1, source_target_pairs={{0,2},{1,3},{2,0},{3,1},{4,6},{5,7},{6,4},{7,5},{8,10},{9,11},{10,... | collective-permute-start | bytes 835592 | tf_op jit(solution)/shard_map/ppermute | solution.py:250
  59.2 5.0 %collective-permute-start.14 = (f32[32,128]{1,0:T(8,128)S(1)}, f32[32,128]{1,0:T(8,128)S(1)}, u32[]{:S(2)}, u32[]{:S(2)}) collective-permute-start(f32[32,128]{1,0:T(8,128)S(1)} %get-tuple-element.43.refs_2_), channel_id=1, source_target_pairs={{0,64},{16,80},{32,96},{48,112},{64,0},{80,16},{96,32},{112,48},{1... | collective-permute-start | bytes 49160 | tf_op jit(solution)/shard_map/ppermute | solution.py:235
  64.2 6.9 %collective-permute-start.15 = (f32[2,32,128]{2,1,0:T(8,128)S(1)}, f32[2,32,128]{2,1,0:T(8,128)S(1)}, u32[]{:S(2)}, u32[]{:S(2)}) collective-permute-start(f32[2,32,128]{2,1,0:T(8,128)S(1)} %pad_maximum_fusion.refs_0_), channel_id=1, source_target_pairs={{0,192},{16,208},{32,224},{48,240},{64,128},{80,144},{96,160},{112... | collective-permute-start | bytes 98312 | tf_op jit(solution)/shard_map/ppermute | solution.py:237
  71.8 4.3 %collective-permute-start.16 = (f32[8,16,128]{2,1,0:T(8,128)S(1)}, f32[8,16,128]{2,1,0:T(8,128)S(1)}, u32[]{:S(2)}, u32[]{:S(2)}) collective-permute-start(f32[8,16,128]{2,1,0:T(8,128)S(1)} %spread.1.refs_0_.refs_5_), channel_id=1, source_target_pairs={{0,16},{16,32},{32,48},{48,0},{64,80},{80,96},{96,112},{112,64},{1... | collective-permute-start | bytes 196616 | tf_op jit(solution)/shard_map/ppermute | solution.py:231
  72.4 5.8 %collective-permute-start.17 = (f32[8,16,128]{2,1,0:T(8,128)S(1)}, f32[8,16,128]{2,1,0:T(8,128)S(1)}, u32[]{:S(2)}, u32[]{:S(2)}) collective-permute-start(f32[8,16,128]{2,1,0:T(8,128)S(1)} %spread.1.refs_0_.refs_5_), channel_id=1, source_target_pairs={{0,32},{16,48},{32,0},{48,16},{64,96},{80,112},{96,64},{112,80},{1... | collective-permute-start | bytes 196616 | tf_op jit(solution)/shard_map/ppermute | solution.py:231
  74.8 5.5 %collective-permute-start.18 = (f32[8,16,128]{2,1,0:T(8,128)S(1)}, f32[8,16,128]{2,1,0:T(8,128)S(1)}, u32[]{:S(2)}, u32[]{:S(2)}) collective-permute-start(f32[8,16,128]{2,1,0:T(8,128)S(1)} %spread.1.refs_0_.refs_5_), channel_id=1, source_target_pairs={{0,48},{16,0},{32,16},{48,32},{64,112},{80,64},{96,80},{112,96},{1... | collective-permute-start | bytes 196616 | tf_op jit(solution)/shard_map/ppermute | solution.py:231
